TPU v7x, 32 devices: a whole 2x2x4 slice. The times are simulated.
32 devices in a mesh: row: 2 (over x), col: 16 (over z, y, core).
Axes of the slice: x: 2, y: 2, z: 4, core: 2. Of those that a mesh axis runs over, the one named last changes fastest.
Arguments:
- image_tokens: bfloat16 [4096, 50, 384], P(('row', 'col')), may hold values from -6 to 6
- text_tokens: bfloat16 [4096, 16, 384], P(('row', 'col')), may hold values from -6 to 6
- lengths: int32 [4096], P(('row', 'col')), may hold values from 1 to 16, as said below
- pair_count: int32 [2, 16], replicated, may hold values from 24 to 128, as said below
- img_qkv: bfloat16 [384, 1152], replicated, may hold values from -0.3125 to 0.3125
- img_out: bfloat16 [384, 384], replicated, may hold values from -0.875 to 0.875
- img_up: bfloat16 [384, 1536], replicated, may hold values from -0.3125 to 0.3125
- img_down: bfloat16 [1536, 384], replicated, may hold values from -0.15625 to 0.15625
- img_proj: bfloat16 [384, 384], replicated, may hold values from -0.3125 to 0.3125
- gain_one: float32 [384], replicated, may hold values from 0.5 to 1.5
- txt_qkv: bfloat16 [384, 1152], replicated, may hold values from -0.3125 to 0.3125
- txt_out: bfloat16 [384, 384], replicated, may hold values from -0.625 to 0.625
- gain_two: float32 [384], replicated, may hold values from 0.5 to 1.5
- txt_up: bfloat16 [384, 1536], replicated, may hold values from -0.3125 to 0.3125
- txt_down: bfloat16 [1536, 384], replicated, may hold values from -0.15625 to 0.15625
- txt_proj: bfloat16 [384, 384], replicated, may hold values from -0.3125 to 0.3125
- log_scale: float32 [1], replicated, may hold values from 3.2 to 3.8
Outputs:
- loss: float32 [1], replicated
- text_grad: bfloat16 [4096, 16, 384], P(('row', 'col'))
- grad_gain_one: float32 [384], replicated
- grad_qkv: float32 [384, 1152], replicated
- grad_out: float32 [384, 384], replicated
- grad_gain_two: float32 [384], replicated
- grad_up: float32 [384, 1536], replicated
- grad_down: float32 [1536, 384], replicated
- grad_proj: float32 [384, 384], replicated
- grad_scale: float32 [1], replicated
Inputs may be any that keep to these rules, and one draw needn't show every extreme that they name: `lengths`: every caption has 1 to 16 live tokens; some caption has 16. `pair_count`: A block's live pairs grow with its row index r, from about a quarter of 128 at r = 0 to nearly 128 at the last row index; some block is full.
All inputs are finite; a program needn't handle non-finite values.
Results may differ from a plain program's by a relative error of at most 0.017.
The roundings to bfloat16 on the way count: a program that leaves them out, or rounds other values in their place, can miss the bound.
Values may be sent and summed in bfloat16 or wider, within the bound.
No kernel may reach another device: no remote copies, remote signals or barrier semaphores. Data moves between devices by JAX's collectives and lax.ppermute only.
A program may use at most 192 MiB of HBM per device.

v0:
```python
import jax
import jax.numpy as jnp
from jax import lax
from jax.sharding import PartitionSpec as P

HEADS = 6
HEAD = 64


epsilon = 1e-06
floor_value = -1e30


def layer_norm_stats(values):
    centred = values - jnp.mean(values, axis=-1, keepdims=True)
    scale_inv = lax.rsqrt(jnp.mean(centred * centred, axis=-1, keepdims=True) + epsilon)
    return (centred * scale_inv, scale_inv)


def layer_norm_back(grad, normed, scale_inv):
    return scale_inv * (
        grad
        - jnp.mean(grad, axis=-1, keepdims=True)
        - normed * jnp.mean(grad * normed, axis=-1, keepdims=True)
    )


def project(left, right):
    return jnp.einsum("...d,de->...e", left, right, preferred_element_type=jnp.float32)


def unit_vector(values):
    return values * lax.rsqrt(jnp.sum(values * values, axis=-1, keepdims=True) + epsilon)


def split_heads(mixed):
    count, length, _ = mixed.shape
    split = mixed.reshape(count, length, 3, HEADS, HEAD)
    return (split[:, :, 0], split[:, :, 1], split[:, :, 2])


def masked_scores(query, keys, key_mask):
    scores = jnp.einsum(
        "nqhd,nkhd->nhqk", query, keys, preferred_element_type=jnp.float32
    ) * HEAD ** (-0.5)
    return jnp.where(key_mask[:, None, None, :], scores, floor_value)


def attend(mixed, key_mask):
    count, length, _ = mixed.shape
    query, keys, values = split_heads(mixed)
    scores = masked_scores(query, keys, key_mask)
    peak = jnp.max(scores, axis=-1, keepdims=True)
    expo = jnp.exp(scores - peak)
    total = jnp.sum(expo, axis=-1, keepdims=True)
    probs = (expo / total).astype(jnp.bfloat16)
    result = jnp.einsum("nhqk,nkhd->nqhd", probs, values, preferred_element_type=jnp.float32)
    return (result.reshape(count, length, HEADS * HEAD).astype(jnp.bfloat16), peak + jnp.log(total))


def attend_back(mixed, key_mask, log_total, grad_heads_flat):
    count, length, _ = mixed.shape
    query, keys, values = split_heads(mixed)
    probs = jnp.exp(masked_scores(query, keys, key_mask) - log_total)
    grad_heads = grad_heads_flat.reshape(count, length, HEADS, HEAD)
    grad_probs = jnp.einsum(
        "nqhd,nkhd->nhqk", grad_heads, values, preferred_element_type=jnp.float32
    )
    grad_values = jnp.einsum(
        "nhqk,nqhd->nkhd",
        probs.astype(jnp.bfloat16),
        grad_heads,
        preferred_element_type=jnp.float32,
    )
    grad_scores = probs * (grad_probs - jnp.sum(probs * grad_probs, axis=-1, keepdims=True))
    grad_scores = grad_scores.astype(jnp.bfloat16)
    factor = HEAD ** (-0.5)
    grad_query = (
        jnp.einsum("nhqk,nkhd->nqhd", grad_scores, keys, preferred_element_type=jnp.float32)
        * factor
    )
    grad_keys = (
        jnp.einsum("nhqk,nqhd->nkhd", grad_scores, query, preferred_element_type=jnp.float32)
        * factor
    )
    stacked = jnp.stack([grad_query, grad_keys, grad_values], axis=2)
    return stacked.reshape(count, length, 3 * HEADS * HEAD)


def body(
    image_tokens,
    text_tokens,
    lengths,
    pair_count,
    img_qkv,
    img_out,
    img_up,
    img_down,
    img_proj,
    gain_one,
    txt_qkv,
    txt_out,
    gain_two,
    txt_up,
    txt_down,
    txt_proj,
    log_scale,
):
    pairs, img_len, width = image_tokens.shape
    txt_len = text_tokens.shape[1]
    row_index = lax.axis_index("row")
    col_index = lax.axis_index("col")
    row_count = lax.axis_size("row")
    col_count = lax.axis_size("col")
    valid_total = jnp.sum(pair_count).astype(jnp.float32)
    own_valid = (jnp.arange(pairs) < pair_count[row_index, col_index]).astype(jnp.float32)
    image_in = image_tokens.astype(jnp.float32)
    normed, _ = layer_norm_stats(image_in)
    mixed = project(normed.astype(jnp.bfloat16), img_qkv).astype(jnp.bfloat16)
    attended, _ = attend(mixed, jnp.ones((pairs, img_len), dtype=bool))
    after = image_in + project(attended, img_out)
    normed, _ = layer_norm_stats(after)
    hidden = jax.nn.gelu(project(normed.astype(jnp.bfloat16), img_up)).astype(jnp.bfloat16)
    output = after + project(hidden, img_down)
    pooled = jnp.mean(output, axis=1).astype(jnp.bfloat16)
    image_unit = unit_vector(project(pooled, img_proj)).astype(jnp.bfloat16)
    text_in = text_tokens.astype(jnp.float32)
    key_mask = jnp.arange(txt_len)[None, :] < lengths[:, None]
    norm_one, inv_one = layer_norm_stats(text_in)
    normed_one = (norm_one * gain_one).astype(jnp.bfloat16)
    mixed_txt = project(normed_one, txt_qkv).astype(jnp.bfloat16)
    attended_txt, log_total = attend(mixed_txt, key_mask)
    after_txt = text_in + project(attended_txt, txt_out)
    norm_two, inv_two = layer_norm_stats(after_txt)
    normed_two = (norm_two * gain_two).astype(jnp.bfloat16)
    hidden_pre = project(normed_two, txt_up)
    hidden_txt = jax.nn.gelu(hidden_pre).astype(jnp.bfloat16)
    output_txt = after_txt + project(hidden_txt, txt_down)
    pool_weights = key_mask.astype(jnp.float32) / lengths[:, None].astype(jnp.float32)
    pooled_txt = jnp.sum(output_txt * pool_weights[:, :, None], axis=1).astype(jnp.bfloat16)
    embedded = project(pooled_txt, txt_proj)
    text_unit = unit_vector(embedded)
    text_low = text_unit.astype(jnp.bfloat16)
    image_rows = lax.all_gather(image_unit, "col", axis=0, tiled=True)
    text_cols = lax.all_gather(text_low, "row", axis=0, tiled=True)
    scale = jnp.exp(log_scale[0])
    sims = scale * jnp.einsum(
        "ie,je->ij", image_rows, text_cols, preferred_element_type=jnp.float32
    )
    row_limit = jnp.repeat(pair_count[row_index], pairs)
    col_limit = jnp.repeat(pair_count[:, col_index], pairs)
    row_ok = jnp.arange(col_count * pairs) % pairs < row_limit
    col_ok = jnp.arange(row_count * pairs) % pairs < col_limit
    row_masked = jnp.where(col_ok[None, :], sims, floor_value)
    col_masked = jnp.where(row_ok[:, None], sims, floor_value)
    row_peak_part = jnp.max(row_masked, axis=1)
    col_peak_part = jnp.max(col_masked, axis=0)
    row_peak = lax.pmax(row_peak_part, "col")
    col_peak = lax.pmax(col_peak_part, "row")
    row_total = lax.psum(jnp.sum(jnp.exp(row_masked - row_peak[:, None]), axis=1), "col")
    col_total = lax.psum(jnp.sum(jnp.exp(col_masked - col_peak[None, :]), axis=0), "row")
    row_lse = row_peak + jnp.log(row_total)
    col_lse = col_peak + jnp.log(col_total)
    inv_pairs = 1.0 / (2.0 * valid_total)
    prob_row = jnp.exp(row_masked - row_lse[:, None])
    prob_col = jnp.exp(col_masked - col_lse[None, :])
    row_weight = row_ok.astype(jnp.float32)
    col_weight = col_ok.astype(jnp.float32)
    grad_sims = (prob_row * row_weight[:, None] + prob_col * col_weight[None, :]) * inv_pairs
    scale_part = jnp.sum(grad_sims * sims)
    grad_cosine = (scale * grad_sims).astype(jnp.bfloat16)
    grad_unit = lax.psum_scatter(
        lax.dot_general(
            grad_cosine, image_rows, (((0,), (0,)), ((), ())), preferred_element_type=jnp.float32
        ),
        "row",
        scatter_dimension=0,
        tiled=True,
    )
    own_cos = jnp.sum(image_unit.astype(jnp.float32) * text_low.astype(jnp.float32), axis=1)
    own_row_lse = lax.dynamic_slice_in_dim(row_lse, col_index * pairs, pairs)
    own_col_lse = lax.dynamic_slice_in_dim(col_lse, row_index * pairs, pairs)
    loss_part = jnp.sum(own_valid * (own_row_lse + own_col_lse - 2.0 * scale * own_cos)) * inv_pairs
    diag_grad = -2.0 * inv_pairs * own_valid
    scale_part = scale_part + jnp.sum(diag_grad * scale * own_cos)
    diag_low = lax.optimization_barrier((scale * diag_grad).astype(jnp.bfloat16)).astype(
        jnp.float32
    )
    grad_unit = grad_unit + diag_low[:, None] * image_unit.astype(jnp.float32)
    inv_length = lax.rsqrt(jnp.sum(embedded * embedded, axis=-1, keepdims=True) + epsilon)
    grad_embed = inv_length * (
        grad_unit - text_unit * jnp.sum(grad_unit * text_unit, axis=-1, keepdims=True)
    )
    grad_embed = grad_embed.astype(jnp.bfloat16)
    grad_proj = jnp.einsum("nd,ne->de", pooled_txt, grad_embed, preferred_element_type=jnp.float32)
    grad_pooled = jnp.einsum("ne,de->nd", grad_embed, txt_proj, preferred_element_type=jnp.float32)
    grad_output = grad_pooled[:, None, :] * pool_weights[:, :, None]
    grad_branch = grad_output.astype(jnp.bfloat16)
    grad_down = jnp.einsum(
        "nlf,nld->fd", hidden_txt, grad_branch, preferred_element_type=jnp.float32
    )
    grad_hidden = jnp.einsum(
        "nld,fd->nlf", grad_branch, txt_down, preferred_element_type=jnp.float32
    )
    _, gelu_back = jax.vjp(jax.nn.gelu, hidden_pre)
    grad_pre = gelu_back(grad_hidden)[0].astype(jnp.bfloat16)
    grad_up = jnp.einsum("nld,nlf->df", normed_two, grad_pre, preferred_element_type=jnp.float32)
    grad_normed_two = jnp.einsum(
        "nlf,df->nld", grad_pre, txt_up, preferred_element_type=jnp.float32
    )
    grad_gain_two = jnp.sum(grad_normed_two * norm_two, axis=(0, 1))
    grad_after = grad_output + layer_norm_back(grad_normed_two * gain_two, norm_two, inv_two)
    grad_attn_out = grad_after.astype(jnp.bfloat16)
    grad_out = jnp.einsum(
        "nld,nle->de", attended_txt, grad_attn_out, preferred_element_type=jnp.float32
    )
    grad_attended = jnp.einsum(
        "nle,de->nld", grad_attn_out, txt_out, preferred_element_type=jnp.float32
    ).astype(jnp.bfloat16)
    grad_mixed = attend_back(mixed_txt, key_mask, log_total, grad_attended).astype(jnp.bfloat16)
    grad_qkv = jnp.einsum("nld,nle->de", normed_one, grad_mixed, preferred_element_type=jnp.float32)
    grad_normed_one = jnp.einsum(
        "nle,de->nld", grad_mixed, txt_qkv, preferred_element_type=jnp.float32
    )
    grad_gain_one = jnp.sum(grad_normed_one * norm_one, axis=(0, 1))
    grad_in = grad_after + layer_norm_back(grad_normed_one * gain_one, norm_one, inv_one)
    text_grad = grad_in.astype(jnp.bfloat16)
    summed = lax.psum(
        (
            grad_qkv,
            grad_out,
            grad_gain_one,
            grad_gain_two,
            grad_up,
            grad_down,
            grad_proj,
            loss_part,
            scale_part,
        ),
        ("row", "col"),
    )
    (
        sum_qkv,
        sum_out,
        sum_gain_one,
        sum_gain_two,
        sum_up,
        sum_down,
        sum_proj,
        loss_total,
        scale_total,
    ) = summed
    return (
        loss_total.reshape(1),
        text_grad,
        sum_gain_one,
        sum_qkv,
        sum_out,
        sum_gain_two,
        sum_up,
        sum_down,
        sum_proj,
        scale_total.reshape(1),
    )


def solution(mesh):
    return jax.shard_map(
        body,
        mesh=mesh,
        in_specs=(
            P(("row", "col"), None, None),
            P(("row", "col"), None, None),
            P(("row", "col")),
            P(),
            P(),
            P(),
            P(),
            P(),
            P(),
            P(),
            P(),
            P(),
            P(),
            P(),
            P(),
            P(),
            P(),
        ),
        out_specs=(P(), P(("row", "col"), None, None), P(), P(), P(), P(), P(), P(), P(), P()),
        check_vma=False,
    )
```

profile of v0, /device:TPU:1, one launch (start us, length us, event | category | flops | bytes accessed | tf_op | source)
XLA Modules:
  0.0 727.5 jit_solution(7048061893108983096)
XLA Ops:
  13.6 11.5 %convolution_convert_fusion = bf16[128,50,1152]{2,0,1:T(8,128)(2,1)} fusion(bf16[128,50,384]{2,0,1:T(8,128)(2,1)S(1)} %copy-done.5, f32[128,50]{0,1:T(8,128)S(1)} %add_rsqrt_fusion.1, f32[128,50]{0,1:T(8,128)S(1)} %broadcast_multiply_fusion.1, bf16[384,1152]{1,0:T(8,128)(2,1)S(1)} %copy-done.53), kind=kOutput, calls=%fused_computation.13 | convolution fusion | flops 5679513600 | bytes 20596736 | tf_op jit(solution)/shard_map/...d,de->...e/dot_general | solution.py:29
  25.1 20.8 %copy.72 = bf16[128,50,1152]{0,2,1:T(8,128)(2,1)} copy(bf16[128,50,1152]{2,0,1:T(8,128)(2,1)} %convolution_convert_fusion) | data formatting | bytes 29491200 | tf_op jit(solution)/shard_map/convert_element_type | solution.py:119
  46.0 15.0 %fusion.139 = (bf16[128,50,1,6,64]{0,4,3,2,1:T(8,128)(2,1)}, bf16[128,50,1,6,64]{0,4,3,2,1:T(8,128)(2,1)}, bf16[128,50,1,6,64]{0,4,3,2,1:T(8,128)(2,1)}) fusion(bf16[128,50,3,6,64]{0,4,3,2,1:T(8,128)(2,1)} %bitcast.142), kind=kLoop, calls=%fused_computation.209 | loop fusion | bytes 29491200 | tf_op jit(solution)/shard_map/slice | solution.py:39
  61.0 18.4 %copy.111 = bf16[128,50,1,6,64]{4,1,3,0,2:T(8,128)(2,1)} copy(bf16[128,50,1,6,64]{0,4,3,2,1:T(8,128)(2,1)} %get-tuple-element.67) | data formatting | bytes 9830400
  79.3 18.4 %copy.112 = bf16[128,50,1,6,64]{4,1,3,0,2:T(8,128)(2,1)} copy(bf16[128,50,1,6,64]{0,4,3,2,1:T(8,128)(2,1)} %get-tuple-element.68) | data formatting | bytes 9830400
  97.7 18.5 %copy.113 = bf16[128,50,1,6,64]{4,1,3,0,2:T(8,128)(2,1)} copy(bf16[128,50,1,6,64]{0,4,3,2,1:T(8,128)(2,1)} %get-tuple-element.69) | data formatting | bytes 9830400
  116.2 14.9 %fusion.24 = f32[128,6,50,50]{2,3,1,0:T(8,128)} fusion(bf16[128,50,1,6,64]{4,1,3,0,2:T(8,128)(2,1)} %copy.113, bf16[128,50,1,6,64]{4,1,3,0,2:T(8,128)(2,1)} %copy.112), kind=kOutput, calls=%fused_computation.33 | convolution fusion | flops 245760000 | bytes 17510400 | tf_op jit(solution)/shard_map/nqhd,nkhd->nhqk/dot_general | solution.py:43
  131.1 25.4 %fusion.142 = (f32[128,6,50]{2,1,0:T(8,128)S(1)}, f32[128,6,50,50]{2,3,1,0:T(8,128)}) fusion(f32[128,6,50,50]{2,3,1,0:T(8,128)} %fusion.24), kind=kOutput, calls=%fused_computation.212 | output fusion | flops 7680049 | bytes 15513600 | tf_op jit(solution)/shard_map/sub | solution.py:54
  156.5 17.4 %convert_bitcast_fusion = bf16[128,50,6,64]{3,1,2,0:T(8,128)(2,1)} fusion(f32[128,6,50,50]{2,3,1,0:T(8,128)} %get-tuple-element.80, f32[128,6,50]{2,1,0:T(8,128)S(1)} %get-tuple-element.79, bf16[128,50,1,6,64]{4,1,3,0,2:T(8,128)(2,1)} %copy.111), kind=kOutput, calls=%fused_computation.37 | convolution fusion | flops 252057600 | bytes 17664000 | tf_op jit(solution)/shard_map/nhqk,nkhd->nqhd/dot_general | solution.py:57
  173.9 16.2 %copy.77 = bf16[128,50,6,64]{0,3,2,1:T(8,128)(2,1)} copy(bf16[128,50,6,64]{3,1,2,0:T(8,128)(2,1)} %convert_bitcast_fusion) | data formatting | bytes 9830400 | tf_op jit(solution)/shard_map/convert_element_type | solution.py:58
  190.1 7.7 %fusion.143 = (f32[128,50]{0,1:T(8,128)S(1)}, f32[128,50,384]{2,0,1:T(8,128)S(1)}) fusion(bf16[128,50,384]{0,2,1:T(8,128)(2,1)} %bitcast.143, bf16[384,384]{1,0:T(8,128)(2,1)S(1)} %copy-done.23, bf16[128,50,384]{2,0,1:T(8,128)(2,1)} %param.17), kind=kOutput, calls=%fused_computation.213 | convolution fusion | flops 1894803200 | bytes 19981312 | tf_op jit(solution)/shard_map/...d,de->...e/dot_general | solution.py:29
  201.7 26.7 %add_reduce_fusion = f32[128,384]{1,0:T(8,128)S(1)} fusion(f32[128,50,384]{2,0,1:T(8,128)} %copy-done.6, f32[128,50]{0,1:T(8,128)S(1)} %add_rsqrt_fusion, f32[128,50]{0,1:T(8,128)S(1)} %broadcast_multiply_fusion, bf16[1536,384]{1,0:T(8,128)(2,1)} %param.24, bf16[384,1536]{1,0:T(8,128)(2,1)} %param.23), kind=kOutput, calls=%fused_computation.42 | convolution fusion | flops 15200206848 | bytes 12437504 | tf_op jit(solution)/shard_map/...d,de->...e/dot_general | solution.py:29
  239.7 6.7 copy.80
  251.7 6.2 copy.116
  270.0 7.3 %fusion.59 = f32[128,6,16,16]{2,3,1,0:T(8,128)} fusion(bf16[128,16,1,6,64]{4,1,3,0,2:T(8,128)(2,1)} %copy.115, bf16[128,16,1,6,64]{4,1,3,0,2:T(8,128)(2,1)} %copy.114), kind=kOutput, calls=%fused_computation.76 | convolution fusion | flops 25165824 | bytes 3932160 | tf_op jit(solution)/shard_map/nqhd,nkhd->nhqk/dot_general | solution.py:43
  284.6 6.2 copy.85
  290.7 6.3 convert_bitcast_fusion.2
  307.9 9.8 %multiply_convert_fusion = (bf16[128,16,1536]{2,0,1:T(8,128)(2,1)S(1)}, f32[128,16,1536]{2,0,1:T(8,128)}) fusion(bf16[384,1536]{1,0:T(8,128)(2,1)S(1)} %copy-done, f32[128,16,384]{2,0,1:T(8,128)} %copy-done.1, f32[384]{0:T(512)} %param.29, f32[128,16]{0,1:T(8,128)S(1)} %add_rsqrt_fusion.2, f32[128,16]{0,1:T(8,128)S(1)} %broadcast_multiply_fusion.6), kind=kOutput, calls=%fused_computation.29 | convolution fusion | flops 2447376384 | bytes 23217664 | tf_op jit(solution)/shard_map/...d,de->...e/dot_general | solution.py:29
  333.4 31.7 %pmax.14 = f32[2048]{0:T(1024)} all-reduce(f32[2048]{0:T(1024)} %get-tuple-element.48), channel_id=1, replica_groups=mesh['row'=2,'col'=16] {'col'}, use_global_device_ids=true, to_apply=%region_17.18 | all-reduce | flops 2048 | bytes 16384 | tf_op jit(solution)/shard_map/pmax | solution.py:158
  372.9 34.5 %psum.77 = f32[2048]{0:T(1024)} all-reduce(f32[2048]{0:T(1024)} %get-tuple-element.46), channel_id=1, replica_groups=mesh['row'=2,'col'=16] {'col'}, use_global_device_ids=true, to_apply=%region_19.20 | all-reduce | flops 2048 | bytes 16384 | tf_op jit(solution)/shard_map/psum | solution.py:160
  421.4 6.8 copy.95
  437.0 7.8 %convolution_bitcast_fusion = f32[1536,384]{1,0:T(8,128)} fusion(bf16[128,16,1536]{2,0,1:T(8,128)(2,1)} %copy-done.55, f32[128,384]{1,0:T(8,128)S(1)} %fusion.144, f32[128,16]{0,1:T(8,128)} %convert_divide_fusion), kind=kOutput, calls=%fused_computation.92 | convolution fusion | flops 2417491968 | bytes 8855552 | tf_op jit(solution)/shard_map/nlf,nld->fd/dot_general | solution.py:199
  444.8 12.3 %fusion.20 = bf16[128,16,1536]{2,0,1:T(8,128)(2,1)S(1)} fusion(f32[128,16,1536]{2,0,1:T(8,128)} %get-tuple-element.78, f32[128,384]{1,0:T(8,128)S(1)} %fusion.144, f32[128,16]{0,1:T(8,128)S(1)} %copy-done.32, bf16[1536,384]{1,0:T(8,128)(2,1)S(1)} %copy-done.52), kind=kOutput, calls=%fused_computation.28 | convolution fusion | flops 2480406528 | bytes 20258816 | tf_op jit(solution)/shard_map/nld,fd->nlf/dot_general | solution.py:202
  474.6 6.2 copy.89
  480.8 7.3 %fusion.64 = f32[128,6,16,16]{2,3,1,0:T(8,128)} fusion(bf16[128,16,6,64]{3,1,2,0:T(8,128)(2,1)} %copy.89, bf16[128,16,1,6,64]{4,1,3,0,2:T(8,128)(2,1)} %copy.116), kind=kOutput, calls=%fused_computation.81 | convolution fusion | flops 25165824 | bytes 3932160 | tf_op jit(solution)/shard_map/nqhd,nkhd->nhqk/dot_general | solution.py:66
  488.1 6.5 copy.91
  497.2 6.8 copy.93
  518.8 12.8 %copy.96 = bf16[128,16,3,6,64]{0,4,3,2,1:T(8,128)(2,1)} copy(bf16[128,16,3,6,64]{4,1,3,0,2:T(8,128)(2,1)} %pad_maximum_fusion) | data formatting | bytes 9437184 | tf_op jit(solution)/shard_map/stack | solution.py:86
  531.6 6.4 convolution_bitcast_fusion.2
  546.4 8.7 %fusion.53 = (f32[384]{0:T(512)S(1)}, f32[128,16]{0,1:T(8,128)S(1)}, f32[128,16]{0,1:T(8,128)S(1)}, f32[128,16,384]{2,0,1:T(8,128)}) fusion(f32[128,16]{0,1:T(8,128)S(1)} %copy-done.34, f32[128,16]{0,1:T(8,128)S(1)} %copy-done.26, bf16[128,16,384]{2,1,0:T(8,128)(2,1)S(1)} %copy-done.10, f32[384]{0:T(512)S(1)} %copy-done.50, ...), kind=kOutput, calls=%fused_computation.70 | convolution fusion | flops 1819012736 | bytes 10357760 | tf_op jit(solution)/shard_map/nle,de->nld/dot_general | solution.py:222
  555.1 42.1 %all-reduce = (f32[1]{0:T(128)}, f32[384]{0:T(512)}, f32[384]{0:T(512)}, f32[1]{0:T(128)}) all-reduce(f32[1]{0:T(128)} %bitcast.25, f32[384]{0:T(512)S(1)} %get-tuple-element.42, f32[384]{0:T(512)S(1)} %copy-done.46, f32[1]{0:T(128)} %bitcast.38), channel_id=1, replica_groups=mesh['row'=2,'col'=16] {'row','col'}, use_global_device_ids=true, to_apply=%region_27.28 | all-reduce | flops 770 | bytes 6160 | tf_op jit(solution)/shard_map/psum | solution.py:228
  602.9 110.2 %all-reduce.4.cloned.1.call-done = (f32[384,1152]{1,0:T(8,128)}, f32[384,384]{1,0:T(8,128)}, f32[384,1536]{1,0:T(8,128)}, f32[1536,384]{1,0:T(8,128)}, f32[384,384]{1,0:T(8,128)}) async-done(((f32[384,1152]{1,0:T(8,128)}, f32[384,384]{1,0:T(8,128)}, f32[384,1536]{1,0:T(8,128)}, f32[1536,384]{1,0:T(8,128)}, f32[384,384]{1,0:T(8,128)}), (f32[384,1152]{1,0:T(8,128)}, f32[384,384]{1,0:T(8,128)}, ...) | async-done | bytes 7667728 | tf_op jit(solution)/shard_map/psum | solution.py:228
  (198 shorter events, 155.8 us)
Async XLA Ops:
  7.2 300.7 %copy-start = (bf16[384,1536]{1,0:T(8,128)(2,1)S(1)}, bf16[384,1536]{1,0:T(8,128)(2,1)}, u32[]{:S(2)}) copy-start(bf16[384,1536]{1,0:T(8,128)(2,1)} %param.30) | copy-start | bytes 3538948
  7.2 322.0 %all-gather.2.cloned.1.call-start = ((), (), s32[]{:S(2)}) async-start(), calls=%async_computation.1 | async-start | bytes 1671168 | tf_op jit(solution)/shard_map/all_gather | solution.py:144
  7.2 4.0 copy-start.5
  173.9 16.2 %copy-start.23 = (bf16[384,384]{1,0:T(8,128)(2,1)S(1)}, bf16[384,384]{1,0:T(8,128)(2,1)}, u32[]{:S(2)}) copy-start(bf16[384,384]{1,0:T(8,128)(2,1)} %param.22) | copy-start | bytes 884740
  201.7 26.7 %copy-start.22 = (bf16[384,384]{1,0:T(8,128)(2,1)S(1)}, bf16[384,384]{1,0:T(8,128)(2,1)}, u32[]{:S(2)}) copy-start(bf16[384,384]{1,0:T(8,128)(2,1)} %param.25) | copy-start | bytes 884740
  201.7 28.5 %copy-start.45 = (s32[128]{0:T(128)S(1)}, s32[128]{0:T(128)}, u32[]{:S(2)}) copy-start(s32[128]{0:T(128)} %param.19) | copy-start | bytes 1540
  201.7 29.2 %copy-start.39 = (s32[2,16]{1,0:T(2,128)S(1)}, s32[2,16]{1,0:T(2,128)}, u32[]{:S(2)}) copy-start(s32[2,16]{1,0:T(2,128)} %param.20) | copy-start | bytes 388
  201.7 31.9 %copy-start.10 = (bf16[128,16,384]{2,1,0:T(8,128)(2,1)S(1)}, bf16[128,16,384]{2,1,0:T(8,128)(2,1)}, u32[]{:S(2)}) copy-start(bf16[128,16,384]{2,1,0:T(8,128)(2,1)} %param.18) | copy-start | bytes 4718596
  228.4 6.4 copy-start.49
  228.8 4.2 copy-start.42
  230.2 200.4 %reduce-scatter.2.cloned.1.call-start = ((), (), s32[]{:S(2)}) async-start(), calls=%async_computation.2 | async-start | bytes 589824 | tf_op jit(solution)/shard_map/reduce_scatter | solution.py:172
  230.2 53.1 %copy-start.28 = (pred[128,16]{0,1:T(8,128)(4,1)}, pred[128,16]{0,1:T(8,128)(4,1)S(1)}, u32[]{:S(2)}) copy-start(pred[128,16]{0,1:T(8,128)(4,1)S(1)} %iota_compare_fusion) | copy-start | bytes 6148
  234.9 4.8 copy-start.33
  307.9 9.8 %copy-start.2 = (f32[128,16,384]{2,0,1:T(8,128)S(1)}, f32[128,16,384]{2,0,1:T(8,128)}, u32[]{:S(2)}) copy-start(f32[128,16,384]{2,0,1:T(8,128)} %copy-done.1) | copy-start | bytes 9437188
  307.9 9.8 %copy-start.31 = (f32[128,16]{0,1:T(8,128)S(1)}, f32[128,16]{0,1:T(8,128)}, u32[]{:S(2)}) copy-start(f32[128,16]{0,1:T(8,128)} %convert_divide_fusion) | copy-start | bytes 24580
  307.9 9.8 %copy-start.51 = (bf16[1536,384]{1,0:T(8,128)(2,1)S(1)}, bf16[1536,384]{1,0:T(8,128)(2,1)}, u32[]{:S(2)}) copy-start(bf16[1536,384]{1,0:T(8,128)(2,1)} %param.31) | copy-start | bytes 3538948
  317.7 10.1 %copy-start.40 = (s32[2,16]{1,0:T(2,128)S(1)}, s32[2,16]{1,0:T(2,128)}, u32[]{:S(2)}) copy-start(s32[2,16]{1,0:T(2,128)} %param.20) | copy-start | bytes 388
  317.8 10.1 %copy-start.47 = (s32[2]{0:T(128)S(1)}, s32[2]{0:T(128)}, u32[]{:S(2)}) copy-start(s32[2]{0:T(128)} %dynamic-slice_reduce_fusion) | copy-start | bytes 28
  321.6 6.2 copy-start.43
  419.0 294.1 %all-reduce.4.cloned.1.call-start = ((), (), s32[]{:S(2)}) async-start(), calls=%async_computation.3 | async-start | bytes 15335424 | tf_op jit(solution)/shard_map/psum | solution.py:228
  437.0 7.9 %copy-start.32 = (f32[128,16]{0,1:T(8,128)S(1)}, f32[128,16]{0,1:T(8,128)}, u32[]{:S(2)}) copy-start(f32[128,16]{0,1:T(8,128)} %convert_divide_fusion) | copy-start | bytes 24580
  437.0 7.9 %copy-start.52 = (bf16[1536,384]{1,0:T(8,128)(2,1)S(1)}, bf16[1536,384]{1,0:T(8,128)(2,1)}, u32[]{:S(2)}) copy-start(bf16[1536,384]{1,0:T(8,128)(2,1)} %param.31) | copy-start | bytes 3538948
  444.8 12.3 %copy-start.3 = (f32[128,16,384]{2,0,1:T(8,128)S(1)}, f32[128,16,384]{2,0,1:T(8,128)}, u32[]{:S(2)}) copy-start(f32[128,16,384]{2,0,1:T(8,128)} %copy-done.1) | copy-start | bytes 9437188
  444.8 12.3 %copy-start.35 = (f32[384]{0:T(512)S(1)}, f32[384]{0:T(512)}, u32[]{:S(2)}) copy-start(f32[384]{0:T(512)} %param.29) | copy-start | bytes 4612
  488.0 6.5 copy-start.29
  504.0 4.2 copy-start.7
  504.0 4.7 copy-start.9
  518.8 12.8 %copy-start.26 = (f32[128,16]{0,1:T(8,128)S(1)}, f32[128,16]{0,1:T(8,128)}, u32[]{:S(2)}) copy-start(f32[128,16]{0,1:T(8,128)} %copy-done.25) | copy-start | bytes 24580
  518.8 12.8 %copy-start.34 = (f32[128,16]{0,1:T(8,128)S(1)}, f32[128,16]{0,1:T(8,128)}, u32[]{:S(2)}) copy-start(f32[128,16]{0,1:T(8,128)} %copy-done.33) | copy-start | bytes 24580
  518.8 12.8 %copy-start.50 = (f32[384]{0:T(512)S(1)}, f32[384]{0:T(512)}, u32[]{:S(2)}) copy-start(f32[384]{0:T(512)} %param.26) | copy-start | bytes 4612
  538.1 5.1 copy-start.48
  546.4 8.7 %copy-start.46 = (f32[384]{0:T(512)S(1)}, f32[384]{0:T(512)}, u32[]{:S(2)}) copy-start(f32[384]{0:T(512)} %get-tuple-element.40) | copy-start | bytes 4612
  (27 other events, 48.3 us)
Sparse Core Ops, SparseCore 0:
  230.3 42.3 all-gather.1
  419.1 11.4 reduce-scatter.1
  538.2 174.7 all-reduce.3
where the time goes:
time: 739 us; the launch traced here: 727 us
  local copies, waits for them, and re-layouts  216 us (29%)
  matrix products  189 us (26%)
  blocking collectives  123 us (17%)
  waiting for transfers between devices  113 us (15%)
  other arithmetic  69.3 us (9%)
  between operations  18.3 us (2%)
    psum x1, waiting for transfers between devices, body(): lax.psum((grad_qkv, grad_out, grad_gain_one, grad_gain_two, grad_up, grad...  110 us
    unnamed x124, local copies, waits for them, and re-layouts  91.2 us
    dot_general x9, matrix products, project(): jnp.einsum('...d,de->...e', left, right, preferred_element_type=jnp.float32)  67.5 us
    psum x1, blocking collectives, body(): lax.psum((grad_qkv, grad_out, grad_gain_one, grad_gain_two, grad_up, grad...  42.1 us
    psum x1, blocking collectives, body(): lax.psum(jnp.sum(jnp.exp(row_masked - row_peak[:, None]), axis=1), 'col')  34.5 us
    pmax x1, blocking collectives, body(): row_peak = lax.pmax(row_peak_part, 'col')  31.7 us
    sub x1, other arithmetic, attend(): expo = jnp.exp(scores - peak)  25.4 us
    dot_general x2, matrix products, attend(): jnp.einsum('nhqk,nkhd->nqhd', probs, values, preferred_element_type=jnp.f...  23.7 us
  transfers between devices with their start and end apart: 3, of which 2 were waited for; matrix products, arithmetic and copies ran while one was open for 16% of the time, Pallas kernels for 0%

commit v1 on v0

v1 whole, which is shorter than its diff:
```python
import functools
import jax
import jax.numpy as jnp
from jax import lax
from jax.experimental import pallas as pl
from jax.experimental.pallas import tpu as pltpu
from jax.sharding import PartitionSpec as P

HEADS = 6
HEAD = 64
epsilon = 1e-6
F32 = jnp.float32
BF16 = jnp.bfloat16
GELU_A = 0.7978845608028654
GELU_B = 0.7978845608028654 * 0.044715
SAFE = 60.0
GROUP = 8
IMAGE_NB = 16
USE = 2
ACTIVE = 3
ORDER = 4
ORDER_ALL = 8
IMAGE_BLOCKS = 12
PLAN = 28
NB = 32
QB = 16
T1_LIMIT = 20
T2_LIMIT = 20
BACK_LIMIT = 30
SIM_LIMIT = 12


def mm(a, b):
    return lax.dot_general(a, b, (((1,), (0,)), ((), ())), preferred_element_type=F32)


def mm_t(a, b):
    return lax.dot_general(a, b, (((1,), (1,)), ((), ())), preferred_element_type=F32)


def mm_split(a, b):
    hi = a.astype(BF16)
    lo = (a - hi.astype(F32)).astype(BF16)
    return mm(hi, b) + mm(lo, b)


def normed(v):
    c = v - jnp.mean(v, axis=-1, keepdims=True)
    return c * lax.rsqrt(jnp.mean(c * c, axis=-1, keepdims=True) + epsilon)


def unit_scale(e):
    return lax.rsqrt(jnp.sum(e * e, axis=-1, keepdims=True) + epsilon)


def lane_halves():
    lane = lax.broadcasted_iota(jnp.int32, (1, 128), 1)
    low = (lane < HEAD).astype(F32)
    return low, 1.0 - low


def image_kernel(first, cut, plan_ref, x_ref, recv_ref, wqkv_ref, wout_ref, wup_ref, wdown_ref, wproj_ref, unit_ref, qkv, att, hsum, xsum):
    step = pl.program_id(0)
    length, nb, width = x_ref.shape
    rows = length * GROUP

    @pl.when(step == 0)
    def _():
        qkv[:, :, rows:, :] = jnp.zeros(qkv.shape[:2] + (qkv.shape[2] - rows, 128), F32)
        hsum[...] = jnp.zeros_like(hsum)
        xsum[...] = jnp.zeros_like(xsum)

    block = first // nb + step

    @pl.when(plan_ref[IMAGE_BLOCKS + block * (nb // GROUP)] > 0)
    def _():
        image_block(step, block, cut, plan_ref, x_ref, recv_ref, wqkv_ref, wout_ref, wup_ref, qkv, att, hsum, xsum)

    @pl.when(step == pl.num_programs(0) - 1)
    def _():
        pooled = xsum[...] * (1.0 / length) + mm_split(hsum[...] * (0.5 / length), wdown_ref[...])
        e = mm(pooled.astype(BF16), wproj_ref[...])
        unit_ref[...] = (e * unit_scale(e)).astype(BF16)


def image_block(step, block, cut, plan_ref, x_ref, recv_ref, wqkv_ref, wout_ref, wup_ref, qkv, att, hsum, xsum):
    length, nb, width = x_ref.shape
    rows = length * GROUP
    slots = qkv.shape[2] // GROUP
    tiles = width // 128
    ff = wup_ref.shape[1]
    groups = nb // GROUP
    moved = (plan_ref[USE] > 0) & (block >= cut // nb)

    def tokens(g):
        x = x_ref[...].astype(F32)
        if recv_ref is not None:
            x = jnp.where(moved, recv_ref[...].astype(F32), x)
        return x[:, g * GROUP : (g + 1) * GROUP, :].reshape(rows, width)

    low, high = lane_halves()
    key_row = lax.broadcasted_iota(jnp.int32, (2 * slots, 128), 0)
    key_lane = lax.broadcasted_iota(jnp.int32, (2 * slots, 128), 1)
    own_head = (key_row < slots) == (key_lane < HEAD)
    real = jnp.where(key_row < slots, key_row, key_row - slots) < length
    ones = jnp.where(own_head & real, 1.0, 0.0).astype(BF16)

    def pairs_of(g):
        return pl.ds(pl.multiple_of(step * nb + g * GROUP, GROUP), GROUP)

    def scores(g, p, h):
        at = pl.ds(p, slots, stride=GROUP)
        q = qkv[g, h, at, :].astype(BF16) * BF16(HEAD**-0.5)
        k = qkv[g, tiles + h, at, :]
        return mm_t(q, jnp.concatenate([k * low, k * high], axis=0).astype(BF16))

    def weighted(g, p, h, e):
        at = pl.ds(p, slots, stride=GROUP)
        v = qkv[g, 2 * tiles + h, at, :]
        vbd = jnp.concatenate([v * low, v * high], axis=0).astype(BF16)
        o = mm(e.astype(BF16), jnp.concatenate([vbd, ones], axis=1))
        att[g, h, at, :] = o[:, :128] / o[:, 128:]

    def projected(g):
        n1 = normed(tokens(g)).astype(BF16)
        for c in range(tiles):
            made = mm(n1, wqkv_ref[:, c * width : (c + 1) * width])
            for h in range(tiles):
                qkv[g, c * tiles + h, :rows, :] = made[:, h * 128 : h * 128 + 128]

    def after_attention(g):
        heads = jnp.concatenate([att[g, h, :rows, :] for h in range(tiles)], axis=1)
        x1 = tokens(g) + mm(heads.astype(BF16), wout_ref[...])
        xsum[pairs_of(g), :] = jnp.sum(x1.reshape(length, GROUP, width), axis=0)
        return normed(x1).astype(BF16)

    def gelu_sum(g, u, c):
        made = u * (1.0 + jnp.tanh(u * (GELU_A + GELU_B * (u * u))))
        hsum[pairs_of(g), pl.ds(c, 256)] = jnp.sum(made.reshape(length, GROUP, 256), axis=0)

    def feed_steps(g):
        n2 = after_attention(g)
        before = None
        for c in range(0, ff, 256):
            u = mm(n2, wup_ref[:, c : c + 256])
            if before is not None:
                gelu_sum(g, *before)
            before = (u, c)
            yield
        gelu_sum(g, *before)
        yield

    largest = jnp.zeros((slots, 2 * slots), F32)
    units = [(p, h) for p in range(GROUP) for h in range(tiles)]
    ahead = 3
    feed = iter(())
    projected(0)
    for g in range(groups):
        s_list, e_list = {}, {}
        for k in range(len(units) + 2 * ahead):
            if k < len(units):
                s_list[k] = scores(g, *units[k])
            if 0 <= k - ahead < len(units):
                s = s_list.pop(k - ahead)
                largest = jnp.maximum(largest, jnp.abs(s))
                e_list[k - ahead] = jnp.exp(s)
            if 0 <= k - 2 * ahead < len(units):
                weighted(g, *units[k - 2 * ahead], e_list.pop(k - 2 * ahead))
            if k % 4 == 2:
                next(feed, None)
            if k == len(units) // 2 and g + 1 < groups:
                projected(g + 1)
        for _ in feed:
            pass
        feed = feed_steps(g)
    for _ in feed:
        pass

    @pl.when(jnp.logical_not(jnp.max(largest) <= SAFE))
    def _():
        key = lax.broadcasted_iota(jnp.int32, (1, 2 * slots), 1)
        in_low = key < slots
        for_low = key < length
        for_high = (key >= slots) & (key < slots + length)
        @pl.loop(0, groups)
        def _(g):
            @pl.loop(0, GROUP)
            def _(p):
                @pl.loop(0, tiles)
                def _(h):
                    s = scores(g, p, h)
                    top_low = jnp.max(jnp.where(for_low, s, -1e30), axis=1, keepdims=True)
                    top_high = jnp.max(jnp.where(for_high, s, -1e30), axis=1, keepdims=True)
                    s = jnp.where(for_low | for_high, s, -1e30) - jnp.where(in_low, top_low, top_high)
                    weighted(g, p, h, jnp.exp(s))

        for g in range(groups):
            n2 = after_attention(g)

            @pl.loop(0, ff // 256)
            def _(c):
                at = pl.multiple_of(c * 256, 256)
                gelu_sum(g, mm(n2, wup_ref[:, pl.ds(at, 256)]), at)


def fixed(shape):
    zeros = (0,) * len(shape)
    return pl.BlockSpec(shape, lambda *_: zeros, pipeline_mode=pl.Buffered(1))


def image_tower(plan, tokens, received, first, count, cut, nb, cost, wqkv, wout, wup, wdown, wproj):
    length, _, width = tokens.shape
    slots = -(-length // 8) * 8
    ff = wup.shape[1]
    weights = (wqkv, wout, wup, wdown, wproj)
    at = first // nb
    specs = [pl.BlockSpec((length, nb, width), lambda i, plan: (0, at + i, 0))]
    if received is None:
        kernel = lambda plan_ref, x_ref, *refs: image_kernel(first, cut, plan_ref, x_ref, None, *refs)
        arrays = (tokens,)
    else:
        kernel = functools.partial(image_kernel, first, cut)
        last = received.shape[1] // nb - 1
        specs.append(
            pl.BlockSpec((length, nb, width), lambda i, plan: (0, jnp.clip(at + i - cut // nb, 0, last), 0))
        )
        arrays = (tokens, received)
    return pl.pallas_call(
        kernel,
        grid_spec=pltpu.PrefetchScalarGridSpec(
            num_scalar_prefetch=1,
            grid=(count // nb,),
            in_specs=specs + [fixed(w.shape) for w in weights],
            out_specs=pl.BlockSpec((count, width), lambda i, plan: (0, 0)),
            scratch_shapes=[
                pltpu.VMEM((nb // GROUP, 3 * width // 128, slots * GROUP, 128), F32),
                pltpu.VMEM((nb // GROUP, width // 128, slots * GROUP, 128), F32),
                pltpu.VMEM((count, ff), F32),
                pltpu.VMEM((count, width), F32),
            ],
        ),
        out_shape=jax.ShapeDtypeStruct((count, width), BF16),
        compiler_params=pltpu.CompilerParams(vmem_limit_bytes=60 * 2**20),
        cost_estimate=pl.CostEstimate(
            flops=int(cost * 2 * count * length * width * (4 * width + ff)),
            bytes_accessed=int(cost * (count * length * width * 2 + 4 * 2**20)),
            transcendentals=int(cost * count * length * ff),
        ),
        name="image_block",
    )(plan, *arrays, *weights)


def mm_tn(a, b):
    return lax.dot_general(a, b, (((0,), (0,)), ((), ())), preferred_element_type=F32)


def stats(v):
    c = v - jnp.mean(v, axis=-1, keepdims=True)
    inv = lax.rsqrt(jnp.mean(c * c, axis=-1, keepdims=True) + epsilon)
    return c * inv, inv


def norm_back(g, n, inv):
    return inv * (
        g - jnp.mean(g, axis=-1, keepdims=True) - n * jnp.mean(g * n, axis=-1, keepdims=True)
    )


def staggered(stages, units, ahead):
    kept = [dict() for _ in stages]
    for k in range(len(units) + (len(stages) - 1) * ahead):
        for at, stage in enumerate(stages):
            u = k - at * ahead
            if 0 <= u < len(units):
                made = stage(units[u], *([kept[at - 1].pop(u)] if at else []))
                kept[at][u] = made


def group_loop(stages, rows, width):
    @pl.loop(0, rows // 256)
    def _(half):
        first = half * 2
        units = [(first + g, h) for g in range(2) for h in range(0, width, 128)]
        staggered(stages, units, 1)


def same_pair(length):
    row = lax.broadcasted_iota(jnp.int32, (128, 128), 0) // length
    lane = lax.broadcasted_iota(jnp.int32, (128, 128), 1) // length
    return row == lane


SMEM = pl.BlockSpec(memory_space=pltpu.SMEM)
VMEM = pl.BlockSpec(memory_space=pltpu.VMEM)


def params(limit=60):
    return pltpu.CompilerParams(vmem_limit_bytes=limit * 2**20)


def as_column(row):
    size = row.shape[1]
    diagonal = lax.broadcasted_iota(jnp.int32, (size, size), 0) == lax.broadcasted_iota(jnp.int32, (size, size), 1)
    return jnp.sum(jnp.where(diagonal, row, 0.0), axis=1, keepdims=True)


def as_row(col):
    size = col.shape[0]
    diagonal = lax.broadcasted_iota(jnp.int32, (size, size), 0) == lax.broadcasted_iota(jnp.int32, (size, size), 1)
    return jnp.sum(jnp.where(diagonal, col, 0.0), axis=0, keepdims=True)


def prepare_kernel(cut, place_ref, count_ref, scale_ref, plan_ref, rlive_ref, tlive_ref, scal_ref):
    rows, cols = count_ref.shape
    across = rows - 1
    col = place_ref[0]
    row = place_ref[1]

    def limits(r, c):
        n = count_ref[r, c]
        other = count_ref[r ^ across, c]
        low = r < rows // 2
        balanced = jnp.where(low, n, other) <= cut
        return n, jnp.where(balanced, jnp.where(low, other, 0), n), low & balanced

    def mask(r, c):
        first, last, _ = limits(r, c)
        slot = lax.broadcasted_iota(jnp.int32, (1, 128), 1)
        return jnp.where(slot < jnp.where(slot < cut, first, last), 1.0, 0.0)

    for c in range(cols):
        rlive_ref[c : c + 1, :] = mask(row, c)
    for p in range(rows):
        tlive_ref[p : p + 1, :] = mask(row ^ p, col)
    first, last, use = limits(row, col)
    limit = lambda start: first if start < cut else last
    plan_ref[0] = col
    plan_ref[1] = row
    plan_ref[USE] = use.astype(jnp.int32)
    blocks = 128 // NB
    active = [(b * NB < limit(b * NB)).astype(jnp.int32) for b in range(blocks)]
    count = sum(active)
    before = jnp.int32(0)
    for b in range(blocks):
        plan_ref[ORDER_ALL + jnp.where(active[b] > 0, before, count + b - before)] = b
        before = before + active[b]
    for i in range(blocks):
        plan_ref[ORDER + i] = plan_ref[ORDER_ALL + jnp.minimum(i, count - 1)]
    plan_ref[ACTIVE] = count
    for b in range(128 // GROUP):
        plan_ref[IMAGE_BLOCKS + b] = (b * GROUP < limit(b * GROUP)).astype(jnp.int32)
    total = jnp.int32(0)
    for r in range(rows):
        for c in range(cols):
            total = total + count_ref[r, c]
    index = lax.broadcasted_iota(jnp.int32, (8, 128), 0)
    scal_ref[...] = jnp.where(index == 0, jnp.exp(jnp.full((8, 128), scale_ref[0], F32)), 0.5 / jnp.full((8, 128), total, jnp.int32).astype(F32))


def prepare(place, pair_count, log_scale, cut):
    rows, cols = pair_count.shape
    return pl.pallas_call(
        functools.partial(prepare_kernel, cut),
        in_specs=[SMEM] * 3,
        out_specs=[SMEM, VMEM, VMEM, VMEM],
        out_shape=[
            jax.ShapeDtypeStruct((PLAN,), jnp.int32),
            jax.ShapeDtypeStruct((cols, 128), F32),
            jax.ShapeDtypeStruct((rows, 128), F32),
            jax.ShapeDtypeStruct((8, 128), F32),
        ],
        name="prepare",
    )(place, pair_count, log_scale)


def lengths_of(plan_ref, cut, part, lens_ref, got_ref):
    moved = (plan_ref[USE] > 0) & (part * QB >= cut)
    got = got_ref[pl.ds(jnp.maximum(part - cut // QB, 0), 1), :]
    return as_column(jnp.where(moved, got, lens_ref[pl.ds(part, 1), :]))


def block_lengths(plan_ref, cut, block, lens_ref, got_ref):
    parts = [lengths_of(plan_ref, cut, block * (NB // QB) + k, lens_ref, got_ref) for k in range(NB // QB)]
    return jnp.concatenate(parts, axis=0)


def all_lengths(plan_ref, cut, lens_ref, got_ref):
    parts = [lengths_of(plan_ref, cut, b, lens_ref, got_ref) for b in range(lens_ref.shape[0])]
    return jnp.concatenate(parts, axis=0)


def live_pick(lens, rows):
    pairs = lens.shape[0]
    length = rows // pairs
    token = lax.broadcasted_iota(jnp.int32, (pairs, rows), 1)
    own = token // length == lax.broadcasted_iota(jnp.int32, (pairs, rows), 0)
    return jnp.where(own & ((token % length).astype(F32) < lens), 1.0, 0.0)


def text_tokens_of(plan_ref, cut, block, x_ref, recv_ref):
    nb, length, width = x_ref.shape
    moved = (plan_ref[USE] > 0) & (block * nb >= cut)
    x = jnp.where(moved, recv_ref[...].astype(F32), x_ref[...].astype(F32))
    return x.reshape(nb * length, width)


def ordered(width, rows):
    return pl.BlockSpec((rows, width), lambda i, plan: (plan[ORDER + i], 0))


def ordered_pairs(shape, order=ORDER):
    return pl.BlockSpec((NB,) + shape[1:], lambda i, plan: (plan[order + i], 0, 0))


def held(shape):
    zeros = (0,) * len(shape)
    return pl.BlockSpec(shape, lambda i, plan: zeros)


def text_first_kernel(cut, plan_ref, x_ref, recv_ref, lens_ref, got_ref, gain_ref, wqkv_ref, wout_ref, qkv_ref, att_ref, y1_ref):
    step = pl.program_id(0)
    block = plan_ref[ORDER + step]

    @pl.when(step < plan_ref[ACTIVE])
    def _():
        x = text_tokens_of(plan_ref, cut, block, x_ref, recv_ref)
        lens = block_lengths(plan_ref, cut, block, lens_ref, got_ref)
        text_attention(x, lens, x_ref.shape[1], gain_ref, wqkv_ref, wout_ref, qkv_ref, att_ref, y1_ref)


def text_attention(x, lens, length, gain_ref, wqkv_ref, wout_ref, qkv_ref, att_ref, y1_ref):
    rows, width = x.shape
    n1 = (normed(x) * gain_ref[...]).astype(BF16)
    for c in range(3):
        at = slice(c * width, (c + 1) * width)
        qkv_ref[:, at] = mm(n1, wqkv_ref[:, at]).astype(BF16)
    lane = lax.broadcasted_iota(jnp.int32, (128, 128), 1)
    low = (lane[:1] < HEAD).astype(BF16)
    high = 1 - low
    half = lax.broadcasted_iota(jnp.int32, (256, 128), 0) < 128
    ones = jnp.where(half == (lax.broadcasted_iota(jnp.int32, (256, 128), 1) < HEAD), 1.0, 0.0).astype(BF16)
    same = same_pair(length)
    live = jnp.sum(live_pick(lens, rows), axis=0, keepdims=True)
    bias = {g: jnp.where(same & (live[:, g : g + 128] > 0), 0.0, -1e30) for g in range(0, rows, 128)}

    def scores(unit):
        g, h = unit
        q = qkv_ref[g : g + 128, h : h + 128] * BF16(HEAD**-0.5)
        k = qkv_ref[g : g + 128, width + h : width + h + 128]
        return mm_t(q, jnp.concatenate([k * low, k * high], axis=0))

    def expo(unit, s):
        one = bias[unit[0]]
        parts = [s[:, :128] + one, s[:, 128:] + one]
        return jnp.concatenate([jnp.exp(p - jnp.max(p, axis=1, keepdims=True)) for p in parts], axis=1).astype(BF16)

    def weighted(unit, e):
        g, h = unit
        v = qkv_ref[g : g + 128, 2 * width + h : 2 * width + h + 128]
        vbd = jnp.concatenate([v * low, v * high], axis=0)
        o = mm(e, jnp.concatenate([vbd, ones], axis=1))
        att_ref[g : g + 128, h : h + 128] = (o[:, :128] / o[:, 128:]).astype(BF16)

    staggered([scores, expo, weighted], [(g, h) for g in range(0, rows, 128) for h in range(0, width, 128)], 1)
    y1_ref[...] = x + mm(att_ref[...], wout_ref[...])


def text_first(plan, x, received, lens, got, cut, gain_one, wqkv, wout):
    pairs, length, width = x.shape
    rows = NB * length
    tokens = pairs * length
    rest = (received, lens, got, gain_one, wqkv, wout)
    wide = [(3 * width, BF16), (width, BF16), (width, F32)]
    return pl.pallas_call(
        functools.partial(text_first_kernel, cut),
        grid_spec=pltpu.PrefetchScalarGridSpec(
            num_scalar_prefetch=1,
            grid=(pairs // NB,),
            in_specs=[ordered_pairs(x.shape)] + [fixed(w.shape) for w in rest],
            out_specs=[ordered(w, rows) for w, _ in wide],
        ),
        out_shape=[(pltpu.HBM if k == 0 else jax.ShapeDtypeStruct)((tokens, w), kind) for k, (w, kind) in enumerate(wide)],
        compiler_params=params(T1_LIMIT),
        cost_estimate=pl.CostEstimate(flops=2 * tokens * width * 5 * width, bytes_accessed=12 * 2**20, transcendentals=0),
        name="text_attention",
    )(plan, x, *rest)


def text_second_kernel(
    cut, plan_ref, y1_ref, lens_ref, got_ref, gain_two_ref, wup_ref, wdown_ref, wproj_ref,
    slope_ref, hsum_ref, pooled_ref, emb_ref, low_ref, ysum,
):
    step = pl.program_id(0)
    block = plan_ref[ORDER + step]

    @pl.when(step == 0)
    def _():
        hsum_ref[...] = jnp.zeros_like(hsum_ref)
        ysum[...] = jnp.zeros_like(ysum)

    @pl.when(step < plan_ref[ACTIVE])
    def _():
        rows = y1_ref.shape[0]
        y1 = y1_ref[...]
        pick = live_pick(block_lengths(plan_ref, cut, block, lens_ref, got_ref), rows).astype(BF16)
        pair = pl.ds(pl.multiple_of(block * NB, NB), NB)
        y1_hi = y1.astype(BF16)
        ysum[pair, :] = mm(pick, y1_hi) + mm(pick, (y1 - y1_hi.astype(F32)).astype(BF16))
        n2 = (normed(y1) * gain_two_ref[...]).astype(BF16)

        live = mm_tn(pick, jnp.ones((NB, 128), BF16))
        live = jnp.concatenate([live, live], axis=1)

        def gelu_parts(u, c):
            square = u * u
            t = 1.0 + jnp.tanh(u * (GELU_A + GELU_B * square))
            half = 0.5 * u
            hsum_ref[pair, c : c + 256] = mm(pick, (half * t).astype(BF16))
            d = t * (0.5 + (2.0 - t) * (half * (GELU_A + (3.0 * GELU_B) * square)))
            slope_ref[:, c : c + 256] = (d * live).astype(BF16)

        in_chunks(n2, wup_ref, gelu_parts)

    @pl.when(step == pl.num_programs(0) - 1)
    def _():
        inv_len = 1.0 / all_lengths(plan_ref, cut, lens_ref, got_ref)
        pooled = (ysum[...] * inv_len + mm_split(hsum_ref[...] * inv_len, wdown_ref[...])).astype(BF16)
        pooled_ref[...] = pooled
        e = mm(pooled, wproj_ref[...])
        emb_ref[...] = e
        low_ref[...] = (e * unit_scale(e)).astype(BF16)


def in_chunks(left, right_ref, use):
    before = None
    for c in range(0, right_ref.shape[1], 256):
        u = mm(left, right_ref[:, c : c + 256])
        if before is not None:
            use(*before)
        before = (u, c)
    use(*before)


def text_second(plan, y1, lens, got, cut, gain_two, wup, wdown, wproj):
    tokens, width = y1.shape
    pairs = lens.size
    rows = NB * tokens // pairs
    ff = wup.shape[1]
    rest = (lens, got, gain_two, wup, wdown, wproj)
    flat = [((pairs, ff), F32), ((pairs, width), BF16), ((pairs, width), F32), ((pairs, width), BF16)]
    return pl.pallas_call(
        functools.partial(text_second_kernel, cut),
        grid_spec=pltpu.PrefetchScalarGridSpec(
            num_scalar_prefetch=1,
            grid=(pairs // NB,),
            in_specs=[ordered(width, rows)] + [fixed(w.shape) for w in rest],
            out_specs=[ordered(ff, rows)] + [held(shape) for shape, _ in flat],
            scratch_shapes=[pltpu.VMEM((pairs, width), F32)],
        ),
        out_shape=[jax.ShapeDtypeStruct((tokens, ff), BF16)] + [jax.ShapeDtypeStruct(shape, kind) for shape, kind in flat],
        compiler_params=params(T2_LIMIT),
        cost_estimate=pl.CostEstimate(flops=2 * tokens * width * ff, bytes_accessed=12 * 2**20, transcendentals=tokens * ff),
        name="text_pool",
    )(plan, y1, *rest)


def image_groups(image_refs):
    for j, ref in enumerate(image_refs):
        yield j, ref.shape[0] // 128, len(image_refs), ref[...]


def sums_kernel(rows, ids_ref, scal_ref, tlive_ref, rlive_ref, *refs):
    text_refs = refs[:rows]
    image_refs = refs[rows:-2]
    rowsum_ref, colsum_ref = refs[-2:]
    me = ids_ref[0]
    scale = scal_ref[:1, :1]
    text = jnp.concatenate([ref[...] for ref in text_refs], axis=0)
    tlive = jnp.concatenate([as_column(tlive_ref[p : p + 1, :]) for p in range(rows)], axis=0)
    col = jnp.zeros((rows * 128, 1), F32)
    for j, high, low, images in image_groups(image_refs):
        e = jnp.exp(scale * mm_t(text, images)) * tlive
        total = jnp.sum(e, axis=0, keepdims=True)
        kept = jnp.zeros((rows * 128, 128), F32)
        for i in range(high):
            at = pl.ds(me ^ (low * i + j), 1)
            rowsum_ref[at, :] = total[:, i * 128 : i * 128 + 128]
            kept = kept + e[:, i * 128 : i * 128 + 128] * rlive_ref[at, :]
        col = col + jnp.sum(kept, axis=1, keepdims=True)
    for p in range(rows):
        colsum_ref[p : p + 1, :] = as_row(col[p * 128 : p * 128 + 128])


def sim_sums(ids, scal, texts, tlive, rlive, images):
    cols = rlive.shape[0]
    rows = len(texts)
    return pl.pallas_call(
        functools.partial(sums_kernel, rows),
        in_specs=[SMEM] + [VMEM] * (3 + rows + len(images)),
        out_specs=[VMEM, VMEM],
        out_shape=[jax.ShapeDtypeStruct((cols, 128), F32), jax.ShapeDtypeStruct((rows, 128), F32)],
        compiler_params=params(SIM_LIMIT),
        cost_estimate=pl.CostEstimate(
            flops=2 * rows * 128 * cols * 128 * 384, bytes_accessed=cols * 128 * 768, transcendentals=rows * cols * 128 * 128
        ),
        name="similarity_sums",
    )(ids, scal, tlive, rlive, *texts, *images)


def grad_kernel(rows, ids_ref, scal_ref, tlive_ref, rlive_ref, rowsum_ref, colsum_ref, *refs):
    text_refs = refs[:rows]
    image_refs = refs[rows : -rows - 1]
    dun_refs = refs[-rows - 1 : -1]
    stat_ref = refs[-1]
    me = ids_ref[0]
    scale = scal_ref[:1, :1]
    inv = scal_ref[1:2, :1]
    text = jnp.concatenate([ref[...] for ref in text_refs], axis=0)
    tlive = jnp.concatenate([as_column(tlive_ref[p : p + 1, :]) for p in range(rows)], axis=0)
    col = jnp.concatenate([as_column(colsum_ref[p : p + 1, :]) for p in range(rows)], axis=0)
    col = jnp.where(tlive > 0, col, 1.0)
    col_inv = inv / col
    total = jnp.zeros(text.shape, F32)
    moved = jnp.zeros((1, 128), F32)
    for j, high, low, images in image_groups(image_refs):
        s = scale * mm_t(text, images)
        e = jnp.exp(s) * tlive
        at = [pl.ds(me ^ (low * i + j), 1) for i in range(high)]
        rlive = jnp.concatenate([rlive_ref[one, :] for one in at], axis=1)
        row_inv = jnp.concatenate([inv / rowsum_ref[one, :] for one in at], axis=1)
        ds = (e * rlive) * (row_inv + col_inv)
        by_lane = jnp.sum(ds * s, axis=0, keepdims=True)
        for i in range(high):
            moved = moved + by_lane[:, i * 128 : i * 128 + 128]
        total = total + mm((scale * ds).astype(BF16), images)
        if j == 0:
            mine = images[:128].astype(F32)
    own_live = tlive[:128]
    cosine = jnp.sum(mine * text[:128].astype(F32), axis=1, keepdims=True)
    live_cosine = jnp.sum(cosine * own_live, axis=0, keepdims=True)
    at = pl.ds(me, 1)
    logs = jnp.sum(jnp.log(rowsum_ref[at, :]) * rlive_ref[at, :], axis=1, keepdims=True)
    logs = logs + jnp.sum(jnp.log(col[:128]) * own_live, axis=0, keepdims=True)
    loss = inv * (logs - 2.0 * scale * live_cosine)
    scale_part = jnp.sum(moved, axis=1, keepdims=True) - 2.0 * inv * scale * live_cosine
    dun_refs[0][...] = total[:128] + (scale * (-2.0 * inv * own_live)).astype(BF16).astype(F32) * mine
    for p in range(1, rows):
        dun_refs[p][...] = total[p * 128 : p * 128 + 128].astype(BF16)
    lane = lax.broadcasted_iota(jnp.int32, (8, 128), 1)
    stat_ref[...] = jnp.where(lane == 0, loss, jnp.where(lane == 1, scale_part, 0.0))


def sim_grads(ids, scal, texts, tlive, rlive, rowsum, colsum, images):
    cols = rlive.shape[0]
    rows = len(texts)
    return pl.pallas_call(
        functools.partial(grad_kernel, rows),
        in_specs=[SMEM] + [VMEM] * (5 + rows + len(images)),
        out_specs=[VMEM] * (rows + 1),
        out_shape=[jax.ShapeDtypeStruct(text.shape, BF16 if k else F32) for k, text in enumerate(texts)] + [jax.ShapeDtypeStruct((8, 128), F32)],
        compiler_params=params(SIM_LIMIT),
        cost_estimate=pl.CostEstimate(
            flops=4 * rows * 128 * cols * 128 * 384, bytes_accessed=cols * 128 * 768, transcendentals=rows * cols * 128 * 128
        ),
        name="similarity_grads",
    )(ids, scal, tlive, rlive, rowsum, colsum, *texts, *images)


def write_halves(core, blocks, keep_ref, send_ref):
    half = len(blocks) // 2
    size = blocks[0].shape[0]

    def put(first, second):
        for at, (kept, sent) in enumerate(zip(first, second)):
            keep_ref[at * size : (at + 1) * size, :] = kept.astype(BF16)
            send_ref[at * size : (at + 1) * size, :] = sent.astype(BF16)

    @pl.when(core == 0)
    def _():
        put(blocks[:half], blocks[half:])

    @pl.when(core != 0)
    def _():
        put(blocks[half:], blocks[:half])


def back_kernel(
    cut, others, plan_ref, x_ref, qkv_ref, att_ref, y1_ref, slope_ref, recv_ref, lens_ref, got_ref,
    dun_ref, emb_ref, pooled_ref, hsum_ref, gain_ref, wqkv_ref, wout_ref, gain_two_ref, wup_ref, wdown_ref, wproj_ref, *refs,
):
    other_refs = refs[:others]
    stat_ref = refs[others]
    grad_ref, keep_a, send_a, keep_b, send_b, keep_c, send_c = refs[others + 1 : others + 8]
    dyp, dhp, dproj, ddown, dmix, dheads, acc_up, acc_out, acc_qkv, bias_ref = refs[others + 8 :]
    step = pl.program_id(0)
    block = plan_ref[ORDER + step]
    active = step < plan_ref[ACTIVE]
    width = dun_ref.shape[1]
    ff = hsum_ref.shape[1]

    @pl.when(step == 0)
    def _():
        acc_up[...] = jnp.zeros_like(acc_up)
        acc_out[...] = jnp.zeros_like(acc_out)
        acc_qkv[...] = jnp.zeros_like(acc_qkv)
        g = dun_ref[...]
        for other in other_refs:
            g = g + other[...].astype(F32)
        e = emb_ref[...]
        inv = unit_scale(e)
        t = e * inv
        demb = (inv * (g - t * jnp.sum(g * t, axis=-1, keepdims=True))).astype(BF16)
        dproj[...] = mm_tn(pooled_ref[...], demb)
        back = mm_t(demb, wproj_ref[...]) * (1.0 / all_lengths(plan_ref, cut, lens_ref, got_ref))
        dyp[...] = back
        db = back.astype(BF16)
        dhp[...] = mm_t(db, wdown_ref[...])
        h = hsum_ref[...]
        hi = h.astype(BF16)
        lo = (h - hi.astype(F32)).astype(BF16)
        ddown[...] = mm_tn(hi, db) + mm_tn(lo, db)

    @pl.when(active)
    def _():
        x = text_tokens_of(plan_ref, cut, block, x_ref, recv_ref)
        lens = block_lengths(plan_ref, cut, block, lens_ref, got_ref)
        grad = back_block(
            block, x, lens, x_ref.shape[1], qkv_ref, att_ref, y1_ref, slope_ref, gain_ref, wqkv_ref, wout_ref,
            gain_two_ref, wup_ref, dyp, dhp, dmix, dheads, acc_up, acc_out, acc_qkv, bias_ref,
        )
        grad_ref[...] = grad.astype(BF16).reshape(grad_ref.shape)

    @pl.when(jnp.logical_not(active))
    def _():
        grad_ref[...] = jnp.zeros_like(grad_ref)

    @pl.when(step == pl.num_programs(0) - 1)
    def _():
        core = plan_ref[0] & 1
        index = lax.broadcasted_iota(jnp.int32, (128, width), 0)
        stat = jnp.concatenate([stat_ref[:1, :]] * (width // 128), axis=1)
        by_qkv = jnp.sum(acc_qkv[...] * wqkv_ref[...].astype(F32), axis=1, keepdims=True)
        by_up = jnp.sum(acc_up[...] * wup_ref[...].astype(F32), axis=1, keepdims=True)
        first = as_row(by_qkv) / gain_ref[...]
        second = as_row(by_up) / gain_two_ref[...]
        small = jnp.where(index == 0, first, jnp.where(index == 1, second, jnp.where(index == 2, stat, 0.0)))
        blocks = [ddown[at : at + 128, :] for at in range(0, ff, 128)]
        blocks += [dproj[at : at + 128, :] for at in range(0, width, 128)]
        write_halves(core, blocks + [small], keep_a, send_a)
        write_halves(core, [acc_up[:, c : c + width] for c in range(0, ff, width)], keep_b, send_b)
        blocks = [acc_out[...]] + [acc_qkv[:, c * width : (c + 1) * width] for c in range(3)]
        write_halves(core, blocks, keep_c, send_c)


def back_block(
    block, x, lens, length, qkv_ref, att_ref, y1_ref, slope_ref, gain_ref, wqkv_ref, wout_ref,
    gain_two_ref, wup_ref, dyp, dhp, dmix, dheads, acc_up, acc_out, acc_qkv, bias_ref,
):
    rows, width = x.shape
    ff = wup_ref.shape[1]
    pair = pl.ds(pl.multiple_of(block * NB, NB), NB)

    def spread(values):
        return jnp.broadcast_to(values[:, None, :], (NB, length, values.shape[1])).reshape(rows, values.shape[1])

    n2, inv = stats(y1_ref[...])
    n2_low = (n2 * gain_two_ref[...]).astype(BF16)
    dn2 = jnp.zeros((rows, width), F32)
    for c in range(0, ff, width):
        at = slice(c, c + width)
        du = (spread(dhp[pair, at]) * slope_ref[:, at].astype(F32)).astype(BF16)
        acc_up[:, at] += mm_tn(n2_low, du)
        dn2 = dn2 + mm_t(du, wup_ref[:, at])
    live = mm_tn(live_pick(lens, rows).astype(BF16), jnp.ones((NB, 128), BF16))
    dy1 = spread(dyp[pair, :]) * jnp.concatenate([live] * (width // 128), axis=1)
    dy1 = dy1 + norm_back(dn2 * gain_two_ref[...], n2, inv)
    da = dy1.astype(BF16)
    acc_out[...] += mm_tn(att_ref[...], da)
    dheads[...] = mm_t(da, wout_ref[...]).astype(BF16)
    attention_grads(length, live, qkv_ref, dmix, dheads, bias_ref)
    n1, inv = stats(x)
    n1_low = (n1 * gain_ref[...]).astype(BF16)
    dn1 = jnp.zeros((rows, width), F32)
    for c in range(3):
        at = slice(c * width, (c + 1) * width)
        acc_qkv[:, at] += mm_tn(n1_low, dmix[:, at])
        dn1 = dn1 + mm_t(dmix[:, at], wqkv_ref[:, at])
    return dy1 + norm_back(dn1 * gain_ref[...], n1, inv)


def attention_grads(length, live, qkv_ref, dmix, dheads, bias_ref):
    rows, width = dheads.shape
    lane = lax.broadcasted_iota(jnp.int32, (128, 128), 1)
    first = lane < HEAD
    low = first[:1].astype(BF16)
    high = 1 - low
    eye = (lane == lax.broadcasted_iota(jnp.int32, (128, 128), 0)).astype(BF16)
    same = same_pair(length)
    for g in range(rows // 128):
        bias_ref[g] = jnp.where(same & (live[g * 128 : g * 128 + 128, :] > 0), 0.0, -1e30)

    def pieces(unit, part):
        g, h = unit
        return qkv_ref[pl.ds(g * 128, 128), part * width + h : part * width + h + 128]

    def scores(unit):
        g, h = unit
        k = pieces(unit, 1)
        v = pieces(unit, 2)
        do = dheads[pl.ds(g * 128, 128), h : h + 128]
        kbd = jnp.concatenate([k * low, k * high], axis=0)
        vbd = jnp.concatenate([v * low, v * high], axis=0)
        s = mm_t(kbd, pieces(unit, 0) * BF16(HEAD**-0.5))
        return s, mm_t(vbd, do)

    def soft(unit, made):
        g, _ = unit
        s, dp = made
        s = s.reshape(2, 128, 128) + bias_ref[g][None]
        e = jnp.exp(s - jnp.max(s, axis=1, keepdims=True))
        p = e * (1.0 / jnp.sum(e, axis=1, keepdims=True))
        dp = dp.reshape(2, 128, 128)
        ds = p * (dp - jnp.sum(p * dp, axis=1, keepdims=True))
        return p.reshape(256, 128).astype(BF16), ds.reshape(256, 128).astype(BF16)

    def products(unit, made):
        g, h = unit
        p, ds = made
        at = pl.ds(g * 128, 128)
        do = dheads[at, h : h + 128]
        dv = mm(p, do)
        dmix[at, 2 * width + h : 2 * width + h + 128] = jnp.where(first, dv[:128], dv[128:]).astype(BF16)
        dk = mm(ds, pieces(unit, 0) * BF16(HEAD**-0.5))
        dmix[at, width + h : width + h + 128] = jnp.where(first, dk[:128], dk[128:]).astype(BF16)
        return mm_t(eye, ds).astype(BF16)

    def query(unit, ds):
        g, h = unit
        k = pieces(unit, 1)
        kbd = jnp.concatenate([k * low, k * high], axis=0)
        dmix[pl.ds(g * 128, 128), h : h + 128] = (mm(ds, kbd) * HEAD**-0.5).astype(BF16)

    group_loop([scores, soft, products, query], rows, width)


def text_backward(
    plan, x, qkv, att, y1, slopes, received, lens, got, cut, dun, emb, pooled, hsum,
    gain_one, wqkv, wout, gain_two, wup, wdown, wproj, others, stat,
):
    pairs, length, width = x.shape
    rows = NB * length
    tokens = pairs * length
    ff = wup.shape[1]
    rest = (received, lens, got, dun, emb, pooled, hsum, gain_one, wqkv, wout, gain_two, wup, wdown, wproj, *others, stat)
    halves = [(ff + width + 128) // 2, ff // 2, 2 * width]
    shapes = [(half, width) for half in halves for _ in range(2)]
    return pl.pallas_call(
        functools.partial(back_kernel, cut, len(others)),
        grid_spec=pltpu.PrefetchScalarGridSpec(
            num_scalar_prefetch=1,
            grid=(pairs // NB,),
            in_specs=[ordered_pairs(x.shape), ordered(3 * width, rows), ordered(width, rows), ordered(width, rows), ordered(ff, rows)]
            + [fixed(w.shape) for w in rest],
            out_specs=[ordered_pairs(x.shape, ORDER_ALL)] + [held(shape) for shape in shapes],
            scratch_shapes=[
                pltpu.VMEM((pairs, width), F32),
                pltpu.VMEM((pairs, ff), F32),
                pltpu.VMEM((width, width), F32),
                pltpu.VMEM((ff, width), F32),
                pltpu.VMEM((rows, 3 * width), BF16),
                pltpu.VMEM((rows, width), BF16),
                pltpu.VMEM((width, ff), F32),
                pltpu.VMEM((width, width), F32),
                pltpu.VMEM((width, 3 * width), F32),
                pltpu.VMEM((rows // 128, 128, 128), F32),
            ],
        ),
        out_shape=[pltpu.HBM(x.shape, BF16)] + [pltpu.HBM(shape, BF16) for shape in shapes],
        compiler_params=params(BACK_LIMIT),
        cost_estimate=pl.CostEstimate(
            flops=2 * tokens * width * (10 * width + 2 * ff), bytes_accessed=24 * 2**20, transcendentals=0
        ),
        name="text_backward",
    )(plan, x, qkv, att, y1, slopes, *rest)


def flip(values, axis, bits):
    size = lax.axis_size(axis)
    return lax.ppermute(values, axis, [(k, k ^ bits) for k in range(size)])


def reduce_round(kept, axis, unit, ways, split):
    if not split:
        low = kept.astype(BF16)
        others = [flip(low, axis, p * unit).astype(F32) for p in range(1, ways)]
        return tree_sum([low.astype(F32)] + others)
    me = (lax.axis_index(axis) // unit) % ways
    pieces = kept.reshape(ways, kept.shape[0] // ways, kept.shape[1])
    total = lax.dynamic_index_in_dim(pieces, me, 0, keepdims=False)
    for p in range(1, ways):
        piece = lax.dynamic_index_in_dim(pieces, me ^ p, 0, keepdims=False)
        total = total + flip(piece.astype(BF16), axis, p * unit).astype(F32)
    return total


def gather_round(piece, axis, unit, ways, split):
    if not split:
        return piece
    return jnp.concatenate([piece] + [flip(piece, axis, p * unit) for p in range(1, ways)], axis=0)


def exchange(keep, send, rounds, back=None):
    kept = keep.astype(F32) + flip(send, "col", 1).astype(F32)
    for one in rounds:
        kept = reduce_round(kept, *one)
    piece = kept.astype(BF16)
    if back is not None:
        piece = tie(piece, back)
    for one in reversed(rounds):
        piece = gather_round(piece, *one)
    return piece, flip(piece, "col", 1)


def tie(first, *others):
    return lax.optimization_barrier((first, *others))[0]


def tree_sum(parts):
    while len(parts) > 1:
        parts = [parts[k] + parts[k + 1] for k in range(0, len(parts), 2)]
    return parts[0]


def sum_over(values, axis, unit, ways):
    return tree_sum([values] + [flip(values, axis, p * unit) for p in range(1, ways)])


def place_kernel(targets, rounds, last, ids_ref, own_ref, other_ref, *outs):
    col = ids_ref[0]
    row = ids_ref[1]
    half, width = own_ref.shape
    steps = []
    size = half
    for axis, unit, ways, split in rounds:
        if split:
            size //= ways
            steps.append((axis, unit, ways, size))
    count = half // size
    places = outs[: len(targets) - 1] + outs[-1:] if last else outs
    for other, source in enumerate((own_ref, other_ref)):

        @pl.loop(0, count)
        def _(k):
            start = ((col & 1) ^ other) * half
            left = k
            weight = count
            for axis, unit, ways, step in steps:
                weight //= ways
                digit = left // weight
                left = left - digit * weight
                index = (col if axis == "col" else row) // unit % ways
                start = start + (index ^ digit) * step
            value = source[pl.ds(pl.multiple_of(k * size, 16), size), :].astype(F32)
            for first, past, by_row, ref in [target + (ref,) for target, ref in zip(targets, places)]:

                @pl.when((start >= first) & (start < past))
                def _():
                    inside = start - first
                    if by_row:
                        ref[pl.ds(pl.multiple_of(inside, 8), size), :] = value
                    else:
                        lane = pl.multiple_of((inside // width) * width, 128)
                        ref[pl.ds(pl.multiple_of(inside % width, 8), size), pl.ds(lane, width)] = value

    if last:
        first_gain, second_gain, loss, moved, small = outs[-5:]
        first_gain[...] = small[0, :]
        second_gain[...] = small[1, :]
        lane = lax.broadcasted_iota(jnp.int32, (1, 128), 1)
        stat = small[2:3, :128]
        loss[0] = jnp.sum(jnp.where(lane == 0, stat, 0.0))
        moved[0] = jnp.sum(jnp.where(lane == 1, stat, 0.0))


def place(ids, gathered, targets, rounds, shapes, last=False):
    width = gathered[0].shape[1]
    specs = [VMEM] * len(shapes)
    made = [jax.ShapeDtypeStruct(shape, F32) for shape in shapes]
    scratch = []
    if last:
        specs = specs + [VMEM, VMEM, SMEM, SMEM]
        made = made + [jax.ShapeDtypeStruct((size,), F32) for size in (width, width, 1, 1)]
        scratch = [pltpu.VMEM((128, width), F32)]
    return pl.pallas_call(
        functools.partial(place_kernel, targets, rounds, last),
        in_specs=[SMEM, VMEM, VMEM],
        out_specs=specs,
        out_shape=made,
        scratch_shapes=scratch,
        compiler_params=params(SIM_LIMIT),
        name="place_gradients",
    )(ids, *gathered)


def body(
    image_tokens, text_tokens, lengths, pair_count, img_qkv, img_out, img_up, img_down, img_proj,
    gain_one, txt_qkv, txt_out, gain_two, txt_up, txt_down, txt_proj, log_scale,
):
    pairs, _, width = image_tokens.shape
    ff = txt_up.shape[1]
    row_index = lax.axis_index("row")
    col_index = lax.axis_index("col")
    row_count = lax.axis_size("row")
    col_count = lax.axis_size("col")
    high = col_count // 4
    cut = pairs - NB
    across = row_count - 1

    by_token = jnp.transpose(image_tokens, (1, 0, 2))
    got_images = flip(by_token[:, cut:], "row", across)
    got_texts = flip(text_tokens[cut:], "row", across)
    lens = lengths.astype(F32).reshape(pairs // QB, QB)
    got_lens = flip(lens[cut // QB :], "row", across)
    plan, rlive, tlive, scal = prepare(jnp.stack([col_index, row_index]).astype(jnp.int32), pair_count, log_scale, cut)
    gain_one = gain_one.reshape(1, width)
    gain_two = gain_two.reshape(1, width)

    weights = (img_qkv, img_out, img_up, img_down, img_proj)
    first_unit = image_tower(plan, by_token, None, 0, cut, cut, IMAGE_NB, 1.0, *weights)
    last_unit = lax.cond(
        plan[IMAGE_BLOCKS + cut // GROUP] > 0,
        lambda: image_tower(plan, by_token, got_images, cut, NB, cut, GROUP, 0.01, *weights),
        lambda: jnp.zeros((NB, width), BF16),
    )
    unit = jnp.concatenate([first_unit, last_unit], axis=0)
    parts = [unit] + [flip(unit, "col", 4 * p) for p in range(1, high)]
    qkv, att, y1 = text_first(plan, text_tokens, got_texts, lens, got_lens, cut, gain_one, txt_qkv, txt_out)
    parts = lax.optimization_barrier((*parts, y1))
    y1 = parts[-1]
    near = jnp.concatenate(parts[:-1], axis=0)
    beside = flip(near, "col", 2)
    core_near = flip(near, "col", 1)
    slopes, hsum, pooled, emb, text_low = text_second(
        plan, y1, lens, got_lens, cut, gain_two, txt_up, txt_down, txt_proj
    )
    images = [near, core_near, beside, flip(tie(beside, text_low), "col", 1)]
    texts = [text_low] + [flip(text_low, "row", p) for p in range(1, row_count)]
    rowsum, colsum = sim_sums(plan, scal, texts, tlive, rlive, images)
    total_col = colsum
    for p in range(1, row_count):
        other = flip(colsum, "row", p)
        total_col = total_col + jnp.concatenate([other[k ^ p : (k ^ p) + 1] for k in range(row_count)], axis=0)
    for bit in range(2, (high * 4).bit_length() - 1):
        rowsum = rowsum + flip(rowsum, "col", 1 << bit)
    rowsum = sum_over(rowsum, "col", 1, 4)
    *duns, stat = sim_grads(plan, scal, texts, tlive, rlive, rowsum, total_col, images)
    others = [flip(duns[p], "row", p) for p in range(1, row_count)]
    split_row = width * 2 % (row_count * 2 * 2 * 16) == 0
    along_row = ("row", 1, row_count, split_row)
    along_y = ("col", 2, 2, True)
    along_z = ("col", 4, 2, high % 2 == 0)
    along_far = ("col", 8, high // 2, False)
    order_a = [along_row, along_y, along_z, along_far]
    order_b = [along_y, along_z, along_row, along_far]
    order_c = [along_z, along_row, along_y, along_far]
    qkv = pltpu.with_memory_space_constraint(qkv, pltpu.HBM)
    text_grad, keep_a, send_a, keep_b, send_b, keep_c, send_c = text_backward(
        plan, text_tokens, qkv, att, y1, slopes, got_texts, lens, got_lens, cut, duns[0], emb, pooled, hsum,
        gain_one, txt_qkv, txt_out, gain_two, txt_up, txt_down, txt_proj, others, stat,
    )
    back = flip(text_grad[cut:], "row", across)
    low_half = row_index < row_count // 2
    counts = pair_count[:, col_index]
    balanced = jnp.where(low_half, counts[row_index], counts[row_index ^ across]) <= cut
    last = jnp.where(balanced, jnp.where(low_half, jnp.zeros_like(back), back), text_grad[cut:])
    text_grad = lax.dynamic_update_slice_in_dim(text_grad, last, cut, 0)
    orders = [order_a, order_b, order_c]
    targets = [
        [(0, ff, True), (ff, ff + width, True), (ff + width, ff + width + 128, True)],
        [(0, ff, False)],
        [(0, width, True), (width, 4 * width, False)],
    ]
    shapes = [[(ff, width), (width, width)], [(width, ff)], [(width, width), (width, 3 * width)]]
    placed = []
    for keep, send, rounds, places, sizes in zip((keep_a, keep_b, keep_c), (send_a, send_b, send_c), orders, targets, shapes):
        gathered = exchange(keep, send, rounds, text_grad if not placed else None)
        placed += place(plan, gathered, places, rounds, sizes, not placed)
    sum_down, sum_proj, sum_one, sum_two, loss, sum_scale, sum_up, sum_out, sum_qkv = placed
    return (
        loss, text_grad, sum_one, sum_qkv, sum_out, sum_two, sum_up, sum_down, sum_proj, sum_scale,
    )


def solution(mesh):
    return jax.shard_map(
        body,
        mesh=mesh,
        in_specs=(
            P(("row", "col"), None, None),
            P(("row", "col"), None, None),
            P(("row", "col")),
            P(),
            P(),
            P(),
            P(),
            P(),
            P(),
            P(),
            P(),
            P(),
            P(),
            P(),
            P(),
            P(),
            P(),
        ),
        out_specs=(P(), P(("row", "col"), None, None), P(), P(), P(), P(), P(), P(), P(), P()),
        check_vma=False,
    )
```

time: 739 us -> 215 us (0.29); the launches traced: 727 us -> 215 us
  local copies, waits for them, and re-layouts: 216 us -> 5.42 us
  matrix products: 189 us -> 0 us
  blocking collectives: 123 us -> 0 us
  Pallas kernels: 0 us -> 84.6 us
  starting transfers between devices: 0.12 us -> 69.7 us
  waiting for transfers between devices: 113 us -> 46.6 us
  other arithmetic: 69.3 us -> 4.43 us
  between operations: 18.3 us -> 3.94 us
    dot_general x29 -> x0, matrix products: 189 us -> none  [the longest x9 67.5 us: project(): jnp.einsum('...d,de->...e', left, right, preferred_element_type=jnp.float32)]
    psum x1 -> x0, waiting for transfers between devices: 110 us -> none  [body(): lax.psum((grad_qkv, grad_out, grad_gain_one, grad_gain_two, grad_up, grad...]
    unnamed x124 -> x40, local copies, waits for them, and re-layouts: 91.2 us -> 0.19 us
    pallas_call x0 -> x11, Pallas kernels: none -> 84.6 us  [the longest x2 34.9 us: image_tower(): pl.pallas_call(kernel, grid_spec=pltpu.PrefetchScalarGridSpec(num_scalar_...]
    psum x3 -> x0, blocking collectives: 81.1 us -> none  [the longest x1 42.1 us: body(): lax.psum((grad_qkv, grad_out, grad_gain_one, grad_gain_two, grad_up, grad...]
    convert_element_type x8 -> x9, local copies, waits for them, and re-layouts: 71.5 us -> 0.29 us  [reduce_round(): total = total + flip(piece.astype(BF16), axis, p * unit).astype(F32)]
    ppermute x0 -> x45, starting transfers between devices: none -> 69.7 us  [flip(): return lax.ppermute(values, axis, [(k, k ^ bits) for k in range(size)])]
    ppermute x0 -> x45, waiting for transfers between devices: none -> 46.6 us  [flip(): return lax.ppermute(values, axis, [(k, k ^ bits) for k in range(size)])]
  transfers between devices with their start and end apart: 3 -> 45, of which waited for: 2 -> 21; matrix products, arithmetic and copies ran while one was open for 16% -> 3% of each run, Pallas kernels for 0% -> 26%
where the time goes in v1:
time: 215 us
  Pallas kernels  84.6 us (39%)
  starting transfers between devices  69.7 us (32%)
  waiting for transfers between devices  46.6 us (22%)
  local copies, waits for them, and re-layouts  5.42 us (3%)
  other arithmetic  4.43 us (2%)
  between operations  3.94 us (2%)
    ppermute x45, starting transfers between devices, flip(): return lax.ppermute(values, axis, [(k, k ^ bits) for k in range(size)])  69.7 us
    ppermute x45, waiting for transfers between devices, flip(): return lax.ppermute(values, axis, [(k, k ^ bits) for k in range(size)])  46.6 us
    pallas_call x2, Pallas kernels, image_tower(): pl.pallas_call(kernel, grid_spec=pltpu.PrefetchScalarGridSpec(num_scalar_...  34.9 us
    pallas_call x1, Pallas kernels, text_backward(): pl.pallas_call(functools.partial(back_kernel, cut, len(others)), grid_spe...  22.7 us
    pallas_call x3, Pallas kernels, place(): pl.pallas_call(functools.partial(place_kernel, targets, rounds, last), in...  8.7 us
    pallas_call x1, Pallas kernels, text_second(): pl.pallas_call(functools.partial(text_second_kernel, cut), grid_spec=pltp...  7.05 us
    pallas_call x1, Pallas kernels, text_first(): pl.pallas_call(functools.partial(text_first_kernel, cut), grid_spec=pltpu...  6.01 us
  transfers between devices with their start and end apart: 45, of which 21 were waited for; matrix products, arithmetic and copies ran while one was open for 3% of the time, Pallas kernels for 26%

profile of v1, /device:TPU:1, one launch (start us, length us, event | category | flops | bytes accessed | tf_op | source)
XLA Modules:
  0.0 214.7 jit_solution(9925063266371112642)
XLA Ops:
  2.2 2.1 collective-permute-start.2
  9.4 18.3 %image_block.3 = bf16[96,384]{1,0:T(8,128)(2,1)} custom-call(s32[28]{0:T(128)S(1)} %get-tuple-element.76.plan_ref.ids_ref, bf16[50,128,384]{2,1,0:T(8,128)(2,1)} %bitcast.58, bf16[384,1152]{1,0:T(8,128)(2,1)} %refs_0_.1, bf16[384,384]{1,0:T(8,128)(2,1)S(1)} %copy-done.12, bf16[384,1536]{1,0:T(8,128)(2,1)} %refs_2_.1, bf16[1536,384]{1,0:T(8,128)(2,1)} %refs_3_.1, ...), custom_call_target="tpu_custom_call" | custom-call | flops 11324620800 | bytes 7880704 | tf_op jit(solution)/shard_map/image_block/pallas_call | solution.py:228
  29.1 2.1 collective-permute-done.2
  31.2 16.6 %conditional.1 = (bf16[32,384]{1,0:T(8,128)(2,1)S(1)}) conditional(s32[]{:T(128)} %bitcast.3, () %tuple.17, (s32[28]{0:T(128)S(1)}, bf16[50,128,384]{2,1,0:T(8,128)(2,1)}, bf16[50,32,384]{2,1,0:T(8,128)(2,1)}, bf16[384,1152]{1,0:T(8,128)(2,1)}, bf16[384,384]{1,0:T(8,128)(2,1)S(1)}, /*index=5*/bf16[384,1536]{1,0:T(8,128)(2,1)}, ...), branch_computations={%region_0.0_spmd, %region_1.0_spmd} | conditional | flops 37748736 | bytes 54239 | solution.py:1030
  31.2 16.6 %image_block.2 = bf16[32,384]{1,0:T(8,128)(2,1)S(1)} custom-call(s32[28]{0:T(128)S(1)} %get-tuple-element.7.plan_ref, bf16[50,128,384]{2,1,0:T(8,128)(2,1)} %get-tuple-element.20.x_ref, bf16[50,32,384]{2,1,0:T(8,128)(2,1)} %get-tuple-element.21.recv_ref, bf16[384,1152]{1,0:T(8,128)(2,1)} %get-tuple-element.22.wqkv_ref, ...), custom_call_target="tpu_custom_call" | custom-call | flops 37748736 | bytes 54231 | tf_op jit(solution)/shard_map/cond/branch_1_fun/image_block/pallas_call | solution.py:228
  50.1 2.3 %collective-permute-start.4 = (bf16[128,384]{1,0:T(8,128)(2,1)S(1)}, bf16[128,384]{1,0:T(8,128)(2,1)S(1)}, u32[]{:S(2)}, u32[]{:S(2)}) collective-permute-start(bf16[128,384]{1,0:T(8,128)(2,1)S(1)} %pad_maximum_fusion.8), channel_id=1, source_target_pairs={{0,8},{1,9},{2,10},{3,11},{4,12},{5,13},{6,14},{7,15},{8,0},{9,1},... | collective-permute-start | bytes 294920 | tf_op jit(solution)/shard_map/ppermute | solution.py:889
  52.4 6.0 %text_attention.1 = (bf16[2048,1152]{1,0:T(8,128)(2,1)}, bf16[2048,384]{1,0:T(8,128)(2,1)S(1)}, f32[2048,384]{1,0:T(8,128)S(1)}) custom-call(s32[28]{0:T(128)S(1)} %get-tuple-element.76.plan_ref.ids_ref, bf16[128,16,384]{2,1,0:T(8,128)(2,1)S(1)} %copy-done, bf16[32,16,384]{2,1,0:T(8,128)(2,1)S(1)} %collective-permute-done.recv_ref, ...), custom_call_target="tpu_custom_call" | custom-call | flops 3019898880 | bytes 12582912 | tf_op jit(solution)/shard_map/text_attention/pallas_call | solution.py:474
  60.2 3.8 %collective-permute-start.7 = (bf16[512,384]{1,0:T(8,128)(2,1)S(1)}, bf16[512,384]{1,0:T(8,128)(2,1)S(1)}, u32[]{:S(2)}, u32[]{:S(2)}) collective-permute-start(bf16[512,384]{1,0:T(8,128)(2,1)S(1)} %constant_dynamic-update-slice_fusion.refs_2_), channel_id=1, source_target_pairs={{0,1},{1,0},{2,3},{3,2},{4,5},{5,4},{6,7},{7,6},{8,9},{9,8},{10,11... | collective-permute-start | bytes 1179656 | tf_op jit(solution)/shard_map/ppermute | solution.py:889
  63.9 7.1 %text_pool.1 = (bf16[2048,1536]{1,0:T(8,128)(2,1)S(1)}, f32[128,1536]{1,0:T(8,128)S(1)}, bf16[128,384]{1,0:T(8,128)(2,1)S(1)}, f32[128,384]{1,0:T(8,128)S(1)}, bf16[128,384]{1,0:T(8,128)(2,1)S(1)}) custom-call(s32[28]{0:T(128)S(1)} %get-tuple-element.76.plan_ref.ids_ref, f32[2048,384]{1,0:T(8,128)S(1)} %get-tuple-element.80.y1_ref, ...), custom_call_target="tpu_custom_call" | custom-call | flops 2415919104 | bytes 12582912 | tf_op jit(solution)/shard_map/text_pool/pallas_call | solution.py:551
  71.1 6.9 %collective-permute-start.6 = (bf16[128,384]{1,0:T(8,128)(2,1)S(1)}, bf16[128,384]{1,0:T(8,128)(2,1)S(1)}, u32[]{:S(2)}, u32[]{:S(2)}) collective-permute-start(bf16[128,384]{1,0:T(8,128)(2,1)S(1)} %get-tuple-element.85.refs_0_), channel_id=1, source_target_pairs={{0,16},{16,0},{1,17},{17,1},{2,18},{18,2},{3,19},{19,3},{4,20},{20... | collective-permute-start | bytes 294920 | tf_op jit(solution)/shard_map/ppermute | solution.py:889
  78.0 2.8 %collective-permute-done.6.refs_1_ = bf16[128,384]{1,0:T(8,128)(2,1)S(1)} collective-permute-done((bf16[128,384]{1,0:T(8,128)(2,1)S(1)}, bf16[128,384]{1,0:T(8,128)(2,1)S(1)}, u32[]{:S(2)}, u32[]{:S(2)}) %collective-permute-start.6) | collective-permute-done | bytes 98336 | tf_op jit(solution)/shard_map/ppermute | solution.py:889
  84.8 2.2 %collective-permute-start.11 = (f32[16,128]{1,0:T(8,128)S(1)}, f32[16,128]{1,0:T(8,128)S(1)}, u32[]{:S(2)}, u32[]{:S(2)}) collective-permute-start(f32[16,128]{1,0:T(8,128)S(1)} %add.131), channel_id=1, source_target_pairs={{0,8},{1,9},{2,10},{3,11},{4,12},{5,13},{6,14},{7,15},{8,0},{9,1},... | collective-permute-start | bytes 24584 | tf_op jit(solution)/shard_map/ppermute | solution.py:889
  88.2 3.2 %collective-permute-start.12 = (f32[16,128]{1,0:T(8,128)S(1)}, f32[16,128]{1,0:T(8,128)S(1)}, u32[]{:S(2)}, u32[]{:S(2)}) collective-permute-start(f32[16,128]{1,0:T(8,128)S(1)} %add.132), channel_id=1, source_target_pairs={{0,1},{1,0},{2,3},{3,2},{4,5},{5,4},{6,7},{7,6},{8,9},{9,8},{10,11... | collective-permute-start | bytes 24584 | tf_op jit(solution)/shard_map/ppermute | solution.py:889
  94.7 2.4 %similarity_grads.1 = (f32[128,384]{1,0:T(8,128)S(1)}, bf16[128,384]{1,0:T(8,128)(2,1)S(1)}, f32[8,128]{1,0:T(8,128)S(1)}) custom-call(s32[28]{0:T(128)S(1)} %get-tuple-element.76.plan_ref.ids_ref, f32[8,128]{1,0:T(8,128)S(1)} %copy-done.2, f32[2,128]{1,0:T(2,128)S(1)} %copy-done.3, f32[16,128]{1,0:T(8,128)S(1)} %copy-done.1, ...), custom_call_target="tpu_custom_call" | custom-call | flops 805306368 | bytes 1572864 | tf_op jit(solution)/shard_map/similarity_grads/pallas_call | solution.py:656
  98.7 2.5 %collective-permute-done.16.refs_0_ = bf16[128,384]{1,0:T(8,128)(2,1)S(1)} collective-permute-done((bf16[128,384]{1,0:T(8,128)(2,1)S(1)}, bf16[128,384]{1,0:T(8,128)(2,1)S(1)}, u32[]{:S(2)}, u32[]{:S(2)}) %collective-permute-start.16) | collective-permute-done | bytes 98336 | tf_op jit(solution)/shard_map/ppermute | solution.py:889
  101.2 22.7 %text_backward.1 = (bf16[128,16,384]{2,1,0:T(8,128)(2,1)}, bf16[1024,384]{1,0:T(8,128)(2,1)}, bf16[1024,384]{1,0:T(8,128)(2,1)}, bf16[768,384]{1,0:T(8,128)(2,1)...) custom-call(s32[28]{0:T(128)S(1)} %get-tuple-element.76.plan_ref.ids_ref, ...), custom_call_target="tpu_custom_call" | custom-call | flops 10871635968 | bytes 25165824 | tf_op jit(solution)/shard_map/text_backward/pallas_call | solution.py:857
  124.9 8.4 %collective-permute-start.22 = (bf16[32,16,384]{2,1,0:T(8,128)(2,1)S(1)}, bf16[32,16,384]{2,1,0:T(8,128)(2,1)S(1)}, u32[]{:S(2)}, u32[]{:S(2)}) collective-permute-start(bf16[32,16,384]{2,1,0:T(8,128)(2,1)S(1)} %slice.40), channel_id=1, source_target_pairs={{0,16},{16,0},{1,17},{17,1},{2,18},{18,2},{3,19},{19,3},{4,20},{20... | collective-permute-start | bytes 1179656 | tf_op jit(solution)/shard_map/ppermute | solution.py:889
  137.3 4.2 %collective-permute-done.22 = bf16[32,16,384]{2,1,0:T(8,128)(2,1)S(1)} collective-permute-done((bf16[32,16,384]{2,1,0:T(8,128)(2,1)S(1)}, bf16[32,16,384]{2,1,0:T(8,128)(2,1)S(1)}, u32[]{:S(2)}, u32[]{:S(2)}) %collective-permute-start.22) | collective-permute-done | bytes 393248 | tf_op jit(solution)/shard_map/ppermute | solution.py:889
  141.5 1.9 select_dynamic-update-slice_fusion
  147.9 2.7 %collective-permute-done.37 = bf16[384,384]{1,0:T(8,128)(2,1)S(1)} collective-permute-done((bf16[384,384]{1,0:T(8,128)(2,1)S(1)}, bf16[384,384]{1,0:T(8,128)(2,1)S(1)}, u32[]{:S(2)}, u32[]{:S(2)}) %collective-permute-start.37) | collective-permute-done | bytes 294944 | tf_op jit(solution)/shard_map/ppermute | solution.py:889
  153.0 3.1 %collective-permute-done.38 = bf16[192,384]{1,0:T(8,128)(2,1)S(1)} collective-permute-done((bf16[192,384]{1,0:T(8,128)(2,1)S(1)}, bf16[192,384]{1,0:T(8,128)(2,1)S(1)}, u32[]{:S(2)}, u32[]{:S(2)}) %collective-permute-start.38) | collective-permute-done | bytes 147488 | tf_op jit(solution)/shard_map/ppermute | solution.py:889
  160.6 2.2 %collective-permute-start.40 = (bf16[96,384]{1,0:T(8,128)(2,1)S(1)}, bf16[96,384]{1,0:T(8,128)(2,1)S(1)}, u32[]{:S(2)}, u32[]{:S(2)}) collective-permute-start(bf16[96,384]{1,0:T(8,128)(2,1)S(1)} %fusion.7), channel_id=1, source_target_pairs={{0,8},{1,9},{2,10},{3,11},{4,12},{5,13},{6,14},{7,15},{8,0},{9,1},... | collective-permute-start | bytes 221192 | tf_op jit(solution)/shard_map/ppermute | solution.py:889
  164.6 3.9 %collective-permute-done.19 = bf16[256,384]{1,0:T(8,128)(2,1)S(1)} collective-permute-done((bf16[256,384]{1,0:T(8,128)(2,1)S(1)}, bf16[256,384]{1,0:T(8,128)(2,1)S(1)}, u32[]{:S(2)}, u32[]{:S(2)}) %collective-permute-start.19) | collective-permute-done | bytes 196640 | tf_op jit(solution)/shard_map/ppermute | solution.py:889
  170.7 2.1 collective-permute-done.20
  174.1 4.3 %collective-permute-done.21 = bf16[128,384]{1,0:T(8,128)(2,1)S(1)} collective-permute-done((bf16[128,384]{1,0:T(8,128)(2,1)S(1)}, bf16[128,384]{1,0:T(8,128)(2,1)S(1)}, u32[]{:S(2)}, u32[]{:S(2)}) %collective-permute-start.21) | collective-permute-done | bytes 98336 | tf_op jit(solution)/shard_map/ppermute | solution.py:889
  180.0 2.4 %collective-permute-done.23 = bf16[128,384]{1,0:T(8,128)(2,1)S(1)} collective-permute-done((bf16[128,384]{1,0:T(8,128)(2,1)S(1)}, bf16[128,384]{1,0:T(8,128)(2,1)S(1)}, u32[]{:S(2)}, u32[]{:S(2)}) %collective-permute-start.23) | collective-permute-done | bytes 98336 | tf_op jit(solution)/shard_map/ppermute | solution.py:889
  189.0 6.4 %collective-permute-done.25 = bf16[512,384]{1,0:T(8,128)(2,1)S(1)} collective-permute-done((bf16[512,384]{1,0:T(8,128)(2,1)S(1)}, bf16[512,384]{1,0:T(8,128)(2,1)S(1)}, u32[]{:S(2)}, u32[]{:S(2)}) %collective-permute-start.25) | collective-permute-done | bytes 393248 | tf_op jit(solution)/shard_map/ppermute | solution.py:889
  195.5 7.5 %collective-permute-start.26 = (bf16[1024,384]{1,0:T(8,128)(2,1)S(1)}, bf16[1024,384]{1,0:T(8,128)(2,1)S(1)}, u32[]{:S(2)}, u32[]{:S(2)}) collective-permute-start(bf16[1024,384]{1,0:T(8,128)(2,1)S(1)} %constant_dynamic-update-slice_fusion.4.own_ref), channel_id=1, source_target_pairs={{0,1},{1,0},{2,3},{3,2},{4,5},{5,4},{6,7},{7,6},{8,9},{9,8},{10,11... | collective-permute-start | bytes 2359304 | tf_op jit(solution)/shard_map/ppermute | solution.py:889
  203.8 2.0 collective-permute-done.44.other_ref
  205.8 2.8 %place_gradients.5 = f32[384,1536]{1,0:T(8,128)} custom-call(s32[28]{0:T(128)S(1)} %get-tuple-element.76.plan_ref.ids_ref, bf16[768,384]{1,0:T(8,128)(2,1)S(1)} %pad_maximum_fusion.1.own_ref, bf16[768,384]{1,0:T(8,128)(2,1)S(1)} %collective-permute-done.44.other_ref), custom_call_target="tpu_custom_call" | custom-call | tf_op jit(solution)/shard_map/place_gradients/pallas_call | solution.py:994
  208.6 2.8 %place_gradients.4 = (f32[384,384]{1,0:T(8,128)}, f32[384,1152]{1,0:T(8,128)}) custom-call(s32[28]{0:T(128)S(1)} %get-tuple-element.76.plan_ref.ids_ref, bf16[768,384]{1,0:T(8,128)(2,1)S(1)} %pad_maximum_fusion.own_ref, bf16[768,384]{1,0:T(8,128)(2,1)S(1)} %collective-permute-done.35.other_ref), custom_call_target="tpu_custom_call" | custom-call | tf_op jit(solution)/shard_map/place_gradients/pallas_call | solution.py:994
  211.4 3.1 %place_gradients.3 = (f32[1536,384]{1,0:T(8,128)}, f32[384,384]{1,0:T(8,128)}, f32[384]{0:T(512)}, f32[384]{0:T(512)}, f32[1]{0:T(128)}, /*index=5*/f32[1]{0:T(128)}) custom-call(s32[28]{0:T(128)S(1)} %get-tuple-element.76.plan_ref.ids_ref, bf16[1024,384]{1,0:T(8,128)(2,1)S(1)} %constant_dynamic-update-slice_fusion.4.own_ref, ...), custom_call_target="tpu_custom_call" | custom-call | tf_op jit(solution)/shard_map/place_gradients/pallas_call | solution.py:994
  (163 shorter events, 50.1 us)
Async XLA Ops:
  2.2 29.0 %collective-permute-start.2 = (bf16[50,32,384]{2,1,0:T(8,128)(2,1)S(1)}, bf16[50,32,384]{2,1,0:T(8,128)(2,1)}, u32[]{:S(2)}, u32[]{:S(2)}) collective-permute-start(bf16[50,32,384]{2,1,0:T(8,128)(2,1)S(1)} %slice.41), channel_id=1, source_target_pairs={{0,16},{16,0},{1,17},{17,1},{2,18},{18,2},{3,19},{19,3},{4,20},{20... | collective-permute-start | bytes 3686408 | tf_op jit(solution)/shard_map/ppermute | solution.py:889
  4.5 47.9 %collective-permute-start.1 = (f32[2,16]{1,0:T(2,128)S(1)}, f32[2,16]{1,0:T(2,128)S(1)}, u32[]{:S(2)}, u32[]{:S(2)}) collective-permute-start(f32[2,16]{1,0:T(2,128)S(1)} %slice.35), channel_id=1, source_target_pairs={{0,16},{16,0},{1,17},{17,1},{2,18},{18,2},{3,19},{19,3},{4,20},{20... | collective-permute-start | bytes 392 | tf_op jit(solution)/shard_map/ppermute | solution.py:889
  5.3 47.1 %collective-permute-start = (bf16[32,16,384]{2,1,0:T(8,128)(2,1)}, bf16[32,16,384]{2,1,0:T(8,128)(2,1)S(1)}, u32[]{:S(2)}, u32[]{:S(2)}) collective-permute-start(bf16[32,16,384]{2,1,0:T(8,128)(2,1)} %slice.33), channel_id=1, source_target_pairs={{0,16},{16,0},{1,17},{17,1},{2,18},{18,2},{3,19},{19,3},{4,20},{20... | collective-permute-start | bytes 1179656 | tf_op jit(solution)/shard_map/ppermute | solution.py:889
  48.8 9.7 %collective-permute-start.3 = (bf16[128,384]{1,0:T(8,128)(2,1)S(1)}, bf16[128,384]{1,0:T(8,128)(2,1)S(1)}, u32[]{:S(2)}, u32[]{:S(2)}) collective-permute-start(bf16[128,384]{1,0:T(8,128)(2,1)S(1)} %pad_maximum_fusion.8), channel_id=1, source_target_pairs={{0,4},{1,5},{2,6},{3,7},{4,0},{5,1},{6,2},{7,3},{8,12},{9,13},{10,... | collective-permute-start | bytes 294920 | tf_op jit(solution)/shard_map/ppermute | solution.py:889
  50.1 8.4 %collective-permute-start.4 = (bf16[128,384]{1,0:T(8,128)(2,1)S(1)}, bf16[128,384]{1,0:T(8,128)(2,1)S(1)}, u32[]{:S(2)}, u32[]{:S(2)}) collective-permute-start(bf16[128,384]{1,0:T(8,128)(2,1)S(1)} %pad_maximum_fusion.8), channel_id=1, source_target_pairs={{0,8},{1,9},{2,10},{3,11},{4,12},{5,13},{6,14},{7,15},{8,0},{9,1},... | collective-permute-start | bytes 294920 | tf_op jit(solution)/shard_map/ppermute | solution.py:889
  52.4 6.4 %collective-permute-start.5 = (bf16[128,384]{1,0:T(8,128)(2,1)S(1)}, bf16[128,384]{1,0:T(8,128)(2,1)S(1)}, u32[]{:S(2)}, u32[]{:S(2)}) collective-permute-start(bf16[128,384]{1,0:T(8,128)(2,1)S(1)} %pad_maximum_fusion.8), channel_id=1, source_target_pairs={{0,12},{1,13},{2,14},{3,15},{4,8},{5,9},{6,10},{7,11},{8,4},{9,5},... | collective-permute-start | bytes 294920 | tf_op jit(solution)/shard_map/ppermute | solution.py:889
  58.9 12.1 %collective-permute-start.8 = (bf16[512,384]{1,0:T(8,128)(2,1)S(1)}, bf16[512,384]{1,0:T(8,128)(2,1)S(1)}, u32[]{:S(2)}, u32[]{:S(2)}) collective-permute-start(bf16[512,384]{1,0:T(8,128)(2,1)S(1)} %constant_dynamic-update-slice_fusion.refs_2_), channel_id=1, source_target_pairs={{0,2},{1,3},{2,0},{3,1},{4,6},{5,7},{6,4},{7,5},{8,10},{9,11},{10,... | collective-permute-start | bytes 1179656 | tf_op jit(solution)/shard_map/ppermute | solution.py:889
  60.2 20.6 %collective-permute-start.7 = (bf16[512,384]{1,0:T(8,128)(2,1)S(1)}, bf16[512,384]{1,0:T(8,128)(2,1)S(1)}, u32[]{:S(2)}, u32[]{:S(2)}) collective-permute-start(bf16[512,384]{1,0:T(8,128)(2,1)S(1)} %constant_dynamic-update-slice_fusion.refs_2_), channel_id=1, source_target_pairs={{0,1},{1,0},{2,3},{3,2},{4,5},{5,4},{6,7},{7,6},{8,9},{9,8},{10,11... | collective-permute-start | bytes 1179656 | tf_op jit(solution)/shard_map/ppermute | solution.py:889
  71.0 9.8 %collective-permute-start.9 = (bf16[512,384]{1,0:T(8,128)(2,1)S(1)}, bf16[512,384]{1,0:T(8,128)(2,1)S(1)}, u32[]{:S(2)}, u32[]{:S(2)}) collective-permute-start(bf16[512,384]{1,0:T(8,128)(2,1)S(1)} %collective-permute-done.8.refs_4_), channel_id=1, source_target_pairs={{0,1},{1,0},{2,3},{3,2},{4,5},{5,4},{6,7},{7,6},{8,9},{9,8},{10,11... | collective-permute-start | bytes 1179656 | tf_op jit(solution)/shard_map/ppermute | solution.py:889
  71.1 9.7 %collective-permute-start.6 = (bf16[128,384]{1,0:T(8,128)(2,1)S(1)}, bf16[128,384]{1,0:T(8,128)(2,1)S(1)}, u32[]{:S(2)}, u32[]{:S(2)}) collective-permute-start(bf16[128,384]{1,0:T(8,128)(2,1)S(1)} %get-tuple-element.85.refs_0_), channel_id=1, source_target_pairs={{0,16},{16,0},{1,17},{17,1},{2,18},{18,2},{3,19},{19,3},{4,20},{20... | collective-permute-start | bytes 294920 | tf_op jit(solution)/shard_map/ppermute | solution.py:889
  124.9 16.6 %collective-permute-start.22 = (bf16[32,16,384]{2,1,0:T(8,128)(2,1)S(1)}, bf16[32,16,384]{2,1,0:T(8,128)(2,1)S(1)}, u32[]{:S(2)}, u32[]{:S(2)}) collective-permute-start(bf16[32,16,384]{2,1,0:T(8,128)(2,1)S(1)} %slice.40), channel_id=1, source_target_pairs={{0,16},{16,0},{1,17},{17,1},{2,18},{18,2},{3,19},{19,3},{4,20},{20... | collective-permute-start | bytes 1179656 | tf_op jit(solution)/shard_map/ppermute | solution.py:889
  133.3 10.0 %collective-permute-start.36 = (bf16[768,384]{1,0:T(8,128)(2,1)}, bf16[768,384]{1,0:T(8,128)(2,1)S(1)}, u32[]{:S(2)}, u32[]{:S(2)}) collective-permute-start(bf16[768,384]{1,0:T(8,128)(2,1)} %get-tuple-element.111), channel_id=1, source_target_pairs={{0,1},{1,0},{2,3},{3,2},{4,5},{5,4},{6,7},{7,6},{8,9},{9,8},{10,11... | collective-permute-start | bytes 1769480 | tf_op jit(solution)/shard_map/ppermute | solution.py:889
  136.8 8.5 %collective-permute-start.27 = (bf16[768,384]{1,0:T(8,128)(2,1)}, bf16[768,384]{1,0:T(8,128)(2,1)S(1)}, u32[]{:S(2)}, u32[]{:S(2)}) collective-permute-start(bf16[768,384]{1,0:T(8,128)(2,1)} %get-tuple-element.106), channel_id=1, source_target_pairs={{0,1},{1,0},{2,3},{3,2},{4,5},{5,4},{6,7},{7,6},{8,9},{9,8},{10,11... | collective-permute-start | bytes 1769480 | tf_op jit(solution)/shard_map/ppermute | solution.py:889
  136.8 9.6 %collective-permute-start.17 = (bf16[1024,384]{1,0:T(8,128)(2,1)}, bf16[1024,384]{1,0:T(8,128)(2,1)S(1)}, u32[]{:S(2)}, u32[]{:S(2)}) collective-permute-start(bf16[1024,384]{1,0:T(8,128)(2,1)} %get-tuple-element.100), channel_id=1, source_target_pairs={{0,1},{1,0},{2,3},{3,2},{4,5},{5,4},{6,7},{7,6},{8,9},{9,8},{10,11... | collective-permute-start | bytes 2359304 | tf_op jit(solution)/shard_map/ppermute | solution.py:889
  143.6 7.0 %collective-permute-start.37 = (bf16[384,384]{1,0:T(8,128)(2,1)S(1)}, bf16[384,384]{1,0:T(8,128)(2,1)S(1)}, u32[]{:S(2)}, u32[]{:S(2)}) collective-permute-start(bf16[384,384]{1,0:T(8,128)(2,1)S(1)} %fusion.2), channel_id=1, source_target_pairs={{0,2},{1,3},{2,0},{3,1},{4,6},{5,7},{6,4},{7,5},{8,10},{9,11},{10,... | collective-permute-start | bytes 884744 | tf_op jit(solution)/shard_map/ppermute | solution.py:889
  145.4 6.6 %collective-permute-start.28 = (bf16[384,384]{1,0:T(8,128)(2,1)S(1)}, bf16[384,384]{1,0:T(8,128)(2,1)S(1)}, u32[]{:S(2)}, u32[]{:S(2)}) collective-permute-start(bf16[384,384]{1,0:T(8,128)(2,1)S(1)} %fusion.1), channel_id=1, source_target_pairs={{0,4},{1,5},{2,6},{3,7},{4,0},{5,1},{6,2},{7,3},{8,12},{9,13},{10,... | collective-permute-start | bytes 884744 | tf_op jit(solution)/shard_map/ppermute | solution.py:889
  146.7 16.1 %collective-permute-start.18 = (bf16[512,384]{1,0:T(8,128)(2,1)S(1)}, bf16[512,384]{1,0:T(8,128)(2,1)S(1)}, u32[]{:S(2)}, u32[]{:S(2)}) collective-permute-start(bf16[512,384]{1,0:T(8,128)(2,1)S(1)} %fusion), channel_id=1, source_target_pairs={{0,16},{16,0},{1,17},{17,1},{2,18},{18,2},{3,19},{19,3},{4,20},{20... | collective-permute-start | bytes 1179656 | tf_op jit(solution)/shard_map/ppermute | solution.py:889
  150.7 5.4 %collective-permute-start.38 = (bf16[192,384]{1,0:T(8,128)(2,1)S(1)}, bf16[192,384]{1,0:T(8,128)(2,1)S(1)}, u32[]{:S(2)}, u32[]{:S(2)}) collective-permute-start(bf16[192,384]{1,0:T(8,128)(2,1)S(1)} %fusion.6), channel_id=1, source_target_pairs={{0,4},{1,5},{2,6},{3,7},{4,0},{5,1},{6,2},{7,3},{8,12},{9,13},{10,... | collective-permute-start | bytes 442376 | tf_op jit(solution)/shard_map/ppermute | solution.py:889
  152.1 6.2 %collective-permute-start.29 = (bf16[192,384]{1,0:T(8,128)(2,1)S(1)}, bf16[192,384]{1,0:T(8,128)(2,1)S(1)}, u32[]{:S(2)}, u32[]{:S(2)}) collective-permute-start(bf16[192,384]{1,0:T(8,128)(2,1)S(1)} %fusion.5), channel_id=1, source_target_pairs={{0,16},{16,0},{1,17},{17,1},{2,18},{18,2},{3,19},{19,3},{4,20},{20... | collective-permute-start | bytes 442376 | tf_op jit(solution)/shard_map/ppermute | solution.py:889
  158.3 5.5 %collective-permute-start.30 = (bf16[96,384]{1,0:T(8,128)(2,1)S(1)}, bf16[96,384]{1,0:T(8,128)(2,1)S(1)}, u32[]{:S(2)}, u32[]{:S(2)}) collective-permute-start(bf16[96,384]{1,0:T(8,128)(2,1)S(1)} %fusion.10), channel_id=1, source_target_pairs={{0,2},{1,3},{2,0},{3,1},{4,6},{5,7},{6,4},{7,5},{8,10},{9,11},{10,... | collective-permute-start | bytes 221192 | tf_op jit(solution)/shard_map/ppermute | solution.py:889
  160.6 8.9 %collective-permute-start.40 = (bf16[96,384]{1,0:T(8,128)(2,1)S(1)}, bf16[96,384]{1,0:T(8,128)(2,1)S(1)}, u32[]{:S(2)}, u32[]{:S(2)}) collective-permute-start(bf16[96,384]{1,0:T(8,128)(2,1)S(1)} %fusion.7), channel_id=1, source_target_pairs={{0,8},{1,9},{2,10},{3,11},{4,12},{5,13},{6,14},{7,15},{8,0},{9,1},... | collective-permute-start | bytes 221192 | tf_op jit(solution)/shard_map/ppermute | solution.py:889
  162.9 5.5 %collective-permute-start.19 = (bf16[256,384]{1,0:T(8,128)(2,1)S(1)}, bf16[256,384]{1,0:T(8,128)(2,1)S(1)}, u32[]{:S(2)}, u32[]{:S(2)}) collective-permute-start(bf16[256,384]{1,0:T(8,128)(2,1)S(1)} %fusion.3), channel_id=1, source_target_pairs={{0,2},{1,3},{2,0},{3,1},{4,6},{5,7},{6,4},{7,5},{8,10},{9,11},{10,... | collective-permute-start | bytes 589832 | tf_op jit(solution)/shard_map/ppermute | solution.py:889
  163.8 9.1 %collective-permute-start.31 = (bf16[96,384]{1,0:T(8,128)(2,1)S(1)}, bf16[96,384]{1,0:T(8,128)(2,1)S(1)}, u32[]{:S(2)}, u32[]{:S(2)}) collective-permute-start(bf16[96,384]{1,0:T(8,128)(2,1)S(1)} %fusion.8), channel_id=1, source_target_pairs={{0,8},{1,9},{2,10},{3,11},{4,12},{5,13},{6,14},{7,15},{8,0},{9,1},... | collective-permute-start | bytes 221192 | tf_op jit(solution)/shard_map/ppermute | solution.py:889
  169.5 9.0 %collective-permute-start.41 = (bf16[96,384]{1,0:T(8,128)(2,1)S(1)}, bf16[96,384]{1,0:T(8,128)(2,1)S(1)}, u32[]{:S(2)}, u32[]{:S(2)}) collective-permute-start(bf16[96,384]{1,0:T(8,128)(2,1)S(1)} %add_convert_fusion.1), channel_id=1, source_target_pairs={{0,16},{16,0},{1,17},{17,1},{2,18},{18,2},{3,19},{19,3},{4,20},{20... | collective-permute-start | bytes 221192 | tf_op jit(solution)/shard_map/ppermute | solution.py:889
  172.9 5.5 %collective-permute-start.21 = (bf16[128,384]{1,0:T(8,128)(2,1)S(1)}, bf16[128,384]{1,0:T(8,128)(2,1)S(1)}, u32[]{:S(2)}, u32[]{:S(2)}) collective-permute-start(bf16[128,384]{1,0:T(8,128)(2,1)S(1)} %fusion.4), channel_id=1, source_target_pairs={{0,8},{1,9},{2,10},{3,11},{4,12},{5,13},{6,14},{7,15},{8,0},{9,1},... | collective-permute-start | bytes 294920 | tf_op jit(solution)/shard_map/ppermute | solution.py:889
  173.0 10.8 %collective-permute-start.32 = (bf16[96,384]{1,0:T(8,128)(2,1)S(1)}, bf16[96,384]{1,0:T(8,128)(2,1)S(1)}, u32[]{:S(2)}, u32[]{:S(2)}) collective-permute-start(bf16[96,384]{1,0:T(8,128)(2,1)S(1)} %add_convert_fusion.2), channel_id=1, source_target_pairs={{0,2},{1,3},{2,0},{3,1},{4,6},{5,7},{6,4},{7,5},{8,10},{9,11},{10,... | collective-permute-start | bytes 221192 | tf_op jit(solution)/shard_map/ppermute | solution.py:889
  178.5 6.5 %collective-permute-start.42 = (bf16[192,384]{1,0:T(8,128)(2,1)S(1)}, bf16[192,384]{1,0:T(8,128)(2,1)S(1)}, u32[]{:S(2)}, u32[]{:S(2)}) collective-permute-start(bf16[192,384]{1,0:T(8,128)(2,1)S(1)} %pad_maximum_fusion.7), channel_id=1, source_target_pairs={{0,4},{1,5},{2,6},{3,7},{4,0},{5,1},{6,2},{7,3},{8,12},{9,13},{10,... | collective-permute-start | bytes 442376 | tf_op jit(solution)/shard_map/ppermute | solution.py:889
  185.1 18.0 %collective-permute-start.43 = (bf16[384,384]{1,0:T(8,128)(2,1)S(1)}, bf16[384,384]{1,0:T(8,128)(2,1)S(1)}, u32[]{:S(2)}, u32[]{:S(2)}) collective-permute-start(bf16[384,384]{1,0:T(8,128)(2,1)S(1)} %pad_maximum_fusion.4), channel_id=1, source_target_pairs={{0,2},{1,3},{2,0},{3,1},{4,6},{5,7},{6,4},{7,5},{8,10},{9,11},{10,... | collective-permute-start | bytes 884744 | tf_op jit(solution)/shard_map/ppermute | solution.py:889
  187.1 8.4 %collective-permute-start.25 = (bf16[512,384]{1,0:T(8,128)(2,1)S(1)}, bf16[512,384]{1,0:T(8,128)(2,1)S(1)}, u32[]{:S(2)}, u32[]{:S(2)}) collective-permute-start(bf16[512,384]{1,0:T(8,128)(2,1)S(1)} %pad_maximum_fusion.2), channel_id=1, source_target_pairs={{0,16},{16,0},{1,17},{17,1},{2,18},{18,2},{3,19},{19,3},{4,20},{20... | collective-permute-start | bytes 1179656 | tf_op jit(solution)/shard_map/ppermute | solution.py:889
  188.3 14.9 %collective-permute-start.34 = (bf16[384,384]{1,0:T(8,128)(2,1)S(1)}, bf16[384,384]{1,0:T(8,128)(2,1)S(1)}, u32[]{:S(2)}, u32[]{:S(2)}) collective-permute-start(bf16[384,384]{1,0:T(8,128)(2,1)S(1)} %pad_maximum_fusion.3), channel_id=1, source_target_pairs={{0,4},{1,5},{2,6},{3,7},{4,0},{5,1},{6,2},{7,3},{8,12},{9,13},{10,... | collective-permute-start | bytes 884744 | tf_op jit(solution)/shard_map/ppermute | solution.py:889
  195.5 15.9 %collective-permute-start.26 = (bf16[1024,384]{1,0:T(8,128)(2,1)S(1)}, bf16[1024,384]{1,0:T(8,128)(2,1)S(1)}, u32[]{:S(2)}, u32[]{:S(2)}) collective-permute-start(bf16[1024,384]{1,0:T(8,128)(2,1)S(1)} %constant_dynamic-update-slice_fusion.4.own_ref), channel_id=1, source_target_pairs={{0,1},{1,0},{2,3},{3,2},{4,5},{5,4},{6,7},{7,6},{8,9},{9,8},{10,11... | collective-permute-start | bytes 2359304 | tf_op jit(solution)/shard_map/ppermute | solution.py:889
  203.2 5.3 %collective-permute-start.35 = (bf16[768,384]{1,0:T(8,128)(2,1)S(1)}, bf16[768,384]{1,0:T(8,128)(2,1)S(1)}, u32[]{:S(2)}, u32[]{:S(2)}) collective-permute-start(bf16[768,384]{1,0:T(8,128)(2,1)S(1)} %pad_maximum_fusion.own_ref), channel_id=1, source_target_pairs={{0,1},{1,0},{2,3},{3,2},{4,5},{5,4},{6,7},{7,6},{8,9},{9,8},{10,11... | collective-permute-start | bytes 1769480 | tf_op jit(solution)/shard_map/ppermute | solution.py:889
  (30 other events, 303.0 us)

commit v2 on v1

--- a/solution.py
+++ b/solution.py
@@ -15,6 +15,7 @@
 GELU_B = 0.7978845608028654 * 0.044715
 SAFE = 60.0
 GROUP = 8
+PITCH = 9
 IMAGE_NB = 16
 USE = 2
 ACTIVE = 3
@@ -44,6 +45,16 @@
     return mm(hi, b) + mm(lo, b)
 
 
+def column_chunks(width):
+    edge = width // 2 // 256 * 256
+    return ((0, edge), (edge, width))
+
+
+def over(a, b):
+    r = pl.reciprocal(b, approx=True)
+    return a * (r * (2.0 - b * r))
+
+
 def normed(v):
     c = v - jnp.mean(v, axis=-1, keepdims=True)
     return c * lax.rsqrt(jnp.mean(c * c, axis=-1, keepdims=True) + epsilon)
@@ -66,7 +77,7 @@
 
     @pl.when(step == 0)
     def _():
-        qkv[:, :, rows:, :] = jnp.zeros(qkv.shape[:2] + (qkv.shape[2] - rows, 128), F32)
+        qkv[...] = jnp.zeros_like(qkv)
         hsum[...] = jnp.zeros_like(hsum)
         xsum[...] = jnp.zeros_like(xsum)
 
@@ -86,7 +97,7 @@
 def image_block(step, block, cut, plan_ref, x_ref, recv_ref, wqkv_ref, wout_ref, wup_ref, qkv, att, hsum, xsum):
     length, nb, width = x_ref.shape
     rows = length * GROUP
-    slots = qkv.shape[2] // GROUP
+    slots = qkv.shape[2] // PITCH
     tiles = width // 128
     ff = wup_ref.shape[1]
     groups = nb // GROUP
@@ -109,27 +120,35 @@
         return pl.ds(pl.multiple_of(step * nb + g * GROUP, GROUP), GROUP)
 
     def scores(g, p, h):
-        at = pl.ds(p, slots, stride=GROUP)
+        at = pl.ds(p, slots, stride=PITCH)
         q = qkv[g, h, at, :].astype(BF16) * BF16(HEAD**-0.5)
         k = qkv[g, tiles + h, at, :]
         return mm_t(q, jnp.concatenate([k * low, k * high], axis=0).astype(BF16))
 
     def weighted(g, p, h, e):
-        at = pl.ds(p, slots, stride=GROUP)
+        at = pl.ds(p, slots, stride=PITCH)
         v = qkv[g, 2 * tiles + h, at, :]
         vbd = jnp.concatenate([v * low, v * high], axis=0).astype(BF16)
         o = mm(e.astype(BF16), jnp.concatenate([vbd, ones], axis=1))
-        att[g, h, at, :] = o[:, :128] / o[:, 128:]
+        att[g, h, at, :] = over(o[:, :128], o[:, 128:])
 
     def projected(g):
         n1 = normed(tokens(g)).astype(BF16)
-        for c in range(tiles):
-            made = mm(n1, wqkv_ref[:, c * width : (c + 1) * width])
-            for h in range(tiles):
-                qkv[g, c * tiles + h, :rows, :] = made[:, h * 128 : h * 128 + 128]
+        for first, last in column_chunks(3 * width):
+            made = mm(n1, wqkv_ref[:, first:last])
+            for c in range(first // 128, last // 128):
+                here = c * 128 - first
+                for t in range(length):
+                    qkv[g, c, t * PITCH : t * PITCH + GROUP, :] = made[t * GROUP : (t + 1) * GROUP, here : here + 128]
 
     def after_attention(g):
-        heads = jnp.concatenate([att[g, h, :rows, :] for h in range(tiles)], axis=1)
+        heads = jnp.concatenate(
+            [
+                jnp.concatenate([att[g, h, t * PITCH : t * PITCH + GROUP, :] for t in range(length)], axis=0)
+                for h in range(tiles)
+            ],
+            axis=1,
+        )
         x1 = tokens(g) + mm(heads.astype(BF16), wout_ref[...])
         xsum[pairs_of(g), :] = jnp.sum(x1.reshape(length, GROUP, width), axis=0)
         return normed(x1).astype(BF16)
@@ -233,8 +252,8 @@
             in_specs=specs + [fixed(w.shape) for w in weights],
             out_specs=pl.BlockSpec((count, width), lambda i, plan: (0, 0)),
             scratch_shapes=[
-                pltpu.VMEM((nb // GROUP, 3 * width // 128, slots * GROUP, 128), F32),
-                pltpu.VMEM((nb // GROUP, width // 128, slots * GROUP, 128), F32),
+                pltpu.VMEM((nb // GROUP, 3 * width // 128, slots * PITCH, 128), F32),
+                pltpu.VMEM((nb // GROUP, width // 128, slots * PITCH, 128), F32),
                 pltpu.VMEM((count, ff), F32),
                 pltpu.VMEM((count, width), F32),
             ],
@@ -310,11 +329,11 @@
     return jnp.sum(jnp.where(diagonal, col, 0.0), axis=0, keepdims=True)
 
 
-def prepare_kernel(cut, place_ref, count_ref, scale_ref, plan_ref, rlive_ref, tlive_ref, scal_ref):
+def prepare_kernel(cut, count_ref, scale_ref, plan_ref, rlive_ref, tlive_ref, scal_ref):
     rows, cols = count_ref.shape
     across = rows - 1
-    col = place_ref[0]
-    row = place_ref[1]
+    col = lax.axis_index("col")
+    row = lax.axis_index("row")
 
     def limits(r, c):
         n = count_ref[r, c]
@@ -357,11 +376,11 @@
     scal_ref[...] = jnp.where(index == 0, jnp.exp(jnp.full((8, 128), scale_ref[0], F32)), 0.5 / jnp.full((8, 128), total, jnp.int32).astype(F32))
 
 
-def prepare(place, pair_count, log_scale, cut):
+def prepare(pair_count, log_scale, cut):
     rows, cols = pair_count.shape
     return pl.pallas_call(
         functools.partial(prepare_kernel, cut),
-        in_specs=[SMEM] * 3,
+        in_specs=[SMEM] * 2,
         out_specs=[SMEM, VMEM, VMEM, VMEM],
         out_shape=[
             jax.ShapeDtypeStruct((PLAN,), jnp.int32),
@@ -370,7 +389,7 @@
             jax.ShapeDtypeStruct((8, 128), F32),
         ],
         name="prepare",
-    )(place, pair_count, log_scale)
+    )(pair_count, log_scale)
 
 
 def lengths_of(plan_ref, cut, part, lens_ref, got_ref):
@@ -431,9 +450,8 @@
 def text_attention(x, lens, length, gain_ref, wqkv_ref, wout_ref, qkv_ref, att_ref, y1_ref):
     rows, width = x.shape
     n1 = (normed(x) * gain_ref[...]).astype(BF16)
-    for c in range(3):
-        at = slice(c * width, (c + 1) * width)
-        qkv_ref[:, at] = mm(n1, wqkv_ref[:, at]).astype(BF16)
+    for first, last in column_chunks(3 * width):
+        qkv_ref[:, first:last] = mm(n1, wqkv_ref[:, first:last]).astype(BF16)
     lane = lax.broadcasted_iota(jnp.int32, (128, 128), 1)
     low = (lane[:1] < HEAD).astype(BF16)
     high = 1 - low
@@ -459,7 +477,7 @@
         v = qkv_ref[g : g + 128, 2 * width + h : 2 * width + h + 128]
         vbd = jnp.concatenate([v * low, v * high], axis=0)
         o = mm(e, jnp.concatenate([vbd, ones], axis=1))
-        att_ref[g : g + 128, h : h + 128] = (o[:, :128] / o[:, 128:]).astype(BF16)
+        att_ref[g : g + 128, h : h + 128] = over(o[:, :128], o[:, 128:]).astype(BF16)
 
     staggered([scores, expo, weighted], [(g, h) for g in range(0, rows, 128) for h in range(0, width, 128)], 1)
     y1_ref[...] = x + mm(att_ref[...], wout_ref[...])
@@ -691,7 +709,7 @@
     other_refs = refs[:others]
     stat_ref = refs[others]
     grad_ref, keep_a, send_a, keep_b, send_b, keep_c, send_c = refs[others + 1 : others + 8]
-    dyp, dhp, dproj, ddown, dmix, dheads, acc_up, acc_out, acc_qkv, bias_ref = refs[others + 8 :]
+    dyp, dhp, dproj, ddown, dmix, dheads, acc_up, acc_out, acc_qkv, bias_ref, du_ref = refs[others + 8 :]
     step = pl.program_id(0)
     block = plan_ref[ORDER + step]
     active = step < plan_ref[ACTIVE]
@@ -726,7 +744,7 @@
         lens = block_lengths(plan_ref, cut, block, lens_ref, got_ref)
         grad = back_block(
             block, x, lens, x_ref.shape[1], qkv_ref, att_ref, y1_ref, slope_ref, gain_ref, wqkv_ref, wout_ref,
-            gain_two_ref, wup_ref, dyp, dhp, dmix, dheads, acc_up, acc_out, acc_qkv, bias_ref,
+            gain_two_ref, wup_ref, dyp, dhp, dmix, dheads, acc_up, acc_out, acc_qkv, bias_ref, du_ref,
         )
         grad_ref[...] = grad.astype(BF16).reshape(grad_ref.shape)
 
@@ -754,7 +772,7 @@
 
 def back_block(
     block, x, lens, length, qkv_ref, att_ref, y1_ref, slope_ref, gain_ref, wqkv_ref, wout_ref,
-    gain_two_ref, wup_ref, dyp, dhp, dmix, dheads, acc_up, acc_out, acc_qkv, bias_ref,
+    gain_two_ref, wup_ref, dyp, dhp, dmix, dheads, acc_up, acc_out, acc_qkv, bias_ref, du_ref,
 ):
     rows, width = x.shape
     ff = wup_ref.shape[1]
@@ -765,12 +783,11 @@
 
     n2, inv = stats(y1_ref[...])
     n2_low = (n2 * gain_two_ref[...]).astype(BF16)
-    dn2 = jnp.zeros((rows, width), F32)
     for c in range(0, ff, width):
         at = slice(c, c + width)
-        du = (spread(dhp[pair, at]) * slope_ref[:, at].astype(F32)).astype(BF16)
-        acc_up[:, at] += mm_tn(n2_low, du)
-        dn2 = dn2 + mm_t(du, wup_ref[:, at])
+        du_ref[:, at] = (spread(dhp[pair, at]) * slope_ref[:, at].astype(F32)).astype(BF16)
+    dn2 = mm_t(du_ref[...], wup_ref[...])
+    acc_up[...] += mm_tn(n2_low, du_ref[...])
     live = mm_tn(live_pick(lens, rows).astype(BF16), jnp.ones((NB, 128), BF16))
     dy1 = spread(dyp[pair, :]) * jnp.concatenate([live] * (width // 128), axis=1)
     dy1 = dy1 + norm_back(dn2 * gain_two_ref[...], n2, inv)
@@ -780,11 +797,8 @@
     attention_grads(length, live, qkv_ref, dmix, dheads, bias_ref)
     n1, inv = stats(x)
     n1_low = (n1 * gain_ref[...]).astype(BF16)
-    dn1 = jnp.zeros((rows, width), F32)
-    for c in range(3):
-        at = slice(c * width, (c + 1) * width)
-        acc_qkv[:, at] += mm_tn(n1_low, dmix[:, at])
-        dn1 = dn1 + mm_t(dmix[:, at], wqkv_ref[:, at])
+    dn1 = mm_t(dmix[...], wqkv_ref[...])
+    acc_qkv[...] += mm_tn(n1_low, dmix[...])
     return dy1 + norm_back(dn1 * gain_ref[...], n1, inv)
 
 
@@ -799,6 +813,13 @@
     for g in range(rows // 128):
         bias_ref[g] = jnp.where(same & (live[g * 128 : g * 128 + 128, :] > 0), 0.0, -1e30)
 
+    zero = jnp.zeros((128, 128), BF16)
+
+    def both_sides(one, two):
+        return jnp.concatenate(
+            [jnp.concatenate([one, zero], axis=1), jnp.concatenate([zero, two], axis=1)], axis=0
+        )
+
     def pieces(unit, part):
         g, h = unit
         return qkv_ref[pl.ds(g * 128, 128), part * width + h : part * width + h + 128]
@@ -808,10 +829,11 @@
         k = pieces(unit, 1)
         v = pieces(unit, 2)
         do = dheads[pl.ds(g * 128, 128), h : h + 128]
-        kbd = jnp.concatenate([k * low, k * high], axis=0)
-        vbd = jnp.concatenate([v * low, v * high], axis=0)
-        s = mm_t(kbd, pieces(unit, 0) * BF16(HEAD**-0.5))
-        return s, mm_t(vbd, do)
+        left = jnp.concatenate(
+            [jnp.concatenate([k * low, v * low], axis=1), jnp.concatenate([k * high, v * high], axis=1)], axis=0
+        )
+        made = mm_t(left, both_sides(pieces(unit, 0) * BF16(HEAD**-0.5), do))
+        return made[:, :128], made[:, 128:]
 
     def soft(unit, made):
         g, _ = unit
@@ -828,9 +850,10 @@
         p, ds = made
         at = pl.ds(g * 128, 128)
         do = dheads[at, h : h + 128]
-        dv = mm(p, do)
+        made = mm(jnp.concatenate([p, ds], axis=1), both_sides(do, pieces(unit, 0) * BF16(HEAD**-0.5)))
+        dv = made[:, :128]
+        dk = made[:, 128:]
         dmix[at, 2 * width + h : 2 * width + h + 128] = jnp.where(first, dv[:128], dv[128:]).astype(BF16)
-        dk = mm(ds, pieces(unit, 0) * BF16(HEAD**-0.5))
         dmix[at, width + h : width + h + 128] = jnp.where(first, dk[:128], dk[128:]).astype(BF16)
         return mm_t(eye, ds).astype(BF16)
 
@@ -873,6 +896,7 @@
                 pltpu.VMEM((width, width), F32),
                 pltpu.VMEM((width, 3 * width), F32),
                 pltpu.VMEM((rows // 128, 128, 128), F32),
+                pltpu.VMEM((rows, ff), BF16),
             ],
         ),
         out_shape=[pltpu.HBM(x.shape, BF16)] + [pltpu.HBM(shape, BF16) for shape in shapes],
@@ -909,14 +933,16 @@
     return jnp.concatenate([piece] + [flip(piece, axis, p * unit) for p in range(1, ways)], axis=0)
 
 
-def exchange(keep, send, rounds, back=None):
+def exchange(keep, send, rounds, before_gather=None, before_last=None):
     kept = keep.astype(F32) + flip(send, "col", 1).astype(F32)
     for one in rounds:
         kept = reduce_round(kept, *one)
     piece = kept.astype(BF16)
-    if back is not None:
-        piece = tie(piece, back)
-    for one in reversed(rounds):
+    if before_gather is not None:
+        piece = tie(piece, before_gather)
+    for k, one in enumerate(reversed(rounds)):
+        if before_last is not None and k == len(rounds) - 1:
+            piece = tie(piece, before_last)
         piece = gather_round(piece, *one)
     return piece, flip(piece, "col", 1)
 
@@ -1021,7 +1047,7 @@
     got_texts = flip(text_tokens[cut:], "row", across)
     lens = lengths.astype(F32).reshape(pairs // QB, QB)
     got_lens = flip(lens[cut // QB :], "row", across)
-    plan, rlive, tlive, scal = prepare(jnp.stack([col_index, row_index]).astype(jnp.int32), pair_count, log_scale, cut)
+    plan, rlive, tlive, scal = prepare(pair_count, log_scale, cut)
     gain_one = gain_one.reshape(1, width)
     gain_two = gain_two.reshape(1, width)
 
@@ -1082,8 +1108,9 @@
     ]
     shapes = [[(ff, width), (width, width)], [(width, ff)], [(width, width), (width, 3 * width)]]
     placed = []
+    waits = [(back, None), (None, None), (None, None)]
     for keep, send, rounds, places, sizes in zip((keep_a, keep_b, keep_c), (send_a, send_b, send_c), orders, targets, shapes):
-        gathered = exchange(keep, send, rounds, text_grad if not placed else None)
+        gathered = exchange(keep, send, rounds, *waits.pop(0))
         placed += place(plan, gathered, places, rounds, sizes, not placed)
     sum_down, sum_proj, sum_one, sum_two, loss, sum_scale, sum_up, sum_out, sum_qkv = placed
     return (

time: 215 us -> 207 us (0.963)
  starting transfers between devices: 69.7 us -> 66.5 us
  waiting for transfers between devices: 46.6 us -> 44.3 us
    ppermute x45, starting transfers between devices: 69.7 us -> 66.5 us  [flip(): return lax.ppermute(values, axis, [(k, k ^ bits) for k in range(size)])]
    ppermute x45, waiting for transfers between devices: 46.6 us -> 44.3 us  [flip(): return lax.ppermute(values, axis, [(k, k ^ bits) for k in range(size)])]
  transfers between devices with their start and end apart: 45 -> 45, of which waited for: 21 -> 18; matrix products, arithmetic and copies ran while one was open for 3% -> 4% of each run, Pallas kernels for 26% -> 27%
where the time goes in v2:
time: 207 us
  Pallas kernels  82.6 us (40%)
  starting transfers between devices  66.5 us (32%)
  waiting for transfers between devices  44.3 us (21%)
  local copies, waits for them, and re-layouts  5.36 us (3%)
  between operations  3.94 us (2%)
  other arithmetic  3.85 us (2%)
    ppermute x45, starting transfers between devices, flip(): return lax.ppermute(values, axis, [(k, k ^ bits) for k in range(size)])  66.5 us
    ppermute x45, waiting for transfers between devices, flip(): return lax.ppermute(values, axis, [(k, k ^ bits) for k in range(size)])  44.3 us
    pallas_call x2, Pallas kernels, image_tower(): pl.pallas_call(kernel, grid_spec=pltpu.PrefetchScalarGridSpec(num_scalar_...  34.3 us
    pallas_call x1, Pallas kernels, text_backward(): pl.pallas_call(functools.partial(back_kernel, cut, len(others)), grid_spe...  20.8 us
    pallas_call x3, Pallas kernels, place(): pl.pallas_call(functools.partial(place_kernel, targets, rounds, last), in...  9.23 us
    pallas_call x1, Pallas kernels, text_second(): pl.pallas_call(functools.partial(text_second_kernel, cut), grid_spec=pltp...  7.05 us
    pallas_call x1, Pallas kernels, text_first(): pl.pallas_call(functools.partial(text_first_kernel, cut), grid_spec=pltpu...  5.92 us
  transfers between devices with their start and end apart: 45, of which 18 were waited for; matrix products, arithmetic and copies ran while one was open for 4% of the time, Pallas kernels for 27%

profile of v2, /device:TPU:1, one launch (start us, length us, event | category | flops | bytes accessed | tf_op | source)
XLA Modules:
  0.0 206.6 jit_solution(10667764386735507232)
XLA Ops:
  2.2 2.1 %collective-permute-start.2 = (bf16[50,32,384]{2,1,0:T(8,128)(2,1)S(1)}, bf16[50,32,384]{2,1,0:T(8,128)(2,1)}, u32[]{:S(2)}, u32[]{:S(2)}) collective-permute-start(bf16[50,32,384]{2,1,0:T(8,128)(2,1)S(1)} %slice.41), channel_id=1, source_target_pairs={{0,16},{16,0},{1,17},{17,1},{2,18},{18,2},{3,19},{19,3},{4,20},{20... | collective-permute-start | bytes 3686408 | tf_op jit(solution)/shard_map/ppermute | solution.py:913
  8.9 18.0 %image_block.3 = bf16[96,384]{1,0:T(8,128)(2,1)} custom-call(s32[28]{0:T(128)S(1)} %get-tuple-element.76.plan_ref.ids_ref, bf16[50,128,384]{2,1,0:T(8,128)(2,1)} %bitcast.56, bf16[384,1152]{1,0:T(8,128)(2,1)} %refs_0_.1, bf16[384,384]{1,0:T(8,128)(2,1)S(1)} %copy-done.13, bf16[384,1536]{1,0:T(8,128)(2,1)} %refs_2_.1, bf16[1536,384]{1,0:T(8,128)(2,1)} %refs_3_.1, ...), custom_call_target="tpu_custom_call" | custom-call | flops 11324620800 | bytes 7880704 | tf_op jit(solution)/shard_map/image_block/pallas_call | solution.py:247
  28.2 3.0 %collective-permute-done.2 = bf16[50,32,384]{2,1,0:T(8,128)(2,1)} collective-permute-done((bf16[50,32,384]{2,1,0:T(8,128)(2,1)S(1)}, bf16[50,32,384]{2,1,0:T(8,128)(2,1)}, u32[]{:S(2)}, u32[]{:S(2)}) %collective-permute-start.2) | collective-permute-done | bytes 1228832 | tf_op jit(solution)/shard_map/ppermute | solution.py:913
  31.2 16.3 %conditional.1 = (bf16[32,384]{1,0:T(8,128)(2,1)S(1)}) conditional(s32[]{:T(128)} %bitcast.1, () %tuple.17, (s32[28]{0:T(128)S(1)}, bf16[50,128,384]{2,1,0:T(8,128)(2,1)}, bf16[50,32,384]{2,1,0:T(8,128)(2,1)}, bf16[384,1152]{1,0:T(8,128)(2,1)}, bf16[384,384]{1,0:T(8,128)(2,1)S(1)}, /*index=5*/bf16[384,1536]{1,0:T(8,128)(2,1)}, ...), branch_computations={%region_0.0_spmd, %region_1.0_spmd} | conditional | flops 37748736 | bytes 54239 | solution.py:1056
  31.2 16.3 %image_block.2 = bf16[32,384]{1,0:T(8,128)(2,1)S(1)} custom-call(s32[28]{0:T(128)S(1)} %get-tuple-element.7.plan_ref, bf16[50,128,384]{2,1,0:T(8,128)(2,1)} %get-tuple-element.20.x_ref, bf16[50,32,384]{2,1,0:T(8,128)(2,1)} %get-tuple-element.21.recv_ref, bf16[384,1152]{1,0:T(8,128)(2,1)} %get-tuple-element.22.wqkv_ref, ...), custom_call_target="tpu_custom_call" | custom-call | flops 37748736 | bytes 54231 | tf_op jit(solution)/shard_map/cond/branch_1_fun/image_block/pallas_call | solution.py:247
  48.6 3.5 %collective-permute-start.4 = (bf16[128,384]{1,0:T(8,128)(2,1)S(1)}, bf16[128,384]{1,0:T(8,128)(2,1)S(1)}, u32[]{:S(2)}, u32[]{:S(2)}) collective-permute-start(bf16[128,384]{1,0:T(8,128)(2,1)S(1)} %pad_maximum_fusion.8), channel_id=1, source_target_pairs={{0,8},{1,9},{2,10},{3,11},{4,12},{5,13},{6,14},{7,15},{8,0},{9,1},... | collective-permute-start | bytes 294920 | tf_op jit(solution)/shard_map/ppermute | solution.py:913
  52.1 5.9 %text_attention.1 = (bf16[2048,1152]{1,0:T(8,128)(2,1)}, bf16[2048,384]{1,0:T(8,128)(2,1)S(1)}, f32[2048,384]{1,0:T(8,128)S(1)}) custom-call(s32[28]{0:T(128)S(1)} %get-tuple-element.76.plan_ref.ids_ref, bf16[128,16,384]{2,1,0:T(8,128)(2,1)S(1)} %copy-done, bf16[32,16,384]{2,1,0:T(8,128)(2,1)S(1)} %collective-permute-done.recv_ref, ...), custom_call_target="tpu_custom_call" | custom-call | flops 3019898880 | bytes 12582912 | tf_op jit(solution)/shard_map/text_attention/pallas_call | solution.py:492
  59.9 3.7 %collective-permute-start.7 = (bf16[512,384]{1,0:T(8,128)(2,1)S(1)}, bf16[512,384]{1,0:T(8,128)(2,1)S(1)}, u32[]{:S(2)}, u32[]{:S(2)}) collective-permute-start(bf16[512,384]{1,0:T(8,128)(2,1)S(1)} %constant_dynamic-update-slice_fusion.refs_2_), channel_id=1, source_target_pairs={{0,1},{1,0},{2,3},{3,2},{4,5},{5,4},{6,7},{7,6},{8,9},{9,8},{10,11... | collective-permute-start | bytes 1179656 | tf_op jit(solution)/shard_map/ppermute | solution.py:913
  63.6 7.0 %text_pool.1 = (bf16[2048,1536]{1,0:T(8,128)(2,1)S(1)}, f32[128,1536]{1,0:T(8,128)S(1)}, bf16[128,384]{1,0:T(8,128)(2,1)S(1)}, f32[128,384]{1,0:T(8,128)S(1)}, bf16[128,384]{1,0:T(8,128)(2,1)S(1)}) custom-call(s32[28]{0:T(128)S(1)} %get-tuple-element.76.plan_ref.ids_ref, f32[2048,384]{1,0:T(8,128)S(1)} %get-tuple-element.80.y1_ref, ...), custom_call_target="tpu_custom_call" | custom-call | flops 2415919104 | bytes 12582912 | tf_op jit(solution)/shard_map/text_pool/pallas_call | solution.py:569
  70.8 5.0 %collective-permute-start.6 = (bf16[128,384]{1,0:T(8,128)(2,1)S(1)}, bf16[128,384]{1,0:T(8,128)(2,1)S(1)}, u32[]{:S(2)}, u32[]{:S(2)}) collective-permute-start(bf16[128,384]{1,0:T(8,128)(2,1)S(1)} %get-tuple-element.85.refs_0_), channel_id=1, source_target_pairs={{0,16},{16,0},{1,17},{17,1},{2,18},{18,2},{3,19},{19,3},{4,20},{20... | collective-permute-start | bytes 294920 | tf_op jit(solution)/shard_map/ppermute | solution.py:913
  75.8 2.8 %collective-permute-done.6.refs_1_ = bf16[128,384]{1,0:T(8,128)(2,1)S(1)} collective-permute-done((bf16[128,384]{1,0:T(8,128)(2,1)S(1)}, bf16[128,384]{1,0:T(8,128)(2,1)S(1)}, u32[]{:S(2)}, u32[]{:S(2)}) %collective-permute-start.6) | collective-permute-done | bytes 98336 | tf_op jit(solution)/shard_map/ppermute | solution.py:913
  82.6 2.3 %collective-permute-start.11 = (f32[16,128]{1,0:T(8,128)S(1)}, f32[16,128]{1,0:T(8,128)S(1)}, u32[]{:S(2)}, u32[]{:S(2)}) collective-permute-start(f32[16,128]{1,0:T(8,128)S(1)} %add.131), channel_id=1, source_target_pairs={{0,8},{1,9},{2,10},{3,11},{4,12},{5,13},{6,14},{7,15},{8,0},{9,1},... | collective-permute-start | bytes 24584 | tf_op jit(solution)/shard_map/ppermute | solution.py:913
  86.0 3.2 %collective-permute-start.12 = (f32[16,128]{1,0:T(8,128)S(1)}, f32[16,128]{1,0:T(8,128)S(1)}, u32[]{:S(2)}, u32[]{:S(2)}) collective-permute-start(f32[16,128]{1,0:T(8,128)S(1)} %add.132), channel_id=1, source_target_pairs={{0,1},{1,0},{2,3},{3,2},{4,5},{5,4},{6,7},{7,6},{8,9},{9,8},{10,11... | collective-permute-start | bytes 24584 | tf_op jit(solution)/shard_map/ppermute | solution.py:913
  92.5 2.4 %similarity_grads.1 = (f32[128,384]{1,0:T(8,128)S(1)}, bf16[128,384]{1,0:T(8,128)(2,1)S(1)}, f32[8,128]{1,0:T(8,128)S(1)}) custom-call(s32[28]{0:T(128)S(1)} %get-tuple-element.76.plan_ref.ids_ref, f32[8,128]{1,0:T(8,128)S(1)} %copy-done.2, f32[2,128]{1,0:T(2,128)S(1)} %copy-done.3, f32[16,128]{1,0:T(8,128)S(1)} %copy-done.1, ...), custom_call_target="tpu_custom_call" | custom-call | flops 805306368 | bytes 1572864 | tf_op jit(solution)/shard_map/similarity_grads/pallas_call | solution.py:674
  96.5 2.5 %collective-permute-done.16.refs_0_ = bf16[128,384]{1,0:T(8,128)(2,1)S(1)} collective-permute-done((bf16[128,384]{1,0:T(8,128)(2,1)S(1)}, bf16[128,384]{1,0:T(8,128)(2,1)S(1)}, u32[]{:S(2)}, u32[]{:S(2)}) %collective-permute-start.16) | collective-permute-done | bytes 98336 | tf_op jit(solution)/shard_map/ppermute | solution.py:913
  99.0 20.8 %text_backward.1 = (bf16[128,16,384]{2,1,0:T(8,128)(2,1)}, bf16[1024,384]{1,0:T(8,128)(2,1)}, bf16[1024,384]{1,0:T(8,128)(2,1)}, bf16[768,384]{1,0:T(8,128)(2,1)...) custom-call(s32[28]{0:T(128)S(1)} %get-tuple-element.76.plan_ref.ids_ref, ...), custom_call_target="tpu_custom_call" | custom-call | flops 10871635968 | bytes 25165824 | tf_op jit(solution)/shard_map/text_backward/pallas_call | solution.py:880
  122.2 7.5 %collective-permute-start.22 = (bf16[32,16,384]{2,1,0:T(8,128)(2,1)S(1)}, bf16[32,16,384]{2,1,0:T(8,128)(2,1)S(1)}, u32[]{:S(2)}, u32[]{:S(2)}) collective-permute-start(bf16[32,16,384]{2,1,0:T(8,128)(2,1)S(1)} %slice.40), channel_id=1, source_target_pairs={{0,16},{16,0},{1,17},{17,1},{2,18},{18,2},{3,19},{19,3},{4,20},{20... | collective-permute-start | bytes 1179656 | tf_op jit(solution)/shard_map/ppermute | solution.py:913
  133.5 5.8 %collective-permute-done.37 = bf16[384,384]{1,0:T(8,128)(2,1)S(1)} collective-permute-done((bf16[384,384]{1,0:T(8,128)(2,1)S(1)}, bf16[384,384]{1,0:T(8,128)(2,1)S(1)}, u32[]{:S(2)}, u32[]{:S(2)}) %collective-permute-start.37) | collective-permute-done | bytes 294944 | tf_op jit(solution)/shard_map/ppermute | solution.py:913
  140.7 3.3 %collective-permute-done.38 = bf16[192,384]{1,0:T(8,128)(2,1)S(1)} collective-permute-done((bf16[192,384]{1,0:T(8,128)(2,1)S(1)}, bf16[192,384]{1,0:T(8,128)(2,1)S(1)}, u32[]{:S(2)}, u32[]{:S(2)}) %collective-permute-start.38) | collective-permute-done | bytes 147488 | tf_op jit(solution)/shard_map/ppermute | solution.py:913
  144.2 6.2 %collective-permute-done.29 = bf16[192,384]{1,0:T(8,128)(2,1)S(1)} collective-permute-done((bf16[192,384]{1,0:T(8,128)(2,1)S(1)}, bf16[192,384]{1,0:T(8,128)(2,1)S(1)}, u32[]{:S(2)}, u32[]{:S(2)}) %collective-permute-start.29) | collective-permute-done | bytes 147488 | tf_op jit(solution)/shard_map/ppermute | solution.py:913
  152.0 2.0 collective-permute-start.40
  156.0 2.7 %collective-permute-done.19 = bf16[256,384]{1,0:T(8,128)(2,1)S(1)} collective-permute-done((bf16[256,384]{1,0:T(8,128)(2,1)S(1)}, bf16[256,384]{1,0:T(8,128)(2,1)S(1)}, u32[]{:S(2)}, u32[]{:S(2)}) %collective-permute-start.19) | collective-permute-done | bytes 196640 | tf_op jit(solution)/shard_map/ppermute | solution.py:913
  158.8 1.8 collective-permute-start.20
  163.0 1.8 collective-permute-start.21
  169.1 2.9 %collective-permute-done.23 = bf16[128,384]{1,0:T(8,128)(2,1)S(1)} collective-permute-done((bf16[128,384]{1,0:T(8,128)(2,1)S(1)}, bf16[128,384]{1,0:T(8,128)(2,1)S(1)}, u32[]{:S(2)}, u32[]{:S(2)}) %collective-permute-start.23) | collective-permute-done | bytes 98336 | tf_op jit(solution)/shard_map/ppermute | solution.py:913
  175.2 1.8 collective-permute-done.24
  179.1 6.5 %collective-permute-done.25 = bf16[512,384]{1,0:T(8,128)(2,1)S(1)} collective-permute-done((bf16[512,384]{1,0:T(8,128)(2,1)S(1)}, bf16[512,384]{1,0:T(8,128)(2,1)S(1)}, u32[]{:S(2)}, u32[]{:S(2)}) %collective-permute-start.25) | collective-permute-done | bytes 393248 | tf_op jit(solution)/shard_map/ppermute | solution.py:913
  185.7 6.7 %collective-permute-start.26 = (bf16[1024,384]{1,0:T(8,128)(2,1)S(1)}, bf16[1024,384]{1,0:T(8,128)(2,1)S(1)}, u32[]{:S(2)}, u32[]{:S(2)}) collective-permute-start(bf16[1024,384]{1,0:T(8,128)(2,1)S(1)} %constant_dynamic-update-slice_fusion.4.own_ref), channel_id=1, source_target_pairs={{0,1},{1,0},{2,3},{3,2},{4,5},{5,4},{6,7},{7,6},{8,9},{9,8},{10,11... | collective-permute-start | bytes 2359304 | tf_op jit(solution)/shard_map/ppermute | solution.py:913
  195.3 1.9 select_dynamic-update-slice_fusion
  197.2 3.3 %place_gradients.5 = f32[384,1536]{1,0:T(8,128)} custom-call(s32[28]{0:T(128)S(1)} %get-tuple-element.76.plan_ref.ids_ref, bf16[768,384]{1,0:T(8,128)(2,1)S(1)} %pad_maximum_fusion.1.own_ref, bf16[768,384]{1,0:T(8,128)(2,1)} %collective-permute-done.44.other_ref), custom_call_target="tpu_custom_call" | custom-call | tf_op jit(solution)/shard_map/place_gradients/pallas_call | solution.py:1020
  200.5 2.8 %place_gradients.4 = (f32[384,384]{1,0:T(8,128)}, f32[384,1152]{1,0:T(8,128)}) custom-call(s32[28]{0:T(128)S(1)} %get-tuple-element.76.plan_ref.ids_ref, bf16[768,384]{1,0:T(8,128)(2,1)S(1)} %pad_maximum_fusion.own_ref, bf16[768,384]{1,0:T(8,128)(2,1)S(1)} %collective-permute-done.35.other_ref), custom_call_target="tpu_custom_call" | custom-call | tf_op jit(solution)/shard_map/place_gradients/pallas_call | solution.py:1020
  203.3 3.1 %place_gradients.3 = (f32[1536,384]{1,0:T(8,128)}, f32[384,384]{1,0:T(8,128)}, f32[384]{0:T(512)}, f32[384]{0:T(512)}, f32[1]{0:T(128)}, /*index=5*/f32[1]{0:T(128)}) custom-call(s32[28]{0:T(128)S(1)} %get-tuple-element.76.plan_ref.ids_ref, bf16[1024,384]{1,0:T(8,128)(2,1)S(1)} %constant_dynamic-update-slice_fusion.4.own_ref, ...), custom_call_target="tpu_custom_call" | custom-call | tf_op jit(solution)/shard_map/place_gradients/pallas_call | solution.py:1020
  (164 shorter events, 43.8 us)
Async XLA Ops:
  2.2 29.0 %collective-permute-start.2 = (bf16[50,32,384]{2,1,0:T(8,128)(2,1)S(1)}, bf16[50,32,384]{2,1,0:T(8,128)(2,1)}, u32[]{:S(2)}, u32[]{:S(2)}) collective-permute-start(bf16[50,32,384]{2,1,0:T(8,128)(2,1)S(1)} %slice.41), channel_id=1, source_target_pairs={{0,16},{16,0},{1,17},{17,1},{2,18},{18,2},{3,19},{19,3},{4,20},{20... | collective-permute-start | bytes 3686408 | tf_op jit(solution)/shard_map/ppermute | solution.py:913
  4.5 47.6 %collective-permute-start.1 = (f32[2,16]{1,0:T(2,128)S(1)}, f32[2,16]{1,0:T(2,128)S(1)}, u32[]{:S(2)}, u32[]{:S(2)}) collective-permute-start(f32[2,16]{1,0:T(2,128)S(1)} %slice.35), channel_id=1, source_target_pairs={{0,16},{16,0},{1,17},{17,1},{2,18},{18,2},{3,19},{19,3},{4,20},{20... | collective-permute-start | bytes 392 | tf_op jit(solution)/shard_map/ppermute | solution.py:913
  5.3 46.8 %collective-permute-start = (bf16[32,16,384]{2,1,0:T(8,128)(2,1)}, bf16[32,16,384]{2,1,0:T(8,128)(2,1)S(1)}, u32[]{:S(2)}, u32[]{:S(2)}) collective-permute-start(bf16[32,16,384]{2,1,0:T(8,128)(2,1)} %slice.33), channel_id=1, source_target_pairs={{0,16},{16,0},{1,17},{17,1},{2,18},{18,2},{3,19},{19,3},{4,20},{20... | collective-permute-start | bytes 1179656 | tf_op jit(solution)/shard_map/ppermute | solution.py:913
  48.5 9.6 %collective-permute-start.3 = (bf16[128,384]{1,0:T(8,128)(2,1)S(1)}, bf16[128,384]{1,0:T(8,128)(2,1)S(1)}, u32[]{:S(2)}, u32[]{:S(2)}) collective-permute-start(bf16[128,384]{1,0:T(8,128)(2,1)S(1)} %pad_maximum_fusion.8), channel_id=1, source_target_pairs={{0,4},{1,5},{2,6},{3,7},{4,0},{5,1},{6,2},{7,3},{8,12},{9,13},{10,... | collective-permute-start | bytes 294920 | tf_op jit(solution)/shard_map/ppermute | solution.py:913
  48.6 9.5 %collective-permute-start.4 = (bf16[128,384]{1,0:T(8,128)(2,1)S(1)}, bf16[128,384]{1,0:T(8,128)(2,1)S(1)}, u32[]{:S(2)}, u32[]{:S(2)}) collective-permute-start(bf16[128,384]{1,0:T(8,128)(2,1)S(1)} %pad_maximum_fusion.8), channel_id=1, source_target_pairs={{0,8},{1,9},{2,10},{3,11},{4,12},{5,13},{6,14},{7,15},{8,0},{9,1},... | collective-permute-start | bytes 294920 | tf_op jit(solution)/shard_map/ppermute | solution.py:913
  52.1 6.4 %collective-permute-start.5 = (bf16[128,384]{1,0:T(8,128)(2,1)S(1)}, bf16[128,384]{1,0:T(8,128)(2,1)S(1)}, u32[]{:S(2)}, u32[]{:S(2)}) collective-permute-start(bf16[128,384]{1,0:T(8,128)(2,1)S(1)} %pad_maximum_fusion.8), channel_id=1, source_target_pairs={{0,12},{1,13},{2,14},{3,15},{4,8},{5,9},{6,10},{7,11},{8,4},{9,5},... | collective-permute-start | bytes 294920 | tf_op jit(solution)/shard_map/ppermute | solution.py:913
  58.6 12.1 %collective-permute-start.8 = (bf16[512,384]{1,0:T(8,128)(2,1)S(1)}, bf16[512,384]{1,0:T(8,128)(2,1)S(1)}, u32[]{:S(2)}, u32[]{:S(2)}) collective-permute-start(bf16[512,384]{1,0:T(8,128)(2,1)S(1)} %constant_dynamic-update-slice_fusion.refs_2_), channel_id=1, source_target_pairs={{0,2},{1,3},{2,0},{3,1},{4,6},{5,7},{6,4},{7,5},{8,10},{9,11},{10,... | collective-permute-start | bytes 1179656 | tf_op jit(solution)/shard_map/ppermute | solution.py:913
  59.9 18.7 %collective-permute-start.7 = (bf16[512,384]{1,0:T(8,128)(2,1)S(1)}, bf16[512,384]{1,0:T(8,128)(2,1)S(1)}, u32[]{:S(2)}, u32[]{:S(2)}) collective-permute-start(bf16[512,384]{1,0:T(8,128)(2,1)S(1)} %constant_dynamic-update-slice_fusion.refs_2_), channel_id=1, source_target_pairs={{0,1},{1,0},{2,3},{3,2},{4,5},{5,4},{6,7},{7,6},{8,9},{9,8},{10,11... | collective-permute-start | bytes 1179656 | tf_op jit(solution)/shard_map/ppermute | solution.py:913
  70.7 7.9 %collective-permute-start.9 = (bf16[512,384]{1,0:T(8,128)(2,1)S(1)}, bf16[512,384]{1,0:T(8,128)(2,1)S(1)}, u32[]{:S(2)}, u32[]{:S(2)}) collective-permute-start(bf16[512,384]{1,0:T(8,128)(2,1)S(1)} %collective-permute-done.8.refs_4_), channel_id=1, source_target_pairs={{0,1},{1,0},{2,3},{3,2},{4,5},{5,4},{6,7},{7,6},{8,9},{9,8},{10,11... | collective-permute-start | bytes 1179656 | tf_op jit(solution)/shard_map/ppermute | solution.py:913
  70.8 7.8 %collective-permute-start.6 = (bf16[128,384]{1,0:T(8,128)(2,1)S(1)}, bf16[128,384]{1,0:T(8,128)(2,1)S(1)}, u32[]{:S(2)}, u32[]{:S(2)}) collective-permute-start(bf16[128,384]{1,0:T(8,128)(2,1)S(1)} %get-tuple-element.85.refs_0_), channel_id=1, source_target_pairs={{0,16},{16,0},{1,17},{17,1},{2,18},{18,2},{3,19},{19,3},{4,20},{20... | collective-permute-start | bytes 294920 | tf_op jit(solution)/shard_map/ppermute | solution.py:913
  86.0 4.9 %collective-permute-start.12 = (f32[16,128]{1,0:T(8,128)S(1)}, f32[16,128]{1,0:T(8,128)S(1)}, u32[]{:S(2)}, u32[]{:S(2)}) collective-permute-start(f32[16,128]{1,0:T(8,128)S(1)} %add.132), channel_id=1, source_target_pairs={{0,1},{1,0},{2,3},{3,2},{4,5},{5,4},{6,7},{7,6},{8,9},{9,8},{10,11... | collective-permute-start | bytes 24584 | tf_op jit(solution)/shard_map/ppermute | solution.py:913
  119.8 10.6 %collective-permute-start.36 = (bf16[768,384]{1,0:T(8,128)(2,1)}, bf16[768,384]{1,0:T(8,128)(2,1)S(1)}, u32[]{:S(2)}, u32[]{:S(2)}) collective-permute-start(bf16[768,384]{1,0:T(8,128)(2,1)} %get-tuple-element.111), channel_id=1, source_target_pairs={{0,1},{1,0},{2,3},{3,2},{4,5},{5,4},{6,7},{7,6},{8,9},{9,8},{10,11... | collective-permute-start | bytes 1769480 | tf_op jit(solution)/shard_map/ppermute | solution.py:913
  121.1 10.8 %collective-permute-start.27 = (bf16[768,384]{1,0:T(8,128)(2,1)}, bf16[768,384]{1,0:T(8,128)(2,1)S(1)}, u32[]{:S(2)}, u32[]{:S(2)}) collective-permute-start(bf16[768,384]{1,0:T(8,128)(2,1)} %get-tuple-element.106), channel_id=1, source_target_pairs={{0,1},{1,0},{2,3},{3,2},{4,5},{5,4},{6,7},{7,6},{8,9},{9,8},{10,11... | collective-permute-start | bytes 1769480 | tf_op jit(solution)/shard_map/ppermute | solution.py:913
  122.2 45.2 %collective-permute-start.22 = (bf16[32,16,384]{2,1,0:T(8,128)(2,1)S(1)}, bf16[32,16,384]{2,1,0:T(8,128)(2,1)S(1)}, u32[]{:S(2)}, u32[]{:S(2)}) collective-permute-start(bf16[32,16,384]{2,1,0:T(8,128)(2,1)S(1)} %slice.40), channel_id=1, source_target_pairs={{0,16},{16,0},{1,17},{17,1},{2,18},{18,2},{3,19},{19,3},{4,20},{20... | collective-permute-start | bytes 1179656 | tf_op jit(solution)/shard_map/ppermute | solution.py:913
  130.6 8.7 %collective-permute-start.37 = (bf16[384,384]{1,0:T(8,128)(2,1)S(1)}, bf16[384,384]{1,0:T(8,128)(2,1)S(1)}, u32[]{:S(2)}, u32[]{:S(2)}) collective-permute-start(bf16[384,384]{1,0:T(8,128)(2,1)S(1)} %fusion.2), channel_id=1, source_target_pairs={{0,2},{1,3},{2,0},{3,1},{4,6},{5,7},{6,4},{7,5},{8,10},{9,11},{10,... | collective-permute-start | bytes 884744 | tf_op jit(solution)/shard_map/ppermute | solution.py:913
  132.1 8.4 %collective-permute-start.28 = (bf16[384,384]{1,0:T(8,128)(2,1)S(1)}, bf16[384,384]{1,0:T(8,128)(2,1)S(1)}, u32[]{:S(2)}, u32[]{:S(2)}) collective-permute-start(bf16[384,384]{1,0:T(8,128)(2,1)S(1)} %fusion.1), channel_id=1, source_target_pairs={{0,4},{1,5},{2,6},{3,7},{4,0},{5,1},{6,2},{7,3},{8,12},{9,13},{10,... | collective-permute-start | bytes 884744 | tf_op jit(solution)/shard_map/ppermute | solution.py:913
  133.4 20.6 %collective-permute-start.18 = (bf16[512,384]{1,0:T(8,128)(2,1)S(1)}, bf16[512,384]{1,0:T(8,128)(2,1)S(1)}, u32[]{:S(2)}, u32[]{:S(2)}) collective-permute-start(bf16[512,384]{1,0:T(8,128)(2,1)S(1)} %fusion), channel_id=1, source_target_pairs={{0,16},{16,0},{1,17},{17,1},{2,18},{18,2},{3,19},{19,3},{4,20},{20... | collective-permute-start | bytes 1179656 | tf_op jit(solution)/shard_map/ppermute | solution.py:913
  140.6 9.8 %collective-permute-start.29 = (bf16[192,384]{1,0:T(8,128)(2,1)S(1)}, bf16[192,384]{1,0:T(8,128)(2,1)S(1)}, u32[]{:S(2)}, u32[]{:S(2)}) collective-permute-start(bf16[192,384]{1,0:T(8,128)(2,1)S(1)} %fusion.5), channel_id=1, source_target_pairs={{0,16},{16,0},{1,17},{17,1},{2,18},{18,2},{3,19},{19,3},{4,20},{20... | collective-permute-start | bytes 442376 | tf_op jit(solution)/shard_map/ppermute | solution.py:913
  144.1 7.9 %collective-permute-start.39 = (bf16[96,384]{1,0:T(8,128)(2,1)S(1)}, bf16[96,384]{1,0:T(8,128)(2,1)S(1)}, u32[]{:S(2)}, u32[]{:S(2)}) collective-permute-start(bf16[96,384]{1,0:T(8,128)(2,1)S(1)} %fusion.11), channel_id=1, source_target_pairs={{0,16},{16,0},{1,17},{17,1},{2,18},{18,2},{3,19},{19,3},{4,20},{20... | collective-permute-start | bytes 221192 | tf_op jit(solution)/shard_map/ppermute | solution.py:913
  150.5 5.0 %collective-permute-start.30 = (bf16[96,384]{1,0:T(8,128)(2,1)S(1)}, bf16[96,384]{1,0:T(8,128)(2,1)S(1)}, u32[]{:S(2)}, u32[]{:S(2)}) collective-permute-start(bf16[96,384]{1,0:T(8,128)(2,1)S(1)} %fusion.10), channel_id=1, source_target_pairs={{0,2},{1,3},{2,0},{3,1},{4,6},{5,7},{6,4},{7,5},{8,10},{9,11},{10,... | collective-permute-start | bytes 221192 | tf_op jit(solution)/shard_map/ppermute | solution.py:913
  152.0 8.6 %collective-permute-start.40 = (bf16[96,384]{1,0:T(8,128)(2,1)S(1)}, bf16[96,384]{1,0:T(8,128)(2,1)S(1)}, u32[]{:S(2)}, u32[]{:S(2)}) collective-permute-start(bf16[96,384]{1,0:T(8,128)(2,1)S(1)} %fusion.7), channel_id=1, source_target_pairs={{0,8},{1,9},{2,10},{3,11},{4,12},{5,13},{6,14},{7,15},{8,0},{9,1},... | collective-permute-start | bytes 221192 | tf_op jit(solution)/shard_map/ppermute | solution.py:913
  155.5 9.3 %collective-permute-start.31 = (bf16[96,384]{1,0:T(8,128)(2,1)S(1)}, bf16[96,384]{1,0:T(8,128)(2,1)S(1)}, u32[]{:S(2)}, u32[]{:S(2)}) collective-permute-start(bf16[96,384]{1,0:T(8,128)(2,1)S(1)} %fusion.8), channel_id=1, source_target_pairs={{0,8},{1,9},{2,10},{3,11},{4,12},{5,13},{6,14},{7,15},{8,0},{9,1},... | collective-permute-start | bytes 221192 | tf_op jit(solution)/shard_map/ppermute | solution.py:913
  160.6 8.4 %collective-permute-start.41 = (bf16[96,384]{1,0:T(8,128)(2,1)S(1)}, bf16[96,384]{1,0:T(8,128)(2,1)S(1)}, u32[]{:S(2)}, u32[]{:S(2)}) collective-permute-start(bf16[96,384]{1,0:T(8,128)(2,1)S(1)} %add_convert_fusion.1), channel_id=1, source_target_pairs={{0,16},{16,0},{1,17},{17,1},{2,18},{18,2},{3,19},{19,3},{4,20},{20... | collective-permute-start | bytes 221192 | tf_op jit(solution)/shard_map/ppermute | solution.py:913
  164.8 8.8 %collective-permute-start.32 = (bf16[96,384]{1,0:T(8,128)(2,1)S(1)}, bf16[96,384]{1,0:T(8,128)(2,1)S(1)}, u32[]{:S(2)}, u32[]{:S(2)}) collective-permute-start(bf16[96,384]{1,0:T(8,128)(2,1)S(1)} %add_convert_fusion.2), channel_id=1, source_target_pairs={{0,2},{1,3},{2,0},{3,1},{4,6},{5,7},{6,4},{7,5},{8,10},{9,11},{10,... | collective-permute-start | bytes 221192 | tf_op jit(solution)/shard_map/ppermute | solution.py:913
  169.0 5.7 %collective-permute-start.42 = (bf16[192,384]{1,0:T(8,128)(2,1)S(1)}, bf16[192,384]{1,0:T(8,128)(2,1)S(1)}, u32[]{:S(2)}, u32[]{:S(2)}) collective-permute-start(bf16[192,384]{1,0:T(8,128)(2,1)S(1)} %pad_maximum_fusion.7), channel_id=1, source_target_pairs={{0,4},{1,5},{2,6},{3,7},{4,0},{5,1},{6,2},{7,3},{8,12},{9,13},{10,... | collective-permute-start | bytes 442376 | tf_op jit(solution)/shard_map/ppermute | solution.py:913
  172.1 4.9 %collective-permute-start.24 = (bf16[256,384]{1,0:T(8,128)(2,1)S(1)}, bf16[256,384]{1,0:T(8,128)(2,1)S(1)}, u32[]{:S(2)}, u32[]{:S(2)}) collective-permute-start(bf16[256,384]{1,0:T(8,128)(2,1)S(1)} %pad_maximum_fusion.5), channel_id=1, source_target_pairs={{0,2},{1,3},{2,0},{3,1},{4,6},{5,7},{6,4},{7,5},{8,10},{9,11},{10,... | collective-permute-start | bytes 589832 | tf_op jit(solution)/shard_map/ppermute | solution.py:913
  174.7 17.6 %collective-permute-start.43 = (bf16[384,384]{1,0:T(8,128)(2,1)S(1)}, bf16[384,384]{1,0:T(8,128)(2,1)S(1)}, u32[]{:S(2)}, u32[]{:S(2)}) collective-permute-start(bf16[384,384]{1,0:T(8,128)(2,1)S(1)} %pad_maximum_fusion.4), channel_id=1, source_target_pairs={{0,2},{1,3},{2,0},{3,1},{4,6},{5,7},{6,4},{7,5},{8,10},{9,11},{10,... | collective-permute-start | bytes 884744 | tf_op jit(solution)/shard_map/ppermute | solution.py:913
  177.0 8.6 %collective-permute-start.25 = (bf16[512,384]{1,0:T(8,128)(2,1)S(1)}, bf16[512,384]{1,0:T(8,128)(2,1)S(1)}, u32[]{:S(2)}, u32[]{:S(2)}) collective-permute-start(bf16[512,384]{1,0:T(8,128)(2,1)S(1)} %pad_maximum_fusion.2), channel_id=1, source_target_pairs={{0,16},{16,0},{1,17},{17,1},{2,18},{18,2},{3,19},{19,3},{4,20},{20... | collective-permute-start | bytes 1179656 | tf_op jit(solution)/shard_map/ppermute | solution.py:913
  177.8 14.7 %collective-permute-start.34 = (bf16[384,384]{1,0:T(8,128)(2,1)S(1)}, bf16[384,384]{1,0:T(8,128)(2,1)S(1)}, u32[]{:S(2)}, u32[]{:S(2)}) collective-permute-start(bf16[384,384]{1,0:T(8,128)(2,1)S(1)} %pad_maximum_fusion.3), channel_id=1, source_target_pairs={{0,4},{1,5},{2,6},{3,7},{4,0},{5,1},{6,2},{7,3},{8,12},{9,13},{10,... | collective-permute-start | bytes 884744 | tf_op jit(solution)/shard_map/ppermute | solution.py:913
  185.7 17.6 %collective-permute-start.26 = (bf16[1024,384]{1,0:T(8,128)(2,1)S(1)}, bf16[1024,384]{1,0:T(8,128)(2,1)S(1)}, u32[]{:S(2)}, u32[]{:S(2)}) collective-permute-start(bf16[1024,384]{1,0:T(8,128)(2,1)S(1)} %constant_dynamic-update-slice_fusion.4.own_ref), channel_id=1, source_target_pairs={{0,1},{1,0},{2,3},{3,2},{4,5},{5,4},{6,7},{7,6},{8,9},{9,8},{10,11... | collective-permute-start | bytes 2359304 | tf_op jit(solution)/shard_map/ppermute | solution.py:913
  192.4 4.8 %collective-permute-start.44 = (bf16[768,384]{1,0:T(8,128)(2,1)S(1)}, bf16[768,384]{1,0:T(8,128)(2,1)}, u32[]{:S(2)}, u32[]{:S(2)}) collective-permute-start(bf16[768,384]{1,0:T(8,128)(2,1)S(1)} %pad_maximum_fusion.1.own_ref), channel_id=1, source_target_pairs={{0,1},{1,0},{2,3},{3,2},{4,5},{5,4},{6,7},{7,6},{8,9},{9,8},{10,11... | collective-permute-start | bytes 1769480 | tf_op jit(solution)/shard_map/ppermute | solution.py:913
  192.6 7.9 %collective-permute-start.35 = (bf16[768,384]{1,0:T(8,128)(2,1)S(1)}, bf16[768,384]{1,0:T(8,128)(2,1)S(1)}, u32[]{:S(2)}, u32[]{:S(2)}) collective-permute-start(bf16[768,384]{1,0:T(8,128)(2,1)S(1)} %pad_maximum_fusion.own_ref), channel_id=1, source_target_pairs={{0,1},{1,0},{2,3},{3,2},{4,5},{5,4},{6,7},{7,6},{8,9},{9,8},{10,11... | collective-permute-start | bytes 1769480 | tf_op jit(solution)/shard_map/ppermute | solution.py:913
  (31 other events, 270.8 us)

commit v3 on v2

--- a/solution.py
+++ b/solution.py
@@ -171,7 +171,7 @@
 
     largest = jnp.zeros((slots, 2 * slots), F32)
     units = [(p, h) for p in range(GROUP) for h in range(tiles)]
-    ahead = 3
+    ahead = 4
     feed = iter(())
     projected(0)
     for g in range(groups):
@@ -295,14 +295,6 @@
                 kept[at][u] = made
 
 
-def group_loop(stages, rows, width):
-    @pl.loop(0, rows // 256)
-    def _(half):
-        first = half * 2
-        units = [(first + g, h) for g in range(2) for h in range(0, width, 128)]
-        staggered(stages, units, 1)
-
-
 def same_pair(length):
     row = lax.broadcasted_iota(jnp.int32, (128, 128), 0) // length
     lane = lax.broadcasted_iota(jnp.int32, (128, 128), 1) // length
@@ -479,7 +471,7 @@
         o = mm(e, jnp.concatenate([vbd, ones], axis=1))
         att_ref[g : g + 128, h : h + 128] = over(o[:, :128], o[:, 128:]).astype(BF16)
 
-    staggered([scores, expo, weighted], [(g, h) for g in range(0, rows, 128) for h in range(0, width, 128)], 1)
+    staggered([scores, expo, weighted], [(g, h) for g in range(0, rows, 128) for h in range(0, width, 128)], 2)
     y1_ref[...] = x + mm(att_ref[...], wout_ref[...])
 
 
@@ -863,7 +855,7 @@
         kbd = jnp.concatenate([k * low, k * high], axis=0)
         dmix[pl.ds(g * 128, 128), h : h + 128] = (mm(ds, kbd) * HEAD**-0.5).astype(BF16)
 
-    group_loop([scores, soft, products, query], rows, width)
+    staggered([scores, soft, products, query], [(g, h) for g in range(rows // 128) for h in range(0, width, 128)], 2)
 
 
 def text_backward(

time: 207 us -> 204 us (0.986)
  no operation moved by 1% of the time
where the time goes in v3:
time: 204 us; the launch traced here: 203 us
  Pallas kernels  80.6 us (40%)
  starting transfers between devices  64.7 us (32%)
  waiting for transfers between devices  44.7 us (22%)
  local copies, waits for them, and re-layouts  5.36 us (3%)
  between operations  3.97 us (2%)
  other arithmetic  3.85 us (2%)
    ppermute x45, starting transfers between devices, flip(): return lax.ppermute(values, axis, [(k, k ^ bits) for k in range(size)])  64.7 us
    ppermute x45, waiting for transfers between devices, flip(): return lax.ppermute(values, axis, [(k, k ^ bits) for k in range(size)])  44.7 us
    pallas_call x2, Pallas kernels, image_tower(): pl.pallas_call(kernel, grid_spec=pltpu.PrefetchScalarGridSpec(num_scalar_...  34.2 us
    pallas_call x1, Pallas kernels, text_backward(): pl.pallas_call(functools.partial(back_kernel, cut, len(others)), grid_spe...  19 us
    pallas_call x3, Pallas kernels, place(): pl.pallas_call(functools.partial(place_kernel, targets, rounds, last), in...  9.23 us
    pallas_call x1, Pallas kernels, text_second(): pl.pallas_call(functools.partial(text_second_kernel, cut), grid_spec=pltp...  7.05 us
    pallas_call x1, Pallas kernels, text_first(): pl.pallas_call(functools.partial(text_first_kernel, cut), grid_spec=pltpu...  5.92 us
  transfers between devices with their start and end apart: 45, of which 18 were waited for; matrix products, arithmetic and copies ran while one was open for 4% of the time, Pallas kernels for 27%

profile of v3, /device:TPU:1, one launch (start us, length us, event | category | flops | bytes accessed | tf_op | source)
XLA Modules:
  0.0 203.2 jit_solution(18062489205167441499)
XLA Ops:
  2.2 2.1 %collective-permute-start.2 = (bf16[50,32,384]{2,1,0:T(8,128)(2,1)S(1)}, bf16[50,32,384]{2,1,0:T(8,128)(2,1)}, u32[]{:S(2)}, u32[]{:S(2)}) collective-permute-start(bf16[50,32,384]{2,1,0:T(8,128)(2,1)S(1)} %slice.41), channel_id=1, source_target_pairs={{0,16},{16,0},{1,17},{17,1},{2,18},{18,2},{3,19},{19,3},{4,20},{20... | collective-permute-start | bytes 3686408 | tf_op jit(solution)/shard_map/ppermute | solution.py:905
  8.9 17.8 %image_block.3 = bf16[96,384]{1,0:T(8,128)(2,1)} custom-call(s32[28]{0:T(128)S(1)} %get-tuple-element.76.plan_ref.ids_ref, bf16[50,128,384]{2,1,0:T(8,128)(2,1)} %bitcast.56, bf16[384,1152]{1,0:T(8,128)(2,1)} %refs_0_.1, bf16[384,384]{1,0:T(8,128)(2,1)S(1)} %copy-done.13, bf16[384,1536]{1,0:T(8,128)(2,1)} %refs_2_.1, bf16[1536,384]{1,0:T(8,128)(2,1)} %refs_3_.1, ...), custom_call_target="tpu_custom_call" | custom-call | flops 11324620800 | bytes 7880704 | tf_op jit(solution)/shard_map/image_block/pallas_call | solution.py:247
  28.0 3.2 %collective-permute-done.2 = bf16[50,32,384]{2,1,0:T(8,128)(2,1)} collective-permute-done((bf16[50,32,384]{2,1,0:T(8,128)(2,1)S(1)}, bf16[50,32,384]{2,1,0:T(8,128)(2,1)}, u32[]{:S(2)}, u32[]{:S(2)}) %collective-permute-start.2) | collective-permute-done | bytes 1228832 | tf_op jit(solution)/shard_map/ppermute | solution.py:905
  31.2 16.4 %conditional.1 = (bf16[32,384]{1,0:T(8,128)(2,1)S(1)}) conditional(s32[]{:T(128)} %bitcast.1, () %tuple.17, (s32[28]{0:T(128)S(1)}, bf16[50,128,384]{2,1,0:T(8,128)(2,1)}, bf16[50,32,384]{2,1,0:T(8,128)(2,1)}, bf16[384,1152]{1,0:T(8,128)(2,1)}, bf16[384,384]{1,0:T(8,128)(2,1)S(1)}, /*index=5*/bf16[384,1536]{1,0:T(8,128)(2,1)}, ...), branch_computations={%region_0.0_spmd, %region_1.0_spmd} | conditional | flops 37748736 | bytes 54239 | solution.py:1048
  31.2 16.4 %image_block.2 = bf16[32,384]{1,0:T(8,128)(2,1)S(1)} custom-call(s32[28]{0:T(128)S(1)} %get-tuple-element.7.plan_ref, bf16[50,128,384]{2,1,0:T(8,128)(2,1)} %get-tuple-element.20.x_ref, bf16[50,32,384]{2,1,0:T(8,128)(2,1)} %get-tuple-element.21.recv_ref, bf16[384,1152]{1,0:T(8,128)(2,1)} %get-tuple-element.22.wqkv_ref, ...), custom_call_target="tpu_custom_call" | custom-call | flops 37748736 | bytes 54231 | tf_op jit(solution)/shard_map/cond/branch_1_fun/image_block/pallas_call | solution.py:247
  49.8 2.3 %collective-permute-start.4 = (bf16[128,384]{1,0:T(8,128)(2,1)S(1)}, bf16[128,384]{1,0:T(8,128)(2,1)S(1)}, u32[]{:S(2)}, u32[]{:S(2)}) collective-permute-start(bf16[128,384]{1,0:T(8,128)(2,1)S(1)} %pad_maximum_fusion.8), channel_id=1, source_target_pairs={{0,8},{1,9},{2,10},{3,11},{4,12},{5,13},{6,14},{7,15},{8,0},{9,1},... | collective-permute-start | bytes 294920 | tf_op jit(solution)/shard_map/ppermute | solution.py:905
  52.2 5.9 %text_attention.1 = (bf16[2048,1152]{1,0:T(8,128)(2,1)}, bf16[2048,384]{1,0:T(8,128)(2,1)S(1)}, f32[2048,384]{1,0:T(8,128)S(1)}) custom-call(s32[28]{0:T(128)S(1)} %get-tuple-element.76.plan_ref.ids_ref, bf16[128,16,384]{2,1,0:T(8,128)(2,1)S(1)} %copy-done, bf16[32,16,384]{2,1,0:T(8,128)(2,1)S(1)} %collective-permute-done.recv_ref, ...), custom_call_target="tpu_custom_call" | custom-call | flops 3019898880 | bytes 12582912 | tf_op jit(solution)/shard_map/text_attention/pallas_call | solution.py:484
  60.0 3.7 %collective-permute-start.7 = (bf16[512,384]{1,0:T(8,128)(2,1)S(1)}, bf16[512,384]{1,0:T(8,128)(2,1)S(1)}, u32[]{:S(2)}, u32[]{:S(2)}) collective-permute-start(bf16[512,384]{1,0:T(8,128)(2,1)S(1)} %constant_dynamic-update-slice_fusion.refs_2_), channel_id=1, source_target_pairs={{0,1},{1,0},{2,3},{3,2},{4,5},{5,4},{6,7},{7,6},{8,9},{9,8},{10,11... | collective-permute-start | bytes 1179656 | tf_op jit(solution)/shard_map/ppermute | solution.py:905
  63.7 7.0 %text_pool.1 = (bf16[2048,1536]{1,0:T(8,128)(2,1)S(1)}, f32[128,1536]{1,0:T(8,128)S(1)}, bf16[128,384]{1,0:T(8,128)(2,1)S(1)}, f32[128,384]{1,0:T(8,128)S(1)}, bf16[128,384]{1,0:T(8,128)(2,1)S(1)}) custom-call(s32[28]{0:T(128)S(1)} %get-tuple-element.76.plan_ref.ids_ref, f32[2048,384]{1,0:T(8,128)S(1)} %get-tuple-element.80.y1_ref, ...), custom_call_target="tpu_custom_call" | custom-call | flops 2415919104 | bytes 12582912 | tf_op jit(solution)/shard_map/text_pool/pallas_call | solution.py:561
  70.9 4.4 %collective-permute-start.6 = (bf16[128,384]{1,0:T(8,128)(2,1)S(1)}, bf16[128,384]{1,0:T(8,128)(2,1)S(1)}, u32[]{:S(2)}, u32[]{:S(2)}) collective-permute-start(bf16[128,384]{1,0:T(8,128)(2,1)S(1)} %get-tuple-element.85.refs_0_), channel_id=1, source_target_pairs={{0,16},{16,0},{1,17},{17,1},{2,18},{18,2},{3,19},{19,3},{4,20},{20... | collective-permute-start | bytes 294920 | tf_op jit(solution)/shard_map/ppermute | solution.py:905
  75.2 2.8 %collective-permute-done.6.refs_1_ = bf16[128,384]{1,0:T(8,128)(2,1)S(1)} collective-permute-done((bf16[128,384]{1,0:T(8,128)(2,1)S(1)}, bf16[128,384]{1,0:T(8,128)(2,1)S(1)}, u32[]{:S(2)}, u32[]{:S(2)}) %collective-permute-start.6) | collective-permute-done | bytes 98336 | tf_op jit(solution)/shard_map/ppermute | solution.py:905
  82.1 2.2 %collective-permute-start.11 = (f32[16,128]{1,0:T(8,128)S(1)}, f32[16,128]{1,0:T(8,128)S(1)}, u32[]{:S(2)}, u32[]{:S(2)}) collective-permute-start(f32[16,128]{1,0:T(8,128)S(1)} %add.131), channel_id=1, source_target_pairs={{0,8},{1,9},{2,10},{3,11},{4,12},{5,13},{6,14},{7,15},{8,0},{9,1},... | collective-permute-start | bytes 24584 | tf_op jit(solution)/shard_map/ppermute | solution.py:905
  85.5 3.2 %collective-permute-start.12 = (f32[16,128]{1,0:T(8,128)S(1)}, f32[16,128]{1,0:T(8,128)S(1)}, u32[]{:S(2)}, u32[]{:S(2)}) collective-permute-start(f32[16,128]{1,0:T(8,128)S(1)} %add.132), channel_id=1, source_target_pairs={{0,1},{1,0},{2,3},{3,2},{4,5},{5,4},{6,7},{7,6},{8,9},{9,8},{10,11... | collective-permute-start | bytes 24584 | tf_op jit(solution)/shard_map/ppermute | solution.py:905
  88.8 1.6 collective-permute-start.14
  92.0 2.4 %similarity_grads.1 = (f32[128,384]{1,0:T(8,128)S(1)}, bf16[128,384]{1,0:T(8,128)(2,1)S(1)}, f32[8,128]{1,0:T(8,128)S(1)}) custom-call(s32[28]{0:T(128)S(1)} %get-tuple-element.76.plan_ref.ids_ref, f32[8,128]{1,0:T(8,128)S(1)} %copy-done.2, f32[2,128]{1,0:T(2,128)S(1)} %copy-done.3, f32[16,128]{1,0:T(8,128)S(1)} %copy-done.1, ...), custom_call_target="tpu_custom_call" | custom-call | flops 805306368 | bytes 1572864 | tf_op jit(solution)/shard_map/similarity_grads/pallas_call | solution.py:666
  95.9 2.5 %collective-permute-done.16.refs_0_ = bf16[128,384]{1,0:T(8,128)(2,1)S(1)} collective-permute-done((bf16[128,384]{1,0:T(8,128)(2,1)S(1)}, bf16[128,384]{1,0:T(8,128)(2,1)S(1)}, u32[]{:S(2)}, u32[]{:S(2)}) %collective-permute-start.16) | collective-permute-done | bytes 98336 | tf_op jit(solution)/shard_map/ppermute | solution.py:905
  98.5 19.0 %text_backward.1 = (bf16[128,16,384]{2,1,0:T(8,128)(2,1)}, bf16[1024,384]{1,0:T(8,128)(2,1)}, bf16[1024,384]{1,0:T(8,128)(2,1)}, bf16[768,384]{1,0:T(8,128)(2,1)...) custom-call(s32[28]{0:T(128)S(1)} %get-tuple-element.76.plan_ref.ids_ref, ...), custom_call_target="tpu_custom_call" | custom-call | flops 10871635968 | bytes 25165824 | tf_op jit(solution)/shard_map/text_backward/pallas_call | solution.py:872
  119.9 6.6 %collective-permute-start.22 = (bf16[32,16,384]{2,1,0:T(8,128)(2,1)S(1)}, bf16[32,16,384]{2,1,0:T(8,128)(2,1)S(1)}, u32[]{:S(2)}, u32[]{:S(2)}) collective-permute-start(bf16[32,16,384]{2,1,0:T(8,128)(2,1)S(1)} %slice.40), channel_id=1, source_target_pairs={{0,16},{16,0},{1,17},{17,1},{2,18},{18,2},{3,19},{19,3},{4,20},{20... | collective-permute-start | bytes 1179656 | tf_op jit(solution)/shard_map/ppermute | solution.py:905
  130.2 5.8 %collective-permute-done.37 = bf16[384,384]{1,0:T(8,128)(2,1)S(1)} collective-permute-done((bf16[384,384]{1,0:T(8,128)(2,1)S(1)}, bf16[384,384]{1,0:T(8,128)(2,1)S(1)}, u32[]{:S(2)}, u32[]{:S(2)}) %collective-permute-start.37) | collective-permute-done | bytes 294944 | tf_op jit(solution)/shard_map/ppermute | solution.py:905
  137.4 3.3 %collective-permute-done.38 = bf16[192,384]{1,0:T(8,128)(2,1)S(1)} collective-permute-done((bf16[192,384]{1,0:T(8,128)(2,1)S(1)}, bf16[192,384]{1,0:T(8,128)(2,1)S(1)}, u32[]{:S(2)}, u32[]{:S(2)}) %collective-permute-start.38) | collective-permute-done | bytes 147488 | tf_op jit(solution)/shard_map/ppermute | solution.py:905
  140.9 6.2 %collective-permute-done.29 = bf16[192,384]{1,0:T(8,128)(2,1)S(1)} collective-permute-done((bf16[192,384]{1,0:T(8,128)(2,1)S(1)}, bf16[192,384]{1,0:T(8,128)(2,1)S(1)}, u32[]{:S(2)}, u32[]{:S(2)}) %collective-permute-start.29) | collective-permute-done | bytes 147488 | tf_op jit(solution)/shard_map/ppermute | solution.py:905
  148.7 2.0 collective-permute-start.40
  152.7 3.0 %collective-permute-done.19 = bf16[256,384]{1,0:T(8,128)(2,1)S(1)} collective-permute-done((bf16[256,384]{1,0:T(8,128)(2,1)S(1)}, bf16[256,384]{1,0:T(8,128)(2,1)S(1)}, u32[]{:S(2)}, u32[]{:S(2)}) %collective-permute-start.19) | collective-permute-done | bytes 196640 | tf_op jit(solution)/shard_map/ppermute | solution.py:905
  159.6 1.9 collective-permute-start.21
  165.8 2.9 %collective-permute-done.23 = bf16[128,384]{1,0:T(8,128)(2,1)S(1)} collective-permute-done((bf16[128,384]{1,0:T(8,128)(2,1)S(1)}, bf16[128,384]{1,0:T(8,128)(2,1)S(1)}, u32[]{:S(2)}, u32[]{:S(2)}) %collective-permute-start.23) | collective-permute-done | bytes 98336 | tf_op jit(solution)/shard_map/ppermute | solution.py:905
  172.1 1.6 collective-permute-done.24
  175.8 6.5 %collective-permute-done.25 = bf16[512,384]{1,0:T(8,128)(2,1)S(1)} collective-permute-done((bf16[512,384]{1,0:T(8,128)(2,1)S(1)}, bf16[512,384]{1,0:T(8,128)(2,1)S(1)}, u32[]{:S(2)}, u32[]{:S(2)}) %collective-permute-start.25) | collective-permute-done | bytes 393248 | tf_op jit(solution)/shard_map/ppermute | solution.py:905
  182.4 6.5 %collective-permute-start.26 = (bf16[1024,384]{1,0:T(8,128)(2,1)S(1)}, bf16[1024,384]{1,0:T(8,128)(2,1)S(1)}, u32[]{:S(2)}, u32[]{:S(2)}) collective-permute-start(bf16[1024,384]{1,0:T(8,128)(2,1)S(1)} %constant_dynamic-update-slice_fusion.4.own_ref), channel_id=1, source_target_pairs={{0,1},{1,0},{2,3},{3,2},{4,5},{5,4},{6,7},{7,6},{8,9},{9,8},{10,11... | collective-permute-start | bytes 2359304 | tf_op jit(solution)/shard_map/ppermute | solution.py:905
  191.9 1.9 select_dynamic-update-slice_fusion
  193.8 3.3 %place_gradients.5 = f32[384,1536]{1,0:T(8,128)} custom-call(s32[28]{0:T(128)S(1)} %get-tuple-element.76.plan_ref.ids_ref, bf16[768,384]{1,0:T(8,128)(2,1)S(1)} %pad_maximum_fusion.1.own_ref, bf16[768,384]{1,0:T(8,128)(2,1)} %collective-permute-done.44.other_ref), custom_call_target="tpu_custom_call" | custom-call | tf_op jit(solution)/shard_map/place_gradients/pallas_call | solution.py:1012
  197.1 2.8 %place_gradients.4 = (f32[384,384]{1,0:T(8,128)}, f32[384,1152]{1,0:T(8,128)}) custom-call(s32[28]{0:T(128)S(1)} %get-tuple-element.76.plan_ref.ids_ref, bf16[768,384]{1,0:T(8,128)(2,1)S(1)} %pad_maximum_fusion.own_ref, bf16[768,384]{1,0:T(8,128)(2,1)S(1)} %collective-permute-done.35.other_ref), custom_call_target="tpu_custom_call" | custom-call | tf_op jit(solution)/shard_map/place_gradients/pallas_call | solution.py:1012
  199.9 3.1 %place_gradients.3 = (f32[1536,384]{1,0:T(8,128)}, f32[384,384]{1,0:T(8,128)}, f32[384]{0:T(512)}, f32[384]{0:T(512)}, f32[1]{0:T(128)}, /*index=5*/f32[1]{0:T(128)}) custom-call(s32[28]{0:T(128)S(1)} %get-tuple-element.76.plan_ref.ids_ref, bf16[1024,384]{1,0:T(8,128)(2,1)S(1)} %constant_dynamic-update-slice_fusion.4.own_ref, ...), custom_call_target="tpu_custom_call" | custom-call | tf_op jit(solution)/shard_map/place_gradients/pallas_call | solution.py:1012
  (164 shorter events, 44.9 us)
Async XLA Ops:
  2.2 29.0 %collective-permute-start.2 = (bf16[50,32,384]{2,1,0:T(8,128)(2,1)S(1)}, bf16[50,32,384]{2,1,0:T(8,128)(2,1)}, u32[]{:S(2)}, u32[]{:S(2)}) collective-permute-start(bf16[50,32,384]{2,1,0:T(8,128)(2,1)S(1)} %slice.41), channel_id=1, source_target_pairs={{0,16},{16,0},{1,17},{17,1},{2,18},{18,2},{3,19},{19,3},{4,20},{20... | collective-permute-start | bytes 3686408 | tf_op jit(solution)/shard_map/ppermute | solution.py:905
  4.5 47.6 %collective-permute-start.1 = (f32[2,16]{1,0:T(2,128)S(1)}, f32[2,16]{1,0:T(2,128)S(1)}, u32[]{:S(2)}, u32[]{:S(2)}) collective-permute-start(f32[2,16]{1,0:T(2,128)S(1)} %slice.35), channel_id=1, source_target_pairs={{0,16},{16,0},{1,17},{17,1},{2,18},{18,2},{3,19},{19,3},{4,20},{20... | collective-permute-start | bytes 392 | tf_op jit(solution)/shard_map/ppermute | solution.py:905
  5.3 46.8 %collective-permute-start = (bf16[32,16,384]{2,1,0:T(8,128)(2,1)}, bf16[32,16,384]{2,1,0:T(8,128)(2,1)S(1)}, u32[]{:S(2)}, u32[]{:S(2)}) collective-permute-start(bf16[32,16,384]{2,1,0:T(8,128)(2,1)} %slice.33), channel_id=1, source_target_pairs={{0,16},{16,0},{1,17},{17,1},{2,18},{18,2},{3,19},{19,3},{4,20},{20... | collective-permute-start | bytes 1179656 | tf_op jit(solution)/shard_map/ppermute | solution.py:905
  48.5 9.6 %collective-permute-start.3 = (bf16[128,384]{1,0:T(8,128)(2,1)S(1)}, bf16[128,384]{1,0:T(8,128)(2,1)S(1)}, u32[]{:S(2)}, u32[]{:S(2)}) collective-permute-start(bf16[128,384]{1,0:T(8,128)(2,1)S(1)} %pad_maximum_fusion.8), channel_id=1, source_target_pairs={{0,4},{1,5},{2,6},{3,7},{4,0},{5,1},{6,2},{7,3},{8,12},{9,13},{10,... | collective-permute-start | bytes 294920 | tf_op jit(solution)/shard_map/ppermute | solution.py:905
  49.8 8.3 %collective-permute-start.4 = (bf16[128,384]{1,0:T(8,128)(2,1)S(1)}, bf16[128,384]{1,0:T(8,128)(2,1)S(1)}, u32[]{:S(2)}, u32[]{:S(2)}) collective-permute-start(bf16[128,384]{1,0:T(8,128)(2,1)S(1)} %pad_maximum_fusion.8), channel_id=1, source_target_pairs={{0,8},{1,9},{2,10},{3,11},{4,12},{5,13},{6,14},{7,15},{8,0},{9,1},... | collective-permute-start | bytes 294920 | tf_op jit(solution)/shard_map/ppermute | solution.py:905
  52.1 6.4 %collective-permute-start.5 = (bf16[128,384]{1,0:T(8,128)(2,1)S(1)}, bf16[128,384]{1,0:T(8,128)(2,1)S(1)}, u32[]{:S(2)}, u32[]{:S(2)}) collective-permute-start(bf16[128,384]{1,0:T(8,128)(2,1)S(1)} %pad_maximum_fusion.8), channel_id=1, source_target_pairs={{0,12},{1,13},{2,14},{3,15},{4,8},{5,9},{6,10},{7,11},{8,4},{9,5},... | collective-permute-start | bytes 294920 | tf_op jit(solution)/shard_map/ppermute | solution.py:905
  58.6 12.1 %collective-permute-start.8 = (bf16[512,384]{1,0:T(8,128)(2,1)S(1)}, bf16[512,384]{1,0:T(8,128)(2,1)S(1)}, u32[]{:S(2)}, u32[]{:S(2)}) collective-permute-start(bf16[512,384]{1,0:T(8,128)(2,1)S(1)} %constant_dynamic-update-slice_fusion.refs_2_), channel_id=1, source_target_pairs={{0,2},{1,3},{2,0},{3,1},{4,6},{5,7},{6,4},{7,5},{8,10},{9,11},{10,... | collective-permute-start | bytes 1179656 | tf_op jit(solution)/shard_map/ppermute | solution.py:905
  60.0 18.1 %collective-permute-start.7 = (bf16[512,384]{1,0:T(8,128)(2,1)S(1)}, bf16[512,384]{1,0:T(8,128)(2,1)S(1)}, u32[]{:S(2)}, u32[]{:S(2)}) collective-permute-start(bf16[512,384]{1,0:T(8,128)(2,1)S(1)} %constant_dynamic-update-slice_fusion.refs_2_), channel_id=1, source_target_pairs={{0,1},{1,0},{2,3},{3,2},{4,5},{5,4},{6,7},{7,6},{8,9},{9,8},{10,11... | collective-permute-start | bytes 1179656 | tf_op jit(solution)/shard_map/ppermute | solution.py:905
  70.7 7.3 %collective-permute-start.9 = (bf16[512,384]{1,0:T(8,128)(2,1)S(1)}, bf16[512,384]{1,0:T(8,128)(2,1)S(1)}, u32[]{:S(2)}, u32[]{:S(2)}) collective-permute-start(bf16[512,384]{1,0:T(8,128)(2,1)S(1)} %collective-permute-done.8.refs_4_), channel_id=1, source_target_pairs={{0,1},{1,0},{2,3},{3,2},{4,5},{5,4},{6,7},{7,6},{8,9},{9,8},{10,11... | collective-permute-start | bytes 1179656 | tf_op jit(solution)/shard_map/ppermute | solution.py:905
  70.9 7.2 %collective-permute-start.6 = (bf16[128,384]{1,0:T(8,128)(2,1)S(1)}, bf16[128,384]{1,0:T(8,128)(2,1)S(1)}, u32[]{:S(2)}, u32[]{:S(2)}) collective-permute-start(bf16[128,384]{1,0:T(8,128)(2,1)S(1)} %get-tuple-element.85.refs_0_), channel_id=1, source_target_pairs={{0,16},{16,0},{1,17},{17,1},{2,18},{18,2},{3,19},{19,3},{4,20},{20... | collective-permute-start | bytes 294920 | tf_op jit(solution)/shard_map/ppermute | solution.py:905
  85.5 4.9 %collective-permute-start.12 = (f32[16,128]{1,0:T(8,128)S(1)}, f32[16,128]{1,0:T(8,128)S(1)}, u32[]{:S(2)}, u32[]{:S(2)}) collective-permute-start(f32[16,128]{1,0:T(8,128)S(1)} %add.132), channel_id=1, source_target_pairs={{0,1},{1,0},{2,3},{3,2},{4,5},{5,4},{6,7},{7,6},{8,9},{9,8},{10,11... | collective-permute-start | bytes 24584 | tf_op jit(solution)/shard_map/ppermute | solution.py:905
  117.5 9.7 %collective-permute-start.36 = (bf16[768,384]{1,0:T(8,128)(2,1)}, bf16[768,384]{1,0:T(8,128)(2,1)S(1)}, u32[]{:S(2)}, u32[]{:S(2)}) collective-permute-start(bf16[768,384]{1,0:T(8,128)(2,1)} %get-tuple-element.111), channel_id=1, source_target_pairs={{0,1},{1,0},{2,3},{3,2},{4,5},{5,4},{6,7},{7,6},{8,9},{9,8},{10,11... | collective-permute-start | bytes 1769480 | tf_op jit(solution)/shard_map/ppermute | solution.py:905
  118.7 9.9 %collective-permute-start.27 = (bf16[768,384]{1,0:T(8,128)(2,1)}, bf16[768,384]{1,0:T(8,128)(2,1)S(1)}, u32[]{:S(2)}, u32[]{:S(2)}) collective-permute-start(bf16[768,384]{1,0:T(8,128)(2,1)} %get-tuple-element.106), channel_id=1, source_target_pairs={{0,1},{1,0},{2,3},{3,2},{4,5},{5,4},{6,7},{7,6},{8,9},{9,8},{10,11... | collective-permute-start | bytes 1769480 | tf_op jit(solution)/shard_map/ppermute | solution.py:905
  119.9 44.2 %collective-permute-start.22 = (bf16[32,16,384]{2,1,0:T(8,128)(2,1)S(1)}, bf16[32,16,384]{2,1,0:T(8,128)(2,1)S(1)}, u32[]{:S(2)}, u32[]{:S(2)}) collective-permute-start(bf16[32,16,384]{2,1,0:T(8,128)(2,1)S(1)} %slice.40), channel_id=1, source_target_pairs={{0,16},{16,0},{1,17},{17,1},{2,18},{18,2},{3,19},{19,3},{4,20},{20... | collective-permute-start | bytes 1179656 | tf_op jit(solution)/shard_map/ppermute | solution.py:905
  127.3 8.7 %collective-permute-start.37 = (bf16[384,384]{1,0:T(8,128)(2,1)S(1)}, bf16[384,384]{1,0:T(8,128)(2,1)S(1)}, u32[]{:S(2)}, u32[]{:S(2)}) collective-permute-start(bf16[384,384]{1,0:T(8,128)(2,1)S(1)} %fusion.2), channel_id=1, source_target_pairs={{0,2},{1,3},{2,0},{3,1},{4,6},{5,7},{6,4},{7,5},{8,10},{9,11},{10,... | collective-permute-start | bytes 884744 | tf_op jit(solution)/shard_map/ppermute | solution.py:905
  128.9 8.4 %collective-permute-start.28 = (bf16[384,384]{1,0:T(8,128)(2,1)S(1)}, bf16[384,384]{1,0:T(8,128)(2,1)S(1)}, u32[]{:S(2)}, u32[]{:S(2)}) collective-permute-start(bf16[384,384]{1,0:T(8,128)(2,1)S(1)} %fusion.1), channel_id=1, source_target_pairs={{0,4},{1,5},{2,6},{3,7},{4,0},{5,1},{6,2},{7,3},{8,12},{9,13},{10,... | collective-permute-start | bytes 884744 | tf_op jit(solution)/shard_map/ppermute | solution.py:905
  130.1 20.6 %collective-permute-start.18 = (bf16[512,384]{1,0:T(8,128)(2,1)S(1)}, bf16[512,384]{1,0:T(8,128)(2,1)S(1)}, u32[]{:S(2)}, u32[]{:S(2)}) collective-permute-start(bf16[512,384]{1,0:T(8,128)(2,1)S(1)} %fusion), channel_id=1, source_target_pairs={{0,16},{16,0},{1,17},{17,1},{2,18},{18,2},{3,19},{19,3},{4,20},{20... | collective-permute-start | bytes 1179656 | tf_op jit(solution)/shard_map/ppermute | solution.py:905
  137.3 9.8 %collective-permute-start.29 = (bf16[192,384]{1,0:T(8,128)(2,1)S(1)}, bf16[192,384]{1,0:T(8,128)(2,1)S(1)}, u32[]{:S(2)}, u32[]{:S(2)}) collective-permute-start(bf16[192,384]{1,0:T(8,128)(2,1)S(1)} %fusion.5), channel_id=1, source_target_pairs={{0,16},{16,0},{1,17},{17,1},{2,18},{18,2},{3,19},{19,3},{4,20},{20... | collective-permute-start | bytes 442376 | tf_op jit(solution)/shard_map/ppermute | solution.py:905
  140.8 7.9 %collective-permute-start.39 = (bf16[96,384]{1,0:T(8,128)(2,1)S(1)}, bf16[96,384]{1,0:T(8,128)(2,1)S(1)}, u32[]{:S(2)}, u32[]{:S(2)}) collective-permute-start(bf16[96,384]{1,0:T(8,128)(2,1)S(1)} %fusion.11), channel_id=1, source_target_pairs={{0,16},{16,0},{1,17},{17,1},{2,18},{18,2},{3,19},{19,3},{4,20},{20... | collective-permute-start | bytes 221192 | tf_op jit(solution)/shard_map/ppermute | solution.py:905
  147.2 5.0 %collective-permute-start.30 = (bf16[96,384]{1,0:T(8,128)(2,1)S(1)}, bf16[96,384]{1,0:T(8,128)(2,1)S(1)}, u32[]{:S(2)}, u32[]{:S(2)}) collective-permute-start(bf16[96,384]{1,0:T(8,128)(2,1)S(1)} %fusion.10), channel_id=1, source_target_pairs={{0,2},{1,3},{2,0},{3,1},{4,6},{5,7},{6,4},{7,5},{8,10},{9,11},{10,... | collective-permute-start | bytes 221192 | tf_op jit(solution)/shard_map/ppermute | solution.py:905
  148.7 8.6 %collective-permute-start.40 = (bf16[96,384]{1,0:T(8,128)(2,1)S(1)}, bf16[96,384]{1,0:T(8,128)(2,1)S(1)}, u32[]{:S(2)}, u32[]{:S(2)}) collective-permute-start(bf16[96,384]{1,0:T(8,128)(2,1)S(1)} %fusion.7), channel_id=1, source_target_pairs={{0,8},{1,9},{2,10},{3,11},{4,12},{5,13},{6,14},{7,15},{8,0},{9,1},... | collective-permute-start | bytes 221192 | tf_op jit(solution)/shard_map/ppermute | solution.py:905
  150.9 4.9 %collective-permute-start.19 = (bf16[256,384]{1,0:T(8,128)(2,1)S(1)}, bf16[256,384]{1,0:T(8,128)(2,1)S(1)}, u32[]{:S(2)}, u32[]{:S(2)}) collective-permute-start(bf16[256,384]{1,0:T(8,128)(2,1)S(1)} %fusion.3), channel_id=1, source_target_pairs={{0,2},{1,3},{2,0},{3,1},{4,6},{5,7},{6,4},{7,5},{8,10},{9,11},{10,... | collective-permute-start | bytes 589832 | tf_op jit(solution)/shard_map/ppermute | solution.py:905
  152.2 9.4 %collective-permute-start.31 = (bf16[96,384]{1,0:T(8,128)(2,1)S(1)}, bf16[96,384]{1,0:T(8,128)(2,1)S(1)}, u32[]{:S(2)}, u32[]{:S(2)}) collective-permute-start(bf16[96,384]{1,0:T(8,128)(2,1)S(1)} %fusion.8), channel_id=1, source_target_pairs={{0,8},{1,9},{2,10},{3,11},{4,12},{5,13},{6,14},{7,15},{8,0},{9,1},... | collective-permute-start | bytes 221192 | tf_op jit(solution)/shard_map/ppermute | solution.py:905
  157.3 8.4 %collective-permute-start.41 = (bf16[96,384]{1,0:T(8,128)(2,1)S(1)}, bf16[96,384]{1,0:T(8,128)(2,1)S(1)}, u32[]{:S(2)}, u32[]{:S(2)}) collective-permute-start(bf16[96,384]{1,0:T(8,128)(2,1)S(1)} %add_convert_fusion.1), channel_id=1, source_target_pairs={{0,16},{16,0},{1,17},{17,1},{2,18},{18,2},{3,19},{19,3},{4,20},{20... | collective-permute-start | bytes 221192 | tf_op jit(solution)/shard_map/ppermute | solution.py:905
  161.6 8.7 %collective-permute-start.32 = (bf16[96,384]{1,0:T(8,128)(2,1)S(1)}, bf16[96,384]{1,0:T(8,128)(2,1)S(1)}, u32[]{:S(2)}, u32[]{:S(2)}) collective-permute-start(bf16[96,384]{1,0:T(8,128)(2,1)S(1)} %add_convert_fusion.2), channel_id=1, source_target_pairs={{0,2},{1,3},{2,0},{3,1},{4,6},{5,7},{6,4},{7,5},{8,10},{9,11},{10,... | collective-permute-start | bytes 221192 | tf_op jit(solution)/shard_map/ppermute | solution.py:905
  165.7 5.7 %collective-permute-start.42 = (bf16[192,384]{1,0:T(8,128)(2,1)S(1)}, bf16[192,384]{1,0:T(8,128)(2,1)S(1)}, u32[]{:S(2)}, u32[]{:S(2)}) collective-permute-start(bf16[192,384]{1,0:T(8,128)(2,1)S(1)} %pad_maximum_fusion.7), channel_id=1, source_target_pairs={{0,4},{1,5},{2,6},{3,7},{4,0},{5,1},{6,2},{7,3},{8,12},{9,13},{10,... | collective-permute-start | bytes 442376 | tf_op jit(solution)/shard_map/ppermute | solution.py:905
  168.8 4.9 %collective-permute-start.24 = (bf16[256,384]{1,0:T(8,128)(2,1)S(1)}, bf16[256,384]{1,0:T(8,128)(2,1)S(1)}, u32[]{:S(2)}, u32[]{:S(2)}) collective-permute-start(bf16[256,384]{1,0:T(8,128)(2,1)S(1)} %pad_maximum_fusion.5), channel_id=1, source_target_pairs={{0,2},{1,3},{2,0},{3,1},{4,6},{5,7},{6,4},{7,5},{8,10},{9,11},{10,... | collective-permute-start | bytes 589832 | tf_op jit(solution)/shard_map/ppermute | solution.py:905
  171.4 17.5 %collective-permute-start.43 = (bf16[384,384]{1,0:T(8,128)(2,1)S(1)}, bf16[384,384]{1,0:T(8,128)(2,1)S(1)}, u32[]{:S(2)}, u32[]{:S(2)}) collective-permute-start(bf16[384,384]{1,0:T(8,128)(2,1)S(1)} %pad_maximum_fusion.4), channel_id=1, source_target_pairs={{0,2},{1,3},{2,0},{3,1},{4,6},{5,7},{6,4},{7,5},{8,10},{9,11},{10,... | collective-permute-start | bytes 884744 | tf_op jit(solution)/shard_map/ppermute | solution.py:905
  173.7 8.6 %collective-permute-start.25 = (bf16[512,384]{1,0:T(8,128)(2,1)S(1)}, bf16[512,384]{1,0:T(8,128)(2,1)S(1)}, u32[]{:S(2)}, u32[]{:S(2)}) collective-permute-start(bf16[512,384]{1,0:T(8,128)(2,1)S(1)} %pad_maximum_fusion.2), channel_id=1, source_target_pairs={{0,16},{16,0},{1,17},{17,1},{2,18},{18,2},{3,19},{19,3},{4,20},{20... | collective-permute-start | bytes 1179656 | tf_op jit(solution)/shard_map/ppermute | solution.py:905
  175.1 14.0 %collective-permute-start.34 = (bf16[384,384]{1,0:T(8,128)(2,1)S(1)}, bf16[384,384]{1,0:T(8,128)(2,1)S(1)}, u32[]{:S(2)}, u32[]{:S(2)}) collective-permute-start(bf16[384,384]{1,0:T(8,128)(2,1)S(1)} %pad_maximum_fusion.3), channel_id=1, source_target_pairs={{0,4},{1,5},{2,6},{3,7},{4,0},{5,1},{6,2},{7,3},{8,12},{9,13},{10,... | collective-permute-start | bytes 884744 | tf_op jit(solution)/shard_map/ppermute | solution.py:905
  182.4 17.5 %collective-permute-start.26 = (bf16[1024,384]{1,0:T(8,128)(2,1)S(1)}, bf16[1024,384]{1,0:T(8,128)(2,1)S(1)}, u32[]{:S(2)}, u32[]{:S(2)}) collective-permute-start(bf16[1024,384]{1,0:T(8,128)(2,1)S(1)} %constant_dynamic-update-slice_fusion.4.own_ref), channel_id=1, source_target_pairs={{0,1},{1,0},{2,3},{3,2},{4,5},{5,4},{6,7},{7,6},{8,9},{9,8},{10,11... | collective-permute-start | bytes 2359304 | tf_op jit(solution)/shard_map/ppermute | solution.py:905
  189.2 7.9 %collective-permute-start.35 = (bf16[768,384]{1,0:T(8,128)(2,1)S(1)}, bf16[768,384]{1,0:T(8,128)(2,1)S(1)}, u32[]{:S(2)}, u32[]{:S(2)}) collective-permute-start(bf16[768,384]{1,0:T(8,128)(2,1)S(1)} %pad_maximum_fusion.own_ref), channel_id=1, source_target_pairs={{0,1},{1,0},{2,3},{3,2},{4,5},{5,4},{6,7},{7,6},{8,9},{9,8},{10,11... | collective-permute-start | bytes 1769480 | tf_op jit(solution)/shard_map/ppermute | solution.py:905
  (31 other events, 268.5 us)

commit v4 on v3

--- a/solution.py
+++ b/solution.py
@@ -171,7 +171,7 @@
 
     largest = jnp.zeros((slots, 2 * slots), F32)
     units = [(p, h) for p in range(GROUP) for h in range(tiles)]
-    ahead = 4
+    ahead = 6
     feed = iter(())
     projected(0)
     for g in range(groups):
@@ -855,7 +855,7 @@
         kbd = jnp.concatenate([k * low, k * high], axis=0)
         dmix[pl.ds(g * 128, 128), h : h + 128] = (mm(ds, kbd) * HEAD**-0.5).astype(BF16)
 
-    staggered([scores, soft, products, query], [(g, h) for g in range(rows // 128) for h in range(0, width, 128)], 2)
+    staggered([scores, soft, products, query], [(g, h) for g in range(rows // 128) for h in range(0, width, 128)], 3)
 
 
 def text_backward(

time: 204 us -> 204 us (level)
  no operation moved by 1% of the time
where the time goes in v4:
time: 204 us; the launch traced here: 203 us
  Pallas kernels  80.4 us (39%)
  starting transfers between devices  65.4 us (32%)
  waiting for transfers between devices  44.4 us (22%)
  local copies, waits for them, and re-layouts  5.36 us (3%)
  between operations  3.96 us (2%)
  other arithmetic  3.85 us (2%)
    ppermute x45, starting transfers between devices, flip(): return lax.ppermute(values, axis, [(k, k ^ bits) for k in range(size)])  65.4 us
    ppermute x45, waiting for transfers between devices, flip(): return lax.ppermute(values, axis, [(k, k ^ bits) for k in range(size)])  44.4 us
    pallas_call x2, Pallas kernels, image_tower(): pl.pallas_call(kernel, grid_spec=pltpu.PrefetchScalarGridSpec(num_scalar_...  34.3 us
    pallas_call x1, Pallas kernels, text_backward(): pl.pallas_call(functools.partial(back_kernel, cut, len(others)), grid_spe...  18.6 us
    pallas_call x3, Pallas kernels, place(): pl.pallas_call(functools.partial(place_kernel, targets, rounds, last), in...  9.23 us
    pallas_call x1, Pallas kernels, text_second(): pl.pallas_call(functools.partial(text_second_kernel, cut), grid_spec=pltp...  7.05 us
    pallas_call x1, Pallas kernels, text_first(): pl.pallas_call(functools.partial(text_first_kernel, cut), grid_spec=pltpu...  5.92 us
  transfers between devices with their start and end apart: 45, of which 18 were waited for; matrix products, arithmetic and copies ran while one was open for 4% of the time, Pallas kernels for 27%

profile of v4, /device:TPU:1, one launch (start us, length us, event | category | flops | bytes accessed | tf_op | source)
XLA Modules:
  0.0 203.3 jit_solution(17225420335087697195)
XLA Ops:
  2.2 2.1 %collective-permute-start.2 = (bf16[50,32,384]{2,1,0:T(8,128)(2,1)S(1)}, bf16[50,32,384]{2,1,0:T(8,128)(2,1)}, u32[]{:S(2)}, u32[]{:S(2)}) collective-permute-start(bf16[50,32,384]{2,1,0:T(8,128)(2,1)S(1)} %slice.41), channel_id=1, source_target_pairs={{0,16},{16,0},{1,17},{17,1},{2,18},{18,2},{3,19},{19,3},{4,20},{20... | collective-permute-start | bytes 3686408 | tf_op jit(solution)/shard_map/ppermute | solution.py:905
  8.9 18.0 %image_block.3 = bf16[96,384]{1,0:T(8,128)(2,1)} custom-call(s32[28]{0:T(128)S(1)} %get-tuple-element.76.plan_ref.ids_ref, bf16[50,128,384]{2,1,0:T(8,128)(2,1)} %bitcast.56, bf16[384,1152]{1,0:T(8,128)(2,1)} %refs_0_.1, bf16[384,384]{1,0:T(8,128)(2,1)S(1)} %copy-done.13, bf16[384,1536]{1,0:T(8,128)(2,1)} %refs_2_.1, bf16[1536,384]{1,0:T(8,128)(2,1)} %refs_3_.1, ...), custom_call_target="tpu_custom_call" | custom-call | flops 11324620800 | bytes 7880704 | tf_op jit(solution)/shard_map/image_block/pallas_call | solution.py:247
  28.2 3.0 %collective-permute-done.2 = bf16[50,32,384]{2,1,0:T(8,128)(2,1)} collective-permute-done((bf16[50,32,384]{2,1,0:T(8,128)(2,1)S(1)}, bf16[50,32,384]{2,1,0:T(8,128)(2,1)}, u32[]{:S(2)}, u32[]{:S(2)}) %collective-permute-start.2) | collective-permute-done | bytes 1228832 | tf_op jit(solution)/shard_map/ppermute | solution.py:905
  31.2 16.3 %conditional.1 = (bf16[32,384]{1,0:T(8,128)(2,1)S(1)}) conditional(s32[]{:T(128)} %bitcast.1, () %tuple.17, (s32[28]{0:T(128)S(1)}, bf16[50,128,384]{2,1,0:T(8,128)(2,1)}, bf16[50,32,384]{2,1,0:T(8,128)(2,1)}, bf16[384,1152]{1,0:T(8,128)(2,1)}, bf16[384,384]{1,0:T(8,128)(2,1)S(1)}, /*index=5*/bf16[384,1536]{1,0:T(8,128)(2,1)}, ...), branch_computations={%region_0.0_spmd, %region_1.0_spmd} | conditional | flops 37748736 | bytes 54239 | solution.py:1048
  31.2 16.3 %image_block.2 = bf16[32,384]{1,0:T(8,128)(2,1)S(1)} custom-call(s32[28]{0:T(128)S(1)} %get-tuple-element.7.plan_ref, bf16[50,128,384]{2,1,0:T(8,128)(2,1)} %get-tuple-element.20.x_ref, bf16[50,32,384]{2,1,0:T(8,128)(2,1)} %get-tuple-element.21.recv_ref, bf16[384,1152]{1,0:T(8,128)(2,1)} %get-tuple-element.22.wqkv_ref, ...), custom_call_target="tpu_custom_call" | custom-call | flops 37748736 | bytes 54231 | tf_op jit(solution)/shard_map/cond/branch_1_fun/image_block/pallas_call | solution.py:247
  49.7 2.3 %collective-permute-start.4 = (bf16[128,384]{1,0:T(8,128)(2,1)S(1)}, bf16[128,384]{1,0:T(8,128)(2,1)S(1)}, u32[]{:S(2)}, u32[]{:S(2)}) collective-permute-start(bf16[128,384]{1,0:T(8,128)(2,1)S(1)} %pad_maximum_fusion.8), channel_id=1, source_target_pairs={{0,8},{1,9},{2,10},{3,11},{4,12},{5,13},{6,14},{7,15},{8,0},{9,1},... | collective-permute-start | bytes 294920 | tf_op jit(solution)/shard_map/ppermute | solution.py:905
  52.1 5.9 %text_attention.1 = (bf16[2048,1152]{1,0:T(8,128)(2,1)}, bf16[2048,384]{1,0:T(8,128)(2,1)S(1)}, f32[2048,384]{1,0:T(8,128)S(1)}) custom-call(s32[28]{0:T(128)S(1)} %get-tuple-element.76.plan_ref.ids_ref, bf16[128,16,384]{2,1,0:T(8,128)(2,1)S(1)} %copy-done, bf16[32,16,384]{2,1,0:T(8,128)(2,1)S(1)} %collective-permute-done.recv_ref, ...), custom_call_target="tpu_custom_call" | custom-call | flops 3019898880 | bytes 12582912 | tf_op jit(solution)/shard_map/text_attention/pallas_call | solution.py:484
  59.9 3.7 %collective-permute-start.7 = (bf16[512,384]{1,0:T(8,128)(2,1)S(1)}, bf16[512,384]{1,0:T(8,128)(2,1)S(1)}, u32[]{:S(2)}, u32[]{:S(2)}) collective-permute-start(bf16[512,384]{1,0:T(8,128)(2,1)S(1)} %constant_dynamic-update-slice_fusion.refs_2_), channel_id=1, source_target_pairs={{0,1},{1,0},{2,3},{3,2},{4,5},{5,4},{6,7},{7,6},{8,9},{9,8},{10,11... | collective-permute-start | bytes 1179656 | tf_op jit(solution)/shard_map/ppermute | solution.py:905
  63.6 7.0 %text_pool.1 = (bf16[2048,1536]{1,0:T(8,128)(2,1)S(1)}, f32[128,1536]{1,0:T(8,128)S(1)}, bf16[128,384]{1,0:T(8,128)(2,1)S(1)}, f32[128,384]{1,0:T(8,128)S(1)}, bf16[128,384]{1,0:T(8,128)(2,1)S(1)}) custom-call(s32[28]{0:T(128)S(1)} %get-tuple-element.76.plan_ref.ids_ref, f32[2048,384]{1,0:T(8,128)S(1)} %get-tuple-element.80.y1_ref, ...), custom_call_target="tpu_custom_call" | custom-call | flops 2415919104 | bytes 12582912 | tf_op jit(solution)/shard_map/text_pool/pallas_call | solution.py:561
  70.8 5.0 %collective-permute-start.6 = (bf16[128,384]{1,0:T(8,128)(2,1)S(1)}, bf16[128,384]{1,0:T(8,128)(2,1)S(1)}, u32[]{:S(2)}, u32[]{:S(2)}) collective-permute-start(bf16[128,384]{1,0:T(8,128)(2,1)S(1)} %get-tuple-element.85.refs_0_), channel_id=1, source_target_pairs={{0,16},{16,0},{1,17},{17,1},{2,18},{18,2},{3,19},{19,3},{4,20},{20... | collective-permute-start | bytes 294920 | tf_op jit(solution)/shard_map/ppermute | solution.py:905
  75.8 2.8 %collective-permute-done.6.refs_1_ = bf16[128,384]{1,0:T(8,128)(2,1)S(1)} collective-permute-done((bf16[128,384]{1,0:T(8,128)(2,1)S(1)}, bf16[128,384]{1,0:T(8,128)(2,1)S(1)}, u32[]{:S(2)}, u32[]{:S(2)}) %collective-permute-start.6) | collective-permute-done | bytes 98336 | tf_op jit(solution)/shard_map/ppermute | solution.py:905
  82.6 2.3 %collective-permute-start.11 = (f32[16,128]{1,0:T(8,128)S(1)}, f32[16,128]{1,0:T(8,128)S(1)}, u32[]{:S(2)}, u32[]{:S(2)}) collective-permute-start(f32[16,128]{1,0:T(8,128)S(1)} %add.131), channel_id=1, source_target_pairs={{0,8},{1,9},{2,10},{3,11},{4,12},{5,13},{6,14},{7,15},{8,0},{9,1},... | collective-permute-start | bytes 24584 | tf_op jit(solution)/shard_map/ppermute | solution.py:905
  86.0 3.2 %collective-permute-start.12 = (f32[16,128]{1,0:T(8,128)S(1)}, f32[16,128]{1,0:T(8,128)S(1)}, u32[]{:S(2)}, u32[]{:S(2)}) collective-permute-start(f32[16,128]{1,0:T(8,128)S(1)} %add.132), channel_id=1, source_target_pairs={{0,1},{1,0},{2,3},{3,2},{4,5},{5,4},{6,7},{7,6},{8,9},{9,8},{10,11... | collective-permute-start | bytes 24584 | tf_op jit(solution)/shard_map/ppermute | solution.py:905
  92.6 2.4 %similarity_grads.1 = (f32[128,384]{1,0:T(8,128)S(1)}, bf16[128,384]{1,0:T(8,128)(2,1)S(1)}, f32[8,128]{1,0:T(8,128)S(1)}) custom-call(s32[28]{0:T(128)S(1)} %get-tuple-element.76.plan_ref.ids_ref, f32[8,128]{1,0:T(8,128)S(1)} %copy-done.2, f32[2,128]{1,0:T(2,128)S(1)} %copy-done.3, f32[16,128]{1,0:T(8,128)S(1)} %copy-done.1, ...), custom_call_target="tpu_custom_call" | custom-call | flops 805306368 | bytes 1572864 | tf_op jit(solution)/shard_map/similarity_grads/pallas_call | solution.py:666
  96.5 2.5 %collective-permute-done.16.refs_0_ = bf16[128,384]{1,0:T(8,128)(2,1)S(1)} collective-permute-done((bf16[128,384]{1,0:T(8,128)(2,1)S(1)}, bf16[128,384]{1,0:T(8,128)(2,1)S(1)}, u32[]{:S(2)}, u32[]{:S(2)}) %collective-permute-start.16) | collective-permute-done | bytes 98336 | tf_op jit(solution)/shard_map/ppermute | solution.py:905
  99.0 18.6 %text_backward.1 = (bf16[128,16,384]{2,1,0:T(8,128)(2,1)}, bf16[1024,384]{1,0:T(8,128)(2,1)}, bf16[1024,384]{1,0:T(8,128)(2,1)}, bf16[768,384]{1,0:T(8,128)(2,1)...) custom-call(s32[28]{0:T(128)S(1)} %get-tuple-element.76.plan_ref.ids_ref, ...), custom_call_target="tpu_custom_call" | custom-call | flops 10871635968 | bytes 25165824 | tf_op jit(solution)/shard_map/text_backward/pallas_call | solution.py:872
  120.0 6.4 %collective-permute-start.22 = (bf16[32,16,384]{2,1,0:T(8,128)(2,1)S(1)}, bf16[32,16,384]{2,1,0:T(8,128)(2,1)S(1)}, u32[]{:S(2)}, u32[]{:S(2)}) collective-permute-start(bf16[32,16,384]{2,1,0:T(8,128)(2,1)S(1)} %slice.40), channel_id=1, source_target_pairs={{0,16},{16,0},{1,17},{17,1},{2,18},{18,2},{3,19},{19,3},{4,20},{20... | collective-permute-start | bytes 1179656 | tf_op jit(solution)/shard_map/ppermute | solution.py:905
  130.2 5.8 %collective-permute-done.37 = bf16[384,384]{1,0:T(8,128)(2,1)S(1)} collective-permute-done((bf16[384,384]{1,0:T(8,128)(2,1)S(1)}, bf16[384,384]{1,0:T(8,128)(2,1)S(1)}, u32[]{:S(2)}, u32[]{:S(2)}) %collective-permute-start.37) | collective-permute-done | bytes 294944 | tf_op jit(solution)/shard_map/ppermute | solution.py:905
  137.4 3.3 %collective-permute-done.38 = bf16[192,384]{1,0:T(8,128)(2,1)S(1)} collective-permute-done((bf16[192,384]{1,0:T(8,128)(2,1)S(1)}, bf16[192,384]{1,0:T(8,128)(2,1)S(1)}, u32[]{:S(2)}, u32[]{:S(2)}) %collective-permute-start.38) | collective-permute-done | bytes 147488 | tf_op jit(solution)/shard_map/ppermute | solution.py:905
  140.9 6.2 %collective-permute-done.29 = bf16[192,384]{1,0:T(8,128)(2,1)S(1)} collective-permute-done((bf16[192,384]{1,0:T(8,128)(2,1)S(1)}, bf16[192,384]{1,0:T(8,128)(2,1)S(1)}, u32[]{:S(2)}, u32[]{:S(2)}) %collective-permute-start.29) | collective-permute-done | bytes 147488 | tf_op jit(solution)/shard_map/ppermute | solution.py:905
  148.7 2.0 collective-permute-start.40
  152.7 2.7 %collective-permute-done.19 = bf16[256,384]{1,0:T(8,128)(2,1)S(1)} collective-permute-done((bf16[256,384]{1,0:T(8,128)(2,1)S(1)}, bf16[256,384]{1,0:T(8,128)(2,1)S(1)}, u32[]{:S(2)}, u32[]{:S(2)}) %collective-permute-start.19) | collective-permute-done | bytes 196640 | tf_op jit(solution)/shard_map/ppermute | solution.py:905
  155.5 1.8 collective-permute-start.20
  159.7 1.8 collective-permute-start.21
  165.9 2.9 %collective-permute-done.23 = bf16[128,384]{1,0:T(8,128)(2,1)S(1)} collective-permute-done((bf16[128,384]{1,0:T(8,128)(2,1)S(1)}, bf16[128,384]{1,0:T(8,128)(2,1)S(1)}, u32[]{:S(2)}, u32[]{:S(2)}) %collective-permute-start.23) | collective-permute-done | bytes 98336 | tf_op jit(solution)/shard_map/ppermute | solution.py:905
  171.9 1.8 collective-permute-done.24
  175.8 6.6 %collective-permute-done.25 = bf16[512,384]{1,0:T(8,128)(2,1)S(1)} collective-permute-done((bf16[512,384]{1,0:T(8,128)(2,1)S(1)}, bf16[512,384]{1,0:T(8,128)(2,1)S(1)}, u32[]{:S(2)}, u32[]{:S(2)}) %collective-permute-start.25) | collective-permute-done | bytes 393248 | tf_op jit(solution)/shard_map/ppermute | solution.py:905
  182.4 6.6 %collective-permute-start.26 = (bf16[1024,384]{1,0:T(8,128)(2,1)S(1)}, bf16[1024,384]{1,0:T(8,128)(2,1)S(1)}, u32[]{:S(2)}, u32[]{:S(2)}) collective-permute-start(bf16[1024,384]{1,0:T(8,128)(2,1)S(1)} %constant_dynamic-update-slice_fusion.4.own_ref), channel_id=1, source_target_pairs={{0,1},{1,0},{2,3},{3,2},{4,5},{5,4},{6,7},{7,6},{8,9},{9,8},{10,11... | collective-permute-start | bytes 2359304 | tf_op jit(solution)/shard_map/ppermute | solution.py:905
  192.0 1.9 select_dynamic-update-slice_fusion
  193.9 3.3 %place_gradients.5 = f32[384,1536]{1,0:T(8,128)} custom-call(s32[28]{0:T(128)S(1)} %get-tuple-element.76.plan_ref.ids_ref, bf16[768,384]{1,0:T(8,128)(2,1)S(1)} %pad_maximum_fusion.1.own_ref, bf16[768,384]{1,0:T(8,128)(2,1)} %collective-permute-done.44.other_ref), custom_call_target="tpu_custom_call" | custom-call | tf_op jit(solution)/shard_map/place_gradients/pallas_call | solution.py:1012
  197.2 2.8 %place_gradients.4 = (f32[384,384]{1,0:T(8,128)}, f32[384,1152]{1,0:T(8,128)}) custom-call(s32[28]{0:T(128)S(1)} %get-tuple-element.76.plan_ref.ids_ref, bf16[768,384]{1,0:T(8,128)(2,1)S(1)} %pad_maximum_fusion.own_ref, bf16[768,384]{1,0:T(8,128)(2,1)S(1)} %collective-permute-done.35.other_ref), custom_call_target="tpu_custom_call" | custom-call | tf_op jit(solution)/shard_map/place_gradients/pallas_call | solution.py:1012
  200.0 3.1 %place_gradients.3 = (f32[1536,384]{1,0:T(8,128)}, f32[384,384]{1,0:T(8,128)}, f32[384]{0:T(512)}, f32[384]{0:T(512)}, f32[1]{0:T(128)}, /*index=5*/f32[1]{0:T(128)}) custom-call(s32[28]{0:T(128)S(1)} %get-tuple-element.76.plan_ref.ids_ref, bf16[1024,384]{1,0:T(8,128)(2,1)S(1)} %constant_dynamic-update-slice_fusion.4.own_ref, ...), custom_call_target="tpu_custom_call" | custom-call | tf_op jit(solution)/shard_map/place_gradients/pallas_call | solution.py:1012
  (164 shorter events, 44.9 us)
Async XLA Ops:
  2.2 29.0 %collective-permute-start.2 = (bf16[50,32,384]{2,1,0:T(8,128)(2,1)S(1)}, bf16[50,32,384]{2,1,0:T(8,128)(2,1)}, u32[]{:S(2)}, u32[]{:S(2)}) collective-permute-start(bf16[50,32,384]{2,1,0:T(8,128)(2,1)S(1)} %slice.41), channel_id=1, source_target_pairs={{0,16},{16,0},{1,17},{17,1},{2,18},{18,2},{3,19},{19,3},{4,20},{20... | collective-permute-start | bytes 3686408 | tf_op jit(solution)/shard_map/ppermute | solution.py:905
  4.5 47.5 %collective-permute-start.1 = (f32[2,16]{1,0:T(2,128)S(1)}, f32[2,16]{1,0:T(2,128)S(1)}, u32[]{:S(2)}, u32[]{:S(2)}) collective-permute-start(f32[2,16]{1,0:T(2,128)S(1)} %slice.35), channel_id=1, source_target_pairs={{0,16},{16,0},{1,17},{17,1},{2,18},{18,2},{3,19},{19,3},{4,20},{20... | collective-permute-start | bytes 392 | tf_op jit(solution)/shard_map/ppermute | solution.py:905
  5.3 46.7 %collective-permute-start = (bf16[32,16,384]{2,1,0:T(8,128)(2,1)}, bf16[32,16,384]{2,1,0:T(8,128)(2,1)S(1)}, u32[]{:S(2)}, u32[]{:S(2)}) collective-permute-start(bf16[32,16,384]{2,1,0:T(8,128)(2,1)} %slice.33), channel_id=1, source_target_pairs={{0,16},{16,0},{1,17},{17,1},{2,18},{18,2},{3,19},{19,3},{4,20},{20... | collective-permute-start | bytes 1179656 | tf_op jit(solution)/shard_map/ppermute | solution.py:905
  48.4 9.6 %collective-permute-start.3 = (bf16[128,384]{1,0:T(8,128)(2,1)S(1)}, bf16[128,384]{1,0:T(8,128)(2,1)S(1)}, u32[]{:S(2)}, u32[]{:S(2)}) collective-permute-start(bf16[128,384]{1,0:T(8,128)(2,1)S(1)} %pad_maximum_fusion.8), channel_id=1, source_target_pairs={{0,4},{1,5},{2,6},{3,7},{4,0},{5,1},{6,2},{7,3},{8,12},{9,13},{10,... | collective-permute-start | bytes 294920 | tf_op jit(solution)/shard_map/ppermute | solution.py:905
  49.7 8.3 %collective-permute-start.4 = (bf16[128,384]{1,0:T(8,128)(2,1)S(1)}, bf16[128,384]{1,0:T(8,128)(2,1)S(1)}, u32[]{:S(2)}, u32[]{:S(2)}) collective-permute-start(bf16[128,384]{1,0:T(8,128)(2,1)S(1)} %pad_maximum_fusion.8), channel_id=1, source_target_pairs={{0,8},{1,9},{2,10},{3,11},{4,12},{5,13},{6,14},{7,15},{8,0},{9,1},... | collective-permute-start | bytes 294920 | tf_op jit(solution)/shard_map/ppermute | solution.py:905
  52.0 6.4 %collective-permute-start.5 = (bf16[128,384]{1,0:T(8,128)(2,1)S(1)}, bf16[128,384]{1,0:T(8,128)(2,1)S(1)}, u32[]{:S(2)}, u32[]{:S(2)}) collective-permute-start(bf16[128,384]{1,0:T(8,128)(2,1)S(1)} %pad_maximum_fusion.8), channel_id=1, source_target_pairs={{0,12},{1,13},{2,14},{3,15},{4,8},{5,9},{6,10},{7,11},{8,4},{9,5},... | collective-permute-start | bytes 294920 | tf_op jit(solution)/shard_map/ppermute | solution.py:905
  58.5 12.1 %collective-permute-start.8 = (bf16[512,384]{1,0:T(8,128)(2,1)S(1)}, bf16[512,384]{1,0:T(8,128)(2,1)S(1)}, u32[]{:S(2)}, u32[]{:S(2)}) collective-permute-start(bf16[512,384]{1,0:T(8,128)(2,1)S(1)} %constant_dynamic-update-slice_fusion.refs_2_), channel_id=1, source_target_pairs={{0,2},{1,3},{2,0},{3,1},{4,6},{5,7},{6,4},{7,5},{8,10},{9,11},{10,... | collective-permute-start | bytes 1179656 | tf_op jit(solution)/shard_map/ppermute | solution.py:905
  59.9 18.7 %collective-permute-start.7 = (bf16[512,384]{1,0:T(8,128)(2,1)S(1)}, bf16[512,384]{1,0:T(8,128)(2,1)S(1)}, u32[]{:S(2)}, u32[]{:S(2)}) collective-permute-start(bf16[512,384]{1,0:T(8,128)(2,1)S(1)} %constant_dynamic-update-slice_fusion.refs_2_), channel_id=1, source_target_pairs={{0,1},{1,0},{2,3},{3,2},{4,5},{5,4},{6,7},{7,6},{8,9},{9,8},{10,11... | collective-permute-start | bytes 1179656 | tf_op jit(solution)/shard_map/ppermute | solution.py:905
  70.6 8.0 %collective-permute-start.9 = (bf16[512,384]{1,0:T(8,128)(2,1)S(1)}, bf16[512,384]{1,0:T(8,128)(2,1)S(1)}, u32[]{:S(2)}, u32[]{:S(2)}) collective-permute-start(bf16[512,384]{1,0:T(8,128)(2,1)S(1)} %collective-permute-done.8.refs_4_), channel_id=1, source_target_pairs={{0,1},{1,0},{2,3},{3,2},{4,5},{5,4},{6,7},{7,6},{8,9},{9,8},{10,11... | collective-permute-start | bytes 1179656 | tf_op jit(solution)/shard_map/ppermute | solution.py:905
  70.8 7.8 %collective-permute-start.6 = (bf16[128,384]{1,0:T(8,128)(2,1)S(1)}, bf16[128,384]{1,0:T(8,128)(2,1)S(1)}, u32[]{:S(2)}, u32[]{:S(2)}) collective-permute-start(bf16[128,384]{1,0:T(8,128)(2,1)S(1)} %get-tuple-element.85.refs_0_), channel_id=1, source_target_pairs={{0,16},{16,0},{1,17},{17,1},{2,18},{18,2},{3,19},{19,3},{4,20},{20... | collective-permute-start | bytes 294920 | tf_op jit(solution)/shard_map/ppermute | solution.py:905
  86.0 4.9 %collective-permute-start.12 = (f32[16,128]{1,0:T(8,128)S(1)}, f32[16,128]{1,0:T(8,128)S(1)}, u32[]{:S(2)}, u32[]{:S(2)}) collective-permute-start(f32[16,128]{1,0:T(8,128)S(1)} %add.132), channel_id=1, source_target_pairs={{0,1},{1,0},{2,3},{3,2},{4,5},{5,4},{6,7},{7,6},{8,9},{9,8},{10,11... | collective-permute-start | bytes 24584 | tf_op jit(solution)/shard_map/ppermute | solution.py:905
  117.6 9.5 %collective-permute-start.36 = (bf16[768,384]{1,0:T(8,128)(2,1)}, bf16[768,384]{1,0:T(8,128)(2,1)S(1)}, u32[]{:S(2)}, u32[]{:S(2)}) collective-permute-start(bf16[768,384]{1,0:T(8,128)(2,1)} %get-tuple-element.111), channel_id=1, source_target_pairs={{0,1},{1,0},{2,3},{3,2},{4,5},{5,4},{6,7},{7,6},{8,9},{9,8},{10,11... | collective-permute-start | bytes 1769480 | tf_op jit(solution)/shard_map/ppermute | solution.py:905
  118.9 9.7 %collective-permute-start.27 = (bf16[768,384]{1,0:T(8,128)(2,1)}, bf16[768,384]{1,0:T(8,128)(2,1)S(1)}, u32[]{:S(2)}, u32[]{:S(2)}) collective-permute-start(bf16[768,384]{1,0:T(8,128)(2,1)} %get-tuple-element.106), channel_id=1, source_target_pairs={{0,1},{1,0},{2,3},{3,2},{4,5},{5,4},{6,7},{7,6},{8,9},{9,8},{10,11... | collective-permute-start | bytes 1769480 | tf_op jit(solution)/shard_map/ppermute | solution.py:905
  120.0 44.1 %collective-permute-start.22 = (bf16[32,16,384]{2,1,0:T(8,128)(2,1)S(1)}, bf16[32,16,384]{2,1,0:T(8,128)(2,1)S(1)}, u32[]{:S(2)}, u32[]{:S(2)}) collective-permute-start(bf16[32,16,384]{2,1,0:T(8,128)(2,1)S(1)} %slice.40), channel_id=1, source_target_pairs={{0,16},{16,0},{1,17},{17,1},{2,18},{18,2},{3,19},{19,3},{4,20},{20... | collective-permute-start | bytes 1179656 | tf_op jit(solution)/shard_map/ppermute | solution.py:905
  127.3 8.7 %collective-permute-start.37 = (bf16[384,384]{1,0:T(8,128)(2,1)S(1)}, bf16[384,384]{1,0:T(8,128)(2,1)S(1)}, u32[]{:S(2)}, u32[]{:S(2)}) collective-permute-start(bf16[384,384]{1,0:T(8,128)(2,1)S(1)} %fusion.2), channel_id=1, source_target_pairs={{0,2},{1,3},{2,0},{3,1},{4,6},{5,7},{6,4},{7,5},{8,10},{9,11},{10,... | collective-permute-start | bytes 884744 | tf_op jit(solution)/shard_map/ppermute | solution.py:905
  128.8 8.4 %collective-permute-start.28 = (bf16[384,384]{1,0:T(8,128)(2,1)S(1)}, bf16[384,384]{1,0:T(8,128)(2,1)S(1)}, u32[]{:S(2)}, u32[]{:S(2)}) collective-permute-start(bf16[384,384]{1,0:T(8,128)(2,1)S(1)} %fusion.1), channel_id=1, source_target_pairs={{0,4},{1,5},{2,6},{3,7},{4,0},{5,1},{6,2},{7,3},{8,12},{9,13},{10,... | collective-permute-start | bytes 884744 | tf_op jit(solution)/shard_map/ppermute | solution.py:905
  130.1 20.6 %collective-permute-start.18 = (bf16[512,384]{1,0:T(8,128)(2,1)S(1)}, bf16[512,384]{1,0:T(8,128)(2,1)S(1)}, u32[]{:S(2)}, u32[]{:S(2)}) collective-permute-start(bf16[512,384]{1,0:T(8,128)(2,1)S(1)} %fusion), channel_id=1, source_target_pairs={{0,16},{16,0},{1,17},{17,1},{2,18},{18,2},{3,19},{19,3},{4,20},{20... | collective-permute-start | bytes 1179656 | tf_op jit(solution)/shard_map/ppermute | solution.py:905
  137.3 9.8 %collective-permute-start.29 = (bf16[192,384]{1,0:T(8,128)(2,1)S(1)}, bf16[192,384]{1,0:T(8,128)(2,1)S(1)}, u32[]{:S(2)}, u32[]{:S(2)}) collective-permute-start(bf16[192,384]{1,0:T(8,128)(2,1)S(1)} %fusion.5), channel_id=1, source_target_pairs={{0,16},{16,0},{1,17},{17,1},{2,18},{18,2},{3,19},{19,3},{4,20},{20... | collective-permute-start | bytes 442376 | tf_op jit(solution)/shard_map/ppermute | solution.py:905
  140.8 7.9 %collective-permute-start.39 = (bf16[96,384]{1,0:T(8,128)(2,1)S(1)}, bf16[96,384]{1,0:T(8,128)(2,1)S(1)}, u32[]{:S(2)}, u32[]{:S(2)}) collective-permute-start(bf16[96,384]{1,0:T(8,128)(2,1)S(1)} %fusion.11), channel_id=1, source_target_pairs={{0,16},{16,0},{1,17},{17,1},{2,18},{18,2},{3,19},{19,3},{4,20},{20... | collective-permute-start | bytes 221192 | tf_op jit(solution)/shard_map/ppermute | solution.py:905
  147.2 5.0 %collective-permute-start.30 = (bf16[96,384]{1,0:T(8,128)(2,1)S(1)}, bf16[96,384]{1,0:T(8,128)(2,1)S(1)}, u32[]{:S(2)}, u32[]{:S(2)}) collective-permute-start(bf16[96,384]{1,0:T(8,128)(2,1)S(1)} %fusion.10), channel_id=1, source_target_pairs={{0,2},{1,3},{2,0},{3,1},{4,6},{5,7},{6,4},{7,5},{8,10},{9,11},{10,... | collective-permute-start | bytes 221192 | tf_op jit(solution)/shard_map/ppermute | solution.py:905
  148.7 8.6 %collective-permute-start.40 = (bf16[96,384]{1,0:T(8,128)(2,1)S(1)}, bf16[96,384]{1,0:T(8,128)(2,1)S(1)}, u32[]{:S(2)}, u32[]{:S(2)}) collective-permute-start(bf16[96,384]{1,0:T(8,128)(2,1)S(1)} %fusion.7), channel_id=1, source_target_pairs={{0,8},{1,9},{2,10},{3,11},{4,12},{5,13},{6,14},{7,15},{8,0},{9,1},... | collective-permute-start | bytes 221192 | tf_op jit(solution)/shard_map/ppermute | solution.py:905
  152.2 9.3 %collective-permute-start.31 = (bf16[96,384]{1,0:T(8,128)(2,1)S(1)}, bf16[96,384]{1,0:T(8,128)(2,1)S(1)}, u32[]{:S(2)}, u32[]{:S(2)}) collective-permute-start(bf16[96,384]{1,0:T(8,128)(2,1)S(1)} %fusion.8), channel_id=1, source_target_pairs={{0,8},{1,9},{2,10},{3,11},{4,12},{5,13},{6,14},{7,15},{8,0},{9,1},... | collective-permute-start | bytes 221192 | tf_op jit(solution)/shard_map/ppermute | solution.py:905
  157.3 8.4 %collective-permute-start.41 = (bf16[96,384]{1,0:T(8,128)(2,1)S(1)}, bf16[96,384]{1,0:T(8,128)(2,1)S(1)}, u32[]{:S(2)}, u32[]{:S(2)}) collective-permute-start(bf16[96,384]{1,0:T(8,128)(2,1)S(1)} %add_convert_fusion.1), channel_id=1, source_target_pairs={{0,16},{16,0},{1,17},{17,1},{2,18},{18,2},{3,19},{19,3},{4,20},{20... | collective-permute-start | bytes 221192 | tf_op jit(solution)/shard_map/ppermute | solution.py:905
  161.5 8.8 %collective-permute-start.32 = (bf16[96,384]{1,0:T(8,128)(2,1)S(1)}, bf16[96,384]{1,0:T(8,128)(2,1)S(1)}, u32[]{:S(2)}, u32[]{:S(2)}) collective-permute-start(bf16[96,384]{1,0:T(8,128)(2,1)S(1)} %add_convert_fusion.2), channel_id=1, source_target_pairs={{0,2},{1,3},{2,0},{3,1},{4,6},{5,7},{6,4},{7,5},{8,10},{9,11},{10,... | collective-permute-start | bytes 221192 | tf_op jit(solution)/shard_map/ppermute | solution.py:905
  165.8 5.5 %collective-permute-start.42 = (bf16[192,384]{1,0:T(8,128)(2,1)S(1)}, bf16[192,384]{1,0:T(8,128)(2,1)S(1)}, u32[]{:S(2)}, u32[]{:S(2)}) collective-permute-start(bf16[192,384]{1,0:T(8,128)(2,1)S(1)} %pad_maximum_fusion.7), channel_id=1, source_target_pairs={{0,4},{1,5},{2,6},{3,7},{4,0},{5,1},{6,2},{7,3},{8,12},{9,13},{10,... | collective-permute-start | bytes 442376 | tf_op jit(solution)/shard_map/ppermute | solution.py:905
  168.9 4.9 %collective-permute-start.24 = (bf16[256,384]{1,0:T(8,128)(2,1)S(1)}, bf16[256,384]{1,0:T(8,128)(2,1)S(1)}, u32[]{:S(2)}, u32[]{:S(2)}) collective-permute-start(bf16[256,384]{1,0:T(8,128)(2,1)S(1)} %pad_maximum_fusion.5), channel_id=1, source_target_pairs={{0,2},{1,3},{2,0},{3,1},{4,6},{5,7},{6,4},{7,5},{8,10},{9,11},{10,... | collective-permute-start | bytes 589832 | tf_op jit(solution)/shard_map/ppermute | solution.py:905
  171.4 17.7 %collective-permute-start.43 = (bf16[384,384]{1,0:T(8,128)(2,1)S(1)}, bf16[384,384]{1,0:T(8,128)(2,1)S(1)}, u32[]{:S(2)}, u32[]{:S(2)}) collective-permute-start(bf16[384,384]{1,0:T(8,128)(2,1)S(1)} %pad_maximum_fusion.4), channel_id=1, source_target_pairs={{0,2},{1,3},{2,0},{3,1},{4,6},{5,7},{6,4},{7,5},{8,10},{9,11},{10,... | collective-permute-start | bytes 884744 | tf_op jit(solution)/shard_map/ppermute | solution.py:905
  173.8 8.6 %collective-permute-start.25 = (bf16[512,384]{1,0:T(8,128)(2,1)S(1)}, bf16[512,384]{1,0:T(8,128)(2,1)S(1)}, u32[]{:S(2)}, u32[]{:S(2)}) collective-permute-start(bf16[512,384]{1,0:T(8,128)(2,1)S(1)} %pad_maximum_fusion.2), channel_id=1, source_target_pairs={{0,16},{16,0},{1,17},{17,1},{2,18},{18,2},{3,19},{19,3},{4,20},{20... | collective-permute-start | bytes 1179656 | tf_op jit(solution)/shard_map/ppermute | solution.py:905
  174.5 14.7 %collective-permute-start.34 = (bf16[384,384]{1,0:T(8,128)(2,1)S(1)}, bf16[384,384]{1,0:T(8,128)(2,1)S(1)}, u32[]{:S(2)}, u32[]{:S(2)}) collective-permute-start(bf16[384,384]{1,0:T(8,128)(2,1)S(1)} %pad_maximum_fusion.3), channel_id=1, source_target_pairs={{0,4},{1,5},{2,6},{3,7},{4,0},{5,1},{6,2},{7,3},{8,12},{9,13},{10,... | collective-permute-start | bytes 884744 | tf_op jit(solution)/shard_map/ppermute | solution.py:905
  182.4 17.6 %collective-permute-start.26 = (bf16[1024,384]{1,0:T(8,128)(2,1)S(1)}, bf16[1024,384]{1,0:T(8,128)(2,1)S(1)}, u32[]{:S(2)}, u32[]{:S(2)}) collective-permute-start(bf16[1024,384]{1,0:T(8,128)(2,1)S(1)} %constant_dynamic-update-slice_fusion.4.own_ref), channel_id=1, source_target_pairs={{0,1},{1,0},{2,3},{3,2},{4,5},{5,4},{6,7},{7,6},{8,9},{9,8},{10,11... | collective-permute-start | bytes 2359304 | tf_op jit(solution)/shard_map/ppermute | solution.py:905
  189.1 4.8 %collective-permute-start.44 = (bf16[768,384]{1,0:T(8,128)(2,1)S(1)}, bf16[768,384]{1,0:T(8,128)(2,1)}, u32[]{:S(2)}, u32[]{:S(2)}) collective-permute-start(bf16[768,384]{1,0:T(8,128)(2,1)S(1)} %pad_maximum_fusion.1.own_ref), channel_id=1, source_target_pairs={{0,1},{1,0},{2,3},{3,2},{4,5},{5,4},{6,7},{7,6},{8,9},{9,8},{10,11... | collective-permute-start | bytes 1769480 | tf_op jit(solution)/shard_map/ppermute | solution.py:905
  189.3 7.9 %collective-permute-start.35 = (bf16[768,384]{1,0:T(8,128)(2,1)S(1)}, bf16[768,384]{1,0:T(8,128)(2,1)S(1)}, u32[]{:S(2)}, u32[]{:S(2)}) collective-permute-start(bf16[768,384]{1,0:T(8,128)(2,1)S(1)} %pad_maximum_fusion.own_ref), channel_id=1, source_target_pairs={{0,1},{1,0},{2,3},{3,2},{4,5},{5,4},{6,7},{7,6},{8,9},{9,8},{10,11... | collective-permute-start | bytes 1769480 | tf_op jit(solution)/shard_map/ppermute | solution.py:905
  (31 other events, 269.8 us)

commit v5 on v4

--- a/solution.py
+++ b/solution.py
@@ -171,7 +171,7 @@
 
     largest = jnp.zeros((slots, 2 * slots), F32)
     units = [(p, h) for p in range(GROUP) for h in range(tiles)]
-    ahead = 6
+    ahead = 4
     feed = iter(())
     projected(0)
     for g in range(groups):

time: 204 us -> 203 us (level)
  no operation moved by 1% of the time
where the time goes in v5:
time: 203 us
  Pallas kernels  80.3 us (40%)
  starting transfers between devices  64.3 us (32%)
  waiting for transfers between devices  44.9 us (22%)
  local copies, waits for them, and re-layouts  5.36 us (3%)
  between operations  3.97 us (2%)
  other arithmetic  3.85 us (2%)
    ppermute x45, starting transfers between devices, flip(): return lax.ppermute(values, axis, [(k, k ^ bits) for k in range(size)])  64.3 us
    ppermute x45, waiting for transfers between devices, flip(): return lax.ppermute(values, axis, [(k, k ^ bits) for k in range(size)])  44.9 us
    pallas_call x2, Pallas kernels, image_tower(): pl.pallas_call(kernel, grid_spec=pltpu.PrefetchScalarGridSpec(num_scalar_...  34.2 us
    pallas_call x1, Pallas kernels, text_backward(): pl.pallas_call(functools.partial(back_kernel, cut, len(others)), grid_spe...  18.6 us
    pallas_call x3, Pallas kernels, place(): pl.pallas_call(functools.partial(place_kernel, targets, rounds, last), in...  9.23 us
    pallas_call x1, Pallas kernels, text_second(): pl.pallas_call(functools.partial(text_second_kernel, cut), grid_spec=pltp...  7.05 us
    pallas_call x1, Pallas kernels, text_first(): pl.pallas_call(functools.partial(text_first_kernel, cut), grid_spec=pltpu...  5.92 us
  transfers between devices with their start and end apart: 45, of which 18 were waited for; matrix products, arithmetic and copies ran while one was open for 4% of the time, Pallas kernels for 27%

profile of v5, /device:TPU:1, one launch (start us, length us, event | category | flops | bytes accessed | tf_op | source)
XLA Modules:
  0.0 202.7 jit_solution(15010563896613422681)
XLA Ops:
  2.2 2.1 %collective-permute-start.2 = (bf16[50,32,384]{2,1,0:T(8,128)(2,1)S(1)}, bf16[50,32,384]{2,1,0:T(8,128)(2,1)}, u32[]{:S(2)}, u32[]{:S(2)}) collective-permute-start(bf16[50,32,384]{2,1,0:T(8,128)(2,1)S(1)} %slice.41), channel_id=1, source_target_pairs={{0,16},{16,0},{1,17},{17,1},{2,18},{18,2},{3,19},{19,3},{4,20},{20... | collective-permute-start | bytes 3686408 | tf_op jit(solution)/shard_map/ppermute | solution.py:905
  8.9 17.8 %image_block.3 = bf16[96,384]{1,0:T(8,128)(2,1)} custom-call(s32[28]{0:T(128)S(1)} %get-tuple-element.76.plan_ref.ids_ref, bf16[50,128,384]{2,1,0:T(8,128)(2,1)} %bitcast.56, bf16[384,1152]{1,0:T(8,128)(2,1)} %refs_0_.1, bf16[384,384]{1,0:T(8,128)(2,1)S(1)} %copy-done.13, bf16[384,1536]{1,0:T(8,128)(2,1)} %refs_2_.1, bf16[1536,384]{1,0:T(8,128)(2,1)} %refs_3_.1, ...), custom_call_target="tpu_custom_call" | custom-call | flops 11324620800 | bytes 7880704 | tf_op jit(solution)/shard_map/image_block/pallas_call | solution.py:247
  28.0 3.2 %collective-permute-done.2 = bf16[50,32,384]{2,1,0:T(8,128)(2,1)} collective-permute-done((bf16[50,32,384]{2,1,0:T(8,128)(2,1)S(1)}, bf16[50,32,384]{2,1,0:T(8,128)(2,1)}, u32[]{:S(2)}, u32[]{:S(2)}) %collective-permute-start.2) | collective-permute-done | bytes 1228832 | tf_op jit(solution)/shard_map/ppermute | solution.py:905
  31.2 16.4 %conditional.1 = (bf16[32,384]{1,0:T(8,128)(2,1)S(1)}) conditional(s32[]{:T(128)} %bitcast.1, () %tuple.17, (s32[28]{0:T(128)S(1)}, bf16[50,128,384]{2,1,0:T(8,128)(2,1)}, bf16[50,32,384]{2,1,0:T(8,128)(2,1)}, bf16[384,1152]{1,0:T(8,128)(2,1)}, bf16[384,384]{1,0:T(8,128)(2,1)S(1)}, /*index=5*/bf16[384,1536]{1,0:T(8,128)(2,1)}, ...), branch_computations={%region_0.0_spmd, %region_1.0_spmd} | conditional | flops 37748736 | bytes 54239 | solution.py:1048
  31.2 16.4 %image_block.2 = bf16[32,384]{1,0:T(8,128)(2,1)S(1)} custom-call(s32[28]{0:T(128)S(1)} %get-tuple-element.7.plan_ref, bf16[50,128,384]{2,1,0:T(8,128)(2,1)} %get-tuple-element.20.x_ref, bf16[50,32,384]{2,1,0:T(8,128)(2,1)} %get-tuple-element.21.recv_ref, bf16[384,1152]{1,0:T(8,128)(2,1)} %get-tuple-element.22.wqkv_ref, ...), custom_call_target="tpu_custom_call" | custom-call | flops 37748736 | bytes 54231 | tf_op jit(solution)/shard_map/cond/branch_1_fun/image_block/pallas_call | solution.py:247
  49.8 2.3 %collective-permute-start.4 = (bf16[128,384]{1,0:T(8,128)(2,1)S(1)}, bf16[128,384]{1,0:T(8,128)(2,1)S(1)}, u32[]{:S(2)}, u32[]{:S(2)}) collective-permute-start(bf16[128,384]{1,0:T(8,128)(2,1)S(1)} %pad_maximum_fusion.8), channel_id=1, source_target_pairs={{0,8},{1,9},{2,10},{3,11},{4,12},{5,13},{6,14},{7,15},{8,0},{9,1},... | collective-permute-start | bytes 294920 | tf_op jit(solution)/shard_map/ppermute | solution.py:905
  52.2 5.9 %text_attention.1 = (bf16[2048,1152]{1,0:T(8,128)(2,1)}, bf16[2048,384]{1,0:T(8,128)(2,1)S(1)}, f32[2048,384]{1,0:T(8,128)S(1)}) custom-call(s32[28]{0:T(128)S(1)} %get-tuple-element.76.plan_ref.ids_ref, bf16[128,16,384]{2,1,0:T(8,128)(2,1)S(1)} %copy-done, bf16[32,16,384]{2,1,0:T(8,128)(2,1)S(1)} %collective-permute-done.recv_ref, ...), custom_call_target="tpu_custom_call" | custom-call | flops 3019898880 | bytes 12582912 | tf_op jit(solution)/shard_map/text_attention/pallas_call | solution.py:484
  60.0 3.7 %collective-permute-start.7 = (bf16[512,384]{1,0:T(8,128)(2,1)S(1)}, bf16[512,384]{1,0:T(8,128)(2,1)S(1)}, u32[]{:S(2)}, u32[]{:S(2)}) collective-permute-start(bf16[512,384]{1,0:T(8,128)(2,1)S(1)} %constant_dynamic-update-slice_fusion.refs_2_), channel_id=1, source_target_pairs={{0,1},{1,0},{2,3},{3,2},{4,5},{5,4},{6,7},{7,6},{8,9},{9,8},{10,11... | collective-permute-start | bytes 1179656 | tf_op jit(solution)/shard_map/ppermute | solution.py:905
  63.7 7.0 %text_pool.1 = (bf16[2048,1536]{1,0:T(8,128)(2,1)S(1)}, f32[128,1536]{1,0:T(8,128)S(1)}, bf16[128,384]{1,0:T(8,128)(2,1)S(1)}, f32[128,384]{1,0:T(8,128)S(1)}, bf16[128,384]{1,0:T(8,128)(2,1)S(1)}) custom-call(s32[28]{0:T(128)S(1)} %get-tuple-element.76.plan_ref.ids_ref, f32[2048,384]{1,0:T(8,128)S(1)} %get-tuple-element.80.y1_ref, ...), custom_call_target="tpu_custom_call" | custom-call | flops 2415919104 | bytes 12582912 | tf_op jit(solution)/shard_map/text_pool/pallas_call | solution.py:561
  70.9 4.4 %collective-permute-start.6 = (bf16[128,384]{1,0:T(8,128)(2,1)S(1)}, bf16[128,384]{1,0:T(8,128)(2,1)S(1)}, u32[]{:S(2)}, u32[]{:S(2)}) collective-permute-start(bf16[128,384]{1,0:T(8,128)(2,1)S(1)} %get-tuple-element.85.refs_0_), channel_id=1, source_target_pairs={{0,16},{16,0},{1,17},{17,1},{2,18},{18,2},{3,19},{19,3},{4,20},{20... | collective-permute-start | bytes 294920 | tf_op jit(solution)/shard_map/ppermute | solution.py:905
  75.2 2.8 %collective-permute-done.6.refs_1_ = bf16[128,384]{1,0:T(8,128)(2,1)S(1)} collective-permute-done((bf16[128,384]{1,0:T(8,128)(2,1)S(1)}, bf16[128,384]{1,0:T(8,128)(2,1)S(1)}, u32[]{:S(2)}, u32[]{:S(2)}) %collective-permute-start.6) | collective-permute-done | bytes 98336 | tf_op jit(solution)/shard_map/ppermute | solution.py:905
  82.1 2.2 %collective-permute-start.11 = (f32[16,128]{1,0:T(8,128)S(1)}, f32[16,128]{1,0:T(8,128)S(1)}, u32[]{:S(2)}, u32[]{:S(2)}) collective-permute-start(f32[16,128]{1,0:T(8,128)S(1)} %add.131), channel_id=1, source_target_pairs={{0,8},{1,9},{2,10},{3,11},{4,12},{5,13},{6,14},{7,15},{8,0},{9,1},... | collective-permute-start | bytes 24584 | tf_op jit(solution)/shard_map/ppermute | solution.py:905
  85.5 3.2 %collective-permute-start.12 = (f32[16,128]{1,0:T(8,128)S(1)}, f32[16,128]{1,0:T(8,128)S(1)}, u32[]{:S(2)}, u32[]{:S(2)}) collective-permute-start(f32[16,128]{1,0:T(8,128)S(1)} %add.132), channel_id=1, source_target_pairs={{0,1},{1,0},{2,3},{3,2},{4,5},{5,4},{6,7},{7,6},{8,9},{9,8},{10,11... | collective-permute-start | bytes 24584 | tf_op jit(solution)/shard_map/ppermute | solution.py:905
  88.8 1.6 collective-permute-start.14
  92.0 2.4 %similarity_grads.1 = (f32[128,384]{1,0:T(8,128)S(1)}, bf16[128,384]{1,0:T(8,128)(2,1)S(1)}, f32[8,128]{1,0:T(8,128)S(1)}) custom-call(s32[28]{0:T(128)S(1)} %get-tuple-element.76.plan_ref.ids_ref, f32[8,128]{1,0:T(8,128)S(1)} %copy-done.2, f32[2,128]{1,0:T(2,128)S(1)} %copy-done.3, f32[16,128]{1,0:T(8,128)S(1)} %copy-done.1, ...), custom_call_target="tpu_custom_call" | custom-call | flops 805306368 | bytes 1572864 | tf_op jit(solution)/shard_map/similarity_grads/pallas_call | solution.py:666
  95.9 2.5 %collective-permute-done.16.refs_0_ = bf16[128,384]{1,0:T(8,128)(2,1)S(1)} collective-permute-done((bf16[128,384]{1,0:T(8,128)(2,1)S(1)}, bf16[128,384]{1,0:T(8,128)(2,1)S(1)}, u32[]{:S(2)}, u32[]{:S(2)}) %collective-permute-start.16) | collective-permute-done | bytes 98336 | tf_op jit(solution)/shard_map/ppermute | solution.py:905
  98.5 18.6 %text_backward.1 = (bf16[128,16,384]{2,1,0:T(8,128)(2,1)}, bf16[1024,384]{1,0:T(8,128)(2,1)}, bf16[1024,384]{1,0:T(8,128)(2,1)}, bf16[768,384]{1,0:T(8,128)(2,1)...) custom-call(s32[28]{0:T(128)S(1)} %get-tuple-element.76.plan_ref.ids_ref, ...), custom_call_target="tpu_custom_call" | custom-call | flops 10871635968 | bytes 25165824 | tf_op jit(solution)/shard_map/text_backward/pallas_call | solution.py:872
  119.5 6.4 %collective-permute-start.22 = (bf16[32,16,384]{2,1,0:T(8,128)(2,1)S(1)}, bf16[32,16,384]{2,1,0:T(8,128)(2,1)S(1)}, u32[]{:S(2)}, u32[]{:S(2)}) collective-permute-start(bf16[32,16,384]{2,1,0:T(8,128)(2,1)S(1)} %slice.40), channel_id=1, source_target_pairs={{0,16},{16,0},{1,17},{17,1},{2,18},{18,2},{3,19},{19,3},{4,20},{20... | collective-permute-start | bytes 1179656 | tf_op jit(solution)/shard_map/ppermute | solution.py:905
  129.6 5.8 %collective-permute-done.37 = bf16[384,384]{1,0:T(8,128)(2,1)S(1)} collective-permute-done((bf16[384,384]{1,0:T(8,128)(2,1)S(1)}, bf16[384,384]{1,0:T(8,128)(2,1)S(1)}, u32[]{:S(2)}, u32[]{:S(2)}) %collective-permute-start.37) | collective-permute-done | bytes 294944 | tf_op jit(solution)/shard_map/ppermute | solution.py:905
  136.8 3.3 %collective-permute-done.38 = bf16[192,384]{1,0:T(8,128)(2,1)S(1)} collective-permute-done((bf16[192,384]{1,0:T(8,128)(2,1)S(1)}, bf16[192,384]{1,0:T(8,128)(2,1)S(1)}, u32[]{:S(2)}, u32[]{:S(2)}) %collective-permute-start.38) | collective-permute-done | bytes 147488 | tf_op jit(solution)/shard_map/ppermute | solution.py:905
  140.3 6.2 %collective-permute-done.29 = bf16[192,384]{1,0:T(8,128)(2,1)S(1)} collective-permute-done((bf16[192,384]{1,0:T(8,128)(2,1)S(1)}, bf16[192,384]{1,0:T(8,128)(2,1)S(1)}, u32[]{:S(2)}, u32[]{:S(2)}) %collective-permute-start.29) | collective-permute-done | bytes 147488 | tf_op jit(solution)/shard_map/ppermute | solution.py:905
  148.2 2.0 collective-permute-start.40
  152.2 3.0 %collective-permute-done.19 = bf16[256,384]{1,0:T(8,128)(2,1)S(1)} collective-permute-done((bf16[256,384]{1,0:T(8,128)(2,1)S(1)}, bf16[256,384]{1,0:T(8,128)(2,1)S(1)}, u32[]{:S(2)}, u32[]{:S(2)}) %collective-permute-start.19) | collective-permute-done | bytes 196640 | tf_op jit(solution)/shard_map/ppermute | solution.py:905
  159.1 1.8 collective-permute-start.21
  165.3 2.9 %collective-permute-done.23 = bf16[128,384]{1,0:T(8,128)(2,1)S(1)} collective-permute-done((bf16[128,384]{1,0:T(8,128)(2,1)S(1)}, bf16[128,384]{1,0:T(8,128)(2,1)S(1)}, u32[]{:S(2)}, u32[]{:S(2)}) %collective-permute-start.23) | collective-permute-done | bytes 98336 | tf_op jit(solution)/shard_map/ppermute | solution.py:905
  171.3 1.8 collective-permute-done.24
  175.2 6.5 %collective-permute-done.25 = bf16[512,384]{1,0:T(8,128)(2,1)S(1)} collective-permute-done((bf16[512,384]{1,0:T(8,128)(2,1)S(1)}, bf16[512,384]{1,0:T(8,128)(2,1)S(1)}, u32[]{:S(2)}, u32[]{:S(2)}) %collective-permute-start.25) | collective-permute-done | bytes 393248 | tf_op jit(solution)/shard_map/ppermute | solution.py:905
  181.8 6.6 %collective-permute-start.26 = (bf16[1024,384]{1,0:T(8,128)(2,1)S(1)}, bf16[1024,384]{1,0:T(8,128)(2,1)S(1)}, u32[]{:S(2)}, u32[]{:S(2)}) collective-permute-start(bf16[1024,384]{1,0:T(8,128)(2,1)S(1)} %constant_dynamic-update-slice_fusion.4.own_ref), channel_id=1, source_target_pairs={{0,1},{1,0},{2,3},{3,2},{4,5},{5,4},{6,7},{7,6},{8,9},{9,8},{10,11... | collective-permute-start | bytes 2359304 | tf_op jit(solution)/shard_map/ppermute | solution.py:905
  191.4 1.9 select_dynamic-update-slice_fusion
  193.2 3.3 %place_gradients.5 = f32[384,1536]{1,0:T(8,128)} custom-call(s32[28]{0:T(128)S(1)} %get-tuple-element.76.plan_ref.ids_ref, bf16[768,384]{1,0:T(8,128)(2,1)S(1)} %pad_maximum_fusion.1.own_ref, bf16[768,384]{1,0:T(8,128)(2,1)} %collective-permute-done.44.other_ref), custom_call_target="tpu_custom_call" | custom-call | tf_op jit(solution)/shard_map/place_gradients/pallas_call | solution.py:1012
  196.6 2.8 %place_gradients.4 = (f32[384,384]{1,0:T(8,128)}, f32[384,1152]{1,0:T(8,128)}) custom-call(s32[28]{0:T(128)S(1)} %get-tuple-element.76.plan_ref.ids_ref, bf16[768,384]{1,0:T(8,128)(2,1)S(1)} %pad_maximum_fusion.own_ref, bf16[768,384]{1,0:T(8,128)(2,1)S(1)} %collective-permute-done.35.other_ref), custom_call_target="tpu_custom_call" | custom-call | tf_op jit(solution)/shard_map/place_gradients/pallas_call | solution.py:1012
  199.4 3.1 %place_gradients.3 = (f32[1536,384]{1,0:T(8,128)}, f32[384,384]{1,0:T(8,128)}, f32[384]{0:T(512)}, f32[384]{0:T(512)}, f32[1]{0:T(128)}, /*index=5*/f32[1]{0:T(128)}) custom-call(s32[28]{0:T(128)S(1)} %get-tuple-element.76.plan_ref.ids_ref, bf16[1024,384]{1,0:T(8,128)(2,1)S(1)} %constant_dynamic-update-slice_fusion.4.own_ref, ...), custom_call_target="tpu_custom_call" | custom-call | tf_op jit(solution)/shard_map/place_gradients/pallas_call | solution.py:1012
  (164 shorter events, 44.8 us)
Async XLA Ops:
  2.2 29.0 %collective-permute-start.2 = (bf16[50,32,384]{2,1,0:T(8,128)(2,1)S(1)}, bf16[50,32,384]{2,1,0:T(8,128)(2,1)}, u32[]{:S(2)}, u32[]{:S(2)}) collective-permute-start(bf16[50,32,384]{2,1,0:T(8,128)(2,1)S(1)} %slice.41), channel_id=1, source_target_pairs={{0,16},{16,0},{1,17},{17,1},{2,18},{18,2},{3,19},{19,3},{4,20},{20... | collective-permute-start | bytes 3686408 | tf_op jit(solution)/shard_map/ppermute | solution.py:905
  4.5 47.6 %collective-permute-start.1 = (f32[2,16]{1,0:T(2,128)S(1)}, f32[2,16]{1,0:T(2,128)S(1)}, u32[]{:S(2)}, u32[]{:S(2)}) collective-permute-start(f32[2,16]{1,0:T(2,128)S(1)} %slice.35), channel_id=1, source_target_pairs={{0,16},{16,0},{1,17},{17,1},{2,18},{18,2},{3,19},{19,3},{4,20},{20... | collective-permute-start | bytes 392 | tf_op jit(solution)/shard_map/ppermute | solution.py:905
  5.3 46.8 %collective-permute-start = (bf16[32,16,384]{2,1,0:T(8,128)(2,1)}, bf16[32,16,384]{2,1,0:T(8,128)(2,1)S(1)}, u32[]{:S(2)}, u32[]{:S(2)}) collective-permute-start(bf16[32,16,384]{2,1,0:T(8,128)(2,1)} %slice.33), channel_id=1, source_target_pairs={{0,16},{16,0},{1,17},{17,1},{2,18},{18,2},{3,19},{19,3},{4,20},{20... | collective-permute-start | bytes 1179656 | tf_op jit(solution)/shard_map/ppermute | solution.py:905
  48.5 9.6 %collective-permute-start.3 = (bf16[128,384]{1,0:T(8,128)(2,1)S(1)}, bf16[128,384]{1,0:T(8,128)(2,1)S(1)}, u32[]{:S(2)}, u32[]{:S(2)}) collective-permute-start(bf16[128,384]{1,0:T(8,128)(2,1)S(1)} %pad_maximum_fusion.8), channel_id=1, source_target_pairs={{0,4},{1,5},{2,6},{3,7},{4,0},{5,1},{6,2},{7,3},{8,12},{9,13},{10,... | collective-permute-start | bytes 294920 | tf_op jit(solution)/shard_map/ppermute | solution.py:905
  49.8 8.3 %collective-permute-start.4 = (bf16[128,384]{1,0:T(8,128)(2,1)S(1)}, bf16[128,384]{1,0:T(8,128)(2,1)S(1)}, u32[]{:S(2)}, u32[]{:S(2)}) collective-permute-start(bf16[128,384]{1,0:T(8,128)(2,1)S(1)} %pad_maximum_fusion.8), channel_id=1, source_target_pairs={{0,8},{1,9},{2,10},{3,11},{4,12},{5,13},{6,14},{7,15},{8,0},{9,1},... | collective-permute-start | bytes 294920 | tf_op jit(solution)/shard_map/ppermute | solution.py:905
  52.1 6.4 %collective-permute-start.5 = (bf16[128,384]{1,0:T(8,128)(2,1)S(1)}, bf16[128,384]{1,0:T(8,128)(2,1)S(1)}, u32[]{:S(2)}, u32[]{:S(2)}) collective-permute-start(bf16[128,384]{1,0:T(8,128)(2,1)S(1)} %pad_maximum_fusion.8), channel_id=1, source_target_pairs={{0,12},{1,13},{2,14},{3,15},{4,8},{5,9},{6,10},{7,11},{8,4},{9,5},... | collective-permute-start | bytes 294920 | tf_op jit(solution)/shard_map/ppermute | solution.py:905
  58.6 12.1 %collective-permute-start.8 = (bf16[512,384]{1,0:T(8,128)(2,1)S(1)}, bf16[512,384]{1,0:T(8,128)(2,1)S(1)}, u32[]{:S(2)}, u32[]{:S(2)}) collective-permute-start(bf16[512,384]{1,0:T(8,128)(2,1)S(1)} %constant_dynamic-update-slice_fusion.refs_2_), channel_id=1, source_target_pairs={{0,2},{1,3},{2,0},{3,1},{4,6},{5,7},{6,4},{7,5},{8,10},{9,11},{10,... | collective-permute-start | bytes 1179656 | tf_op jit(solution)/shard_map/ppermute | solution.py:905
  60.0 18.1 %collective-permute-start.7 = (bf16[512,384]{1,0:T(8,128)(2,1)S(1)}, bf16[512,384]{1,0:T(8,128)(2,1)S(1)}, u32[]{:S(2)}, u32[]{:S(2)}) collective-permute-start(bf16[512,384]{1,0:T(8,128)(2,1)S(1)} %constant_dynamic-update-slice_fusion.refs_2_), channel_id=1, source_target_pairs={{0,1},{1,0},{2,3},{3,2},{4,5},{5,4},{6,7},{7,6},{8,9},{9,8},{10,11... | collective-permute-start | bytes 1179656 | tf_op jit(solution)/shard_map/ppermute | solution.py:905
  70.7 7.3 %collective-permute-start.9 = (bf16[512,384]{1,0:T(8,128)(2,1)S(1)}, bf16[512,384]{1,0:T(8,128)(2,1)S(1)}, u32[]{:S(2)}, u32[]{:S(2)}) collective-permute-start(bf16[512,384]{1,0:T(8,128)(2,1)S(1)} %collective-permute-done.8.refs_4_), channel_id=1, source_target_pairs={{0,1},{1,0},{2,3},{3,2},{4,5},{5,4},{6,7},{7,6},{8,9},{9,8},{10,11... | collective-permute-start | bytes 1179656 | tf_op jit(solution)/shard_map/ppermute | solution.py:905
  70.9 7.2 %collective-permute-start.6 = (bf16[128,384]{1,0:T(8,128)(2,1)S(1)}, bf16[128,384]{1,0:T(8,128)(2,1)S(1)}, u32[]{:S(2)}, u32[]{:S(2)}) collective-permute-start(bf16[128,384]{1,0:T(8,128)(2,1)S(1)} %get-tuple-element.85.refs_0_), channel_id=1, source_target_pairs={{0,16},{16,0},{1,17},{17,1},{2,18},{18,2},{3,19},{19,3},{4,20},{20... | collective-permute-start | bytes 294920 | tf_op jit(solution)/shard_map/ppermute | solution.py:905
  85.5 4.9 %collective-permute-start.12 = (f32[16,128]{1,0:T(8,128)S(1)}, f32[16,128]{1,0:T(8,128)S(1)}, u32[]{:S(2)}, u32[]{:S(2)}) collective-permute-start(f32[16,128]{1,0:T(8,128)S(1)} %add.132), channel_id=1, source_target_pairs={{0,1},{1,0},{2,3},{3,2},{4,5},{5,4},{6,7},{7,6},{8,9},{9,8},{10,11... | collective-permute-start | bytes 24584 | tf_op jit(solution)/shard_map/ppermute | solution.py:905
  117.1 9.5 %collective-permute-start.36 = (bf16[768,384]{1,0:T(8,128)(2,1)}, bf16[768,384]{1,0:T(8,128)(2,1)S(1)}, u32[]{:S(2)}, u32[]{:S(2)}) collective-permute-start(bf16[768,384]{1,0:T(8,128)(2,1)} %get-tuple-element.111), channel_id=1, source_target_pairs={{0,1},{1,0},{2,3},{3,2},{4,5},{5,4},{6,7},{7,6},{8,9},{9,8},{10,11... | collective-permute-start | bytes 1769480 | tf_op jit(solution)/shard_map/ppermute | solution.py:905
  118.4 9.7 %collective-permute-start.27 = (bf16[768,384]{1,0:T(8,128)(2,1)}, bf16[768,384]{1,0:T(8,128)(2,1)S(1)}, u32[]{:S(2)}, u32[]{:S(2)}) collective-permute-start(bf16[768,384]{1,0:T(8,128)(2,1)} %get-tuple-element.106), channel_id=1, source_target_pairs={{0,1},{1,0},{2,3},{3,2},{4,5},{5,4},{6,7},{7,6},{8,9},{9,8},{10,11... | collective-permute-start | bytes 1769480 | tf_op jit(solution)/shard_map/ppermute | solution.py:905
  119.5 44.1 %collective-permute-start.22 = (bf16[32,16,384]{2,1,0:T(8,128)(2,1)S(1)}, bf16[32,16,384]{2,1,0:T(8,128)(2,1)S(1)}, u32[]{:S(2)}, u32[]{:S(2)}) collective-permute-start(bf16[32,16,384]{2,1,0:T(8,128)(2,1)S(1)} %slice.40), channel_id=1, source_target_pairs={{0,16},{16,0},{1,17},{17,1},{2,18},{18,2},{3,19},{19,3},{4,20},{20... | collective-permute-start | bytes 1179656 | tf_op jit(solution)/shard_map/ppermute | solution.py:905
  126.8 8.7 %collective-permute-start.37 = (bf16[384,384]{1,0:T(8,128)(2,1)S(1)}, bf16[384,384]{1,0:T(8,128)(2,1)S(1)}, u32[]{:S(2)}, u32[]{:S(2)}) collective-permute-start(bf16[384,384]{1,0:T(8,128)(2,1)S(1)} %fusion.2), channel_id=1, source_target_pairs={{0,2},{1,3},{2,0},{3,1},{4,6},{5,7},{6,4},{7,5},{8,10},{9,11},{10,... | collective-permute-start | bytes 884744 | tf_op jit(solution)/shard_map/ppermute | solution.py:905
  128.3 8.4 %collective-permute-start.28 = (bf16[384,384]{1,0:T(8,128)(2,1)S(1)}, bf16[384,384]{1,0:T(8,128)(2,1)S(1)}, u32[]{:S(2)}, u32[]{:S(2)}) collective-permute-start(bf16[384,384]{1,0:T(8,128)(2,1)S(1)} %fusion.1), channel_id=1, source_target_pairs={{0,4},{1,5},{2,6},{3,7},{4,0},{5,1},{6,2},{7,3},{8,12},{9,13},{10,... | collective-permute-start | bytes 884744 | tf_op jit(solution)/shard_map/ppermute | solution.py:905
  129.6 20.6 %collective-permute-start.18 = (bf16[512,384]{1,0:T(8,128)(2,1)S(1)}, bf16[512,384]{1,0:T(8,128)(2,1)S(1)}, u32[]{:S(2)}, u32[]{:S(2)}) collective-permute-start(bf16[512,384]{1,0:T(8,128)(2,1)S(1)} %fusion), channel_id=1, source_target_pairs={{0,16},{16,0},{1,17},{17,1},{2,18},{18,2},{3,19},{19,3},{4,20},{20... | collective-permute-start | bytes 1179656 | tf_op jit(solution)/shard_map/ppermute | solution.py:905
  136.8 9.8 %collective-permute-start.29 = (bf16[192,384]{1,0:T(8,128)(2,1)S(1)}, bf16[192,384]{1,0:T(8,128)(2,1)S(1)}, u32[]{:S(2)}, u32[]{:S(2)}) collective-permute-start(bf16[192,384]{1,0:T(8,128)(2,1)S(1)} %fusion.5), channel_id=1, source_target_pairs={{0,16},{16,0},{1,17},{17,1},{2,18},{18,2},{3,19},{19,3},{4,20},{20... | collective-permute-start | bytes 442376 | tf_op jit(solution)/shard_map/ppermute | solution.py:905
  140.2 7.9 %collective-permute-start.39 = (bf16[96,384]{1,0:T(8,128)(2,1)S(1)}, bf16[96,384]{1,0:T(8,128)(2,1)S(1)}, u32[]{:S(2)}, u32[]{:S(2)}) collective-permute-start(bf16[96,384]{1,0:T(8,128)(2,1)S(1)} %fusion.11), channel_id=1, source_target_pairs={{0,16},{16,0},{1,17},{17,1},{2,18},{18,2},{3,19},{19,3},{4,20},{20... | collective-permute-start | bytes 221192 | tf_op jit(solution)/shard_map/ppermute | solution.py:905
  146.6 5.0 %collective-permute-start.30 = (bf16[96,384]{1,0:T(8,128)(2,1)S(1)}, bf16[96,384]{1,0:T(8,128)(2,1)S(1)}, u32[]{:S(2)}, u32[]{:S(2)}) collective-permute-start(bf16[96,384]{1,0:T(8,128)(2,1)S(1)} %fusion.10), channel_id=1, source_target_pairs={{0,2},{1,3},{2,0},{3,1},{4,6},{5,7},{6,4},{7,5},{8,10},{9,11},{10,... | collective-permute-start | bytes 221192 | tf_op jit(solution)/shard_map/ppermute | solution.py:905
  148.2 8.6 %collective-permute-start.40 = (bf16[96,384]{1,0:T(8,128)(2,1)S(1)}, bf16[96,384]{1,0:T(8,128)(2,1)S(1)}, u32[]{:S(2)}, u32[]{:S(2)}) collective-permute-start(bf16[96,384]{1,0:T(8,128)(2,1)S(1)} %fusion.7), channel_id=1, source_target_pairs={{0,8},{1,9},{2,10},{3,11},{4,12},{5,13},{6,14},{7,15},{8,0},{9,1},... | collective-permute-start | bytes 221192 | tf_op jit(solution)/shard_map/ppermute | solution.py:905
  150.3 4.9 %collective-permute-start.19 = (bf16[256,384]{1,0:T(8,128)(2,1)S(1)}, bf16[256,384]{1,0:T(8,128)(2,1)S(1)}, u32[]{:S(2)}, u32[]{:S(2)}) collective-permute-start(bf16[256,384]{1,0:T(8,128)(2,1)S(1)} %fusion.3), channel_id=1, source_target_pairs={{0,2},{1,3},{2,0},{3,1},{4,6},{5,7},{6,4},{7,5},{8,10},{9,11},{10,... | collective-permute-start | bytes 589832 | tf_op jit(solution)/shard_map/ppermute | solution.py:905
  151.6 9.3 %collective-permute-start.31 = (bf16[96,384]{1,0:T(8,128)(2,1)S(1)}, bf16[96,384]{1,0:T(8,128)(2,1)S(1)}, u32[]{:S(2)}, u32[]{:S(2)}) collective-permute-start(bf16[96,384]{1,0:T(8,128)(2,1)S(1)} %fusion.8), channel_id=1, source_target_pairs={{0,8},{1,9},{2,10},{3,11},{4,12},{5,13},{6,14},{7,15},{8,0},{9,1},... | collective-permute-start | bytes 221192 | tf_op jit(solution)/shard_map/ppermute | solution.py:905
  156.8 8.4 %collective-permute-start.41 = (bf16[96,384]{1,0:T(8,128)(2,1)S(1)}, bf16[96,384]{1,0:T(8,128)(2,1)S(1)}, u32[]{:S(2)}, u32[]{:S(2)}) collective-permute-start(bf16[96,384]{1,0:T(8,128)(2,1)S(1)} %add_convert_fusion.1), channel_id=1, source_target_pairs={{0,16},{16,0},{1,17},{17,1},{2,18},{18,2},{3,19},{19,3},{4,20},{20... | collective-permute-start | bytes 221192 | tf_op jit(solution)/shard_map/ppermute | solution.py:905
  161.0 8.8 %collective-permute-start.32 = (bf16[96,384]{1,0:T(8,128)(2,1)S(1)}, bf16[96,384]{1,0:T(8,128)(2,1)S(1)}, u32[]{:S(2)}, u32[]{:S(2)}) collective-permute-start(bf16[96,384]{1,0:T(8,128)(2,1)S(1)} %add_convert_fusion.2), channel_id=1, source_target_pairs={{0,2},{1,3},{2,0},{3,1},{4,6},{5,7},{6,4},{7,5},{8,10},{9,11},{10,... | collective-permute-start | bytes 221192 | tf_op jit(solution)/shard_map/ppermute | solution.py:905
  165.2 5.6 %collective-permute-start.42 = (bf16[192,384]{1,0:T(8,128)(2,1)S(1)}, bf16[192,384]{1,0:T(8,128)(2,1)S(1)}, u32[]{:S(2)}, u32[]{:S(2)}) collective-permute-start(bf16[192,384]{1,0:T(8,128)(2,1)S(1)} %pad_maximum_fusion.7), channel_id=1, source_target_pairs={{0,4},{1,5},{2,6},{3,7},{4,0},{5,1},{6,2},{7,3},{8,12},{9,13},{10,... | collective-permute-start | bytes 442376 | tf_op jit(solution)/shard_map/ppermute | solution.py:905
  168.3 4.9 %collective-permute-start.24 = (bf16[256,384]{1,0:T(8,128)(2,1)S(1)}, bf16[256,384]{1,0:T(8,128)(2,1)S(1)}, u32[]{:S(2)}, u32[]{:S(2)}) collective-permute-start(bf16[256,384]{1,0:T(8,128)(2,1)S(1)} %pad_maximum_fusion.5), channel_id=1, source_target_pairs={{0,2},{1,3},{2,0},{3,1},{4,6},{5,7},{6,4},{7,5},{8,10},{9,11},{10,... | collective-permute-start | bytes 589832 | tf_op jit(solution)/shard_map/ppermute | solution.py:905
  170.9 17.5 %collective-permute-start.43 = (bf16[384,384]{1,0:T(8,128)(2,1)S(1)}, bf16[384,384]{1,0:T(8,128)(2,1)S(1)}, u32[]{:S(2)}, u32[]{:S(2)}) collective-permute-start(bf16[384,384]{1,0:T(8,128)(2,1)S(1)} %pad_maximum_fusion.4), channel_id=1, source_target_pairs={{0,2},{1,3},{2,0},{3,1},{4,6},{5,7},{6,4},{7,5},{8,10},{9,11},{10,... | collective-permute-start | bytes 884744 | tf_op jit(solution)/shard_map/ppermute | solution.py:905
  173.2 8.6 %collective-permute-start.25 = (bf16[512,384]{1,0:T(8,128)(2,1)S(1)}, bf16[512,384]{1,0:T(8,128)(2,1)S(1)}, u32[]{:S(2)}, u32[]{:S(2)}) collective-permute-start(bf16[512,384]{1,0:T(8,128)(2,1)S(1)} %pad_maximum_fusion.2), channel_id=1, source_target_pairs={{0,16},{16,0},{1,17},{17,1},{2,18},{18,2},{3,19},{19,3},{4,20},{20... | collective-permute-start | bytes 1179656 | tf_op jit(solution)/shard_map/ppermute | solution.py:905
  174.0 14.6 %collective-permute-start.34 = (bf16[384,384]{1,0:T(8,128)(2,1)S(1)}, bf16[384,384]{1,0:T(8,128)(2,1)S(1)}, u32[]{:S(2)}, u32[]{:S(2)}) collective-permute-start(bf16[384,384]{1,0:T(8,128)(2,1)S(1)} %pad_maximum_fusion.3), channel_id=1, source_target_pairs={{0,4},{1,5},{2,6},{3,7},{4,0},{5,1},{6,2},{7,3},{8,12},{9,13},{10,... | collective-permute-start | bytes 884744 | tf_op jit(solution)/shard_map/ppermute | solution.py:905
  181.8 17.6 %collective-permute-start.26 = (bf16[1024,384]{1,0:T(8,128)(2,1)S(1)}, bf16[1024,384]{1,0:T(8,128)(2,1)S(1)}, u32[]{:S(2)}, u32[]{:S(2)}) collective-permute-start(bf16[1024,384]{1,0:T(8,128)(2,1)S(1)} %constant_dynamic-update-slice_fusion.4.own_ref), channel_id=1, source_target_pairs={{0,1},{1,0},{2,3},{3,2},{4,5},{5,4},{6,7},{7,6},{8,9},{9,8},{10,11... | collective-permute-start | bytes 2359304 | tf_op jit(solution)/shard_map/ppermute | solution.py:905
  188.6 7.9 %collective-permute-start.35 = (bf16[768,384]{1,0:T(8,128)(2,1)S(1)}, bf16[768,384]{1,0:T(8,128)(2,1)S(1)}, u32[]{:S(2)}, u32[]{:S(2)}) collective-permute-start(bf16[768,384]{1,0:T(8,128)(2,1)S(1)} %pad_maximum_fusion.own_ref), channel_id=1, source_target_pairs={{0,1},{1,0},{2,3},{3,2},{4,5},{5,4},{6,7},{7,6},{8,9},{9,8},{10,11... | collective-permute-start | bytes 1769480 | tf_op jit(solution)/shard_map/ppermute | solution.py:905
  (31 other events, 267.8 us)
